TPU v7x, 32 devices: a whole 2x2x4 slice. The times are simulated.
32 devices in a mesh: gx: 4 (over z), gy: 4 (over y, core), gz: 2 (over x).
Axes of the slice: x: 2, y: 2, z: 4, core: 2. Of those that a mesh axis runs over, the one named last changes fastest.
Arguments:
- sol_pos: float32 [3, 4, 4, 2, 49152], P(None, 'gx', 'gy', 'gz'), as said below
- sol_vel: float32 [3, 4, 4, 2, 49152], P(None, 'gx', 'gy', 'gz'), may hold values from -6 to 6
- sol_rows: int32 [4, 4, 2], P('gx', 'gy', 'gz'), may hold values from 192 to 384, as said below
- mig_pos: float32 [3, 4, 4, 2, 6, 3072], P(None, 'gx', 'gy', 'gz'), as said below
- mig_vel: float32 [3, 4, 4, 2, 6, 3072], P(None, 'gx', 'gy', 'gz'), may hold values from -6 to 6
- mig_rows: int32 [4, 4, 2, 6], P('gx', 'gy', 'gz'), may hold values from 0 to 24, as said below
- bead_pos: float32 [3, 4, 4, 2, 256], P(None, 'gx', 'gy', 'gz'), as said below
- bead_vel: float32 [3, 4, 4, 2, 256], P(None, 'gx', 'gy', 'gz'), may hold values from -2.7 to 2.7
- bead_chains: int32 [4, 4, 2], P('gx', 'gy', 'gz'), may hold values from 5 to 32, as said below
- bond_list: int32 [2, 4, 4, 2, 224], P(None, 'gx', 'gy', 'gz'), may hold values from 0 to 255, as said below
- cell_axis: int32 [64, 64, 64], P('gx', 'gy', 'gz'), may hold values from 0 to 31
- shift: int32 [3], replicated, may hold values from 0 to 15
Outputs:
- sol_pos_out: float32 [3, 4, 4, 2, 67584], P(None, 'gx', 'gy', 'gz')
- sol_vel_out: float32 [3, 4, 4, 2, 67584], P(None, 'gx', 'gy', 'gz')
- bead_pos_out: float32 [3, 4, 4, 2, 256], P(None, 'gx', 'gy', 'gz')
- bead_vel_out: float32 [3, 4, 4, 2, 256], P(None, 'gx', 'gy', 'gz')
Inputs may be any that keep to these rules, and one draw needn't show every extreme that they name: `sol_rows`: some device's resident slots are all live. `mig_rows`: some device receives full buffers across all six faces. `sol_pos`: every resident position lies in its device's region (cells i * 16 to (i + 1) * 16 - 1 along the first dimension, likewise for the others), and x * 16 is at least 0.1 from a whole number. `mig_pos`: buffer f holds positions in the region of the neighbour across face f, with the same margin. `bead_pos`: beads lie in their device's region with the same margin; bonded live beads are 0.88 to 1.13 apart and no two live beads are closer than 0.88. `bead_chains`: some device holds 32 chains. `bond_list`: a live bond joins two live slots of its device.
All inputs are finite; a program needn't handle non-finite values.
Results may differ from a plain program's by a relative error of at most 0.0003.
Values sent between devices are 32-bit elements; how exact they have to be, the bound alone decides.
No kernel may reach another device: no remote copies, remote signals or barrier semaphores. Data moves between devices by JAX's collectives and lax.ppermute only.
A program may use at most 128 MiB of HBM per device.

v0:
```python
import functools
import math

import jax
import jax.numpy as jnp
from jax import lax
from jax.experimental import pallas as pl
from jax.experimental.pallas import tpu as pltpu
from jax.sharding import PartitionSpec as P

UNITS = 16
NAXES = 32
CHAIN = 8
LANES = 128
GROUP = 8

bead_mass = 5.0
step_size = 0.02
spring = 30.0
reach_square = 2.25
cut_square = 2.0 ** (1.0 / 3.0)
turn_cosine = math.cos(130.0 * math.pi / 180.0)
turn_sine = math.sin(130.0 * math.pi / 180.0)
golden = math.pi * (3.0 - math.sqrt(5.0))
half_kick = 0.5 * step_size / bead_mass
far_own = 3000.0
far_ghost = 9000.0
vmem_limit = 48 * 1024 * 1024
NT = (((1,), (1,)), ((), ()))
NN = (((1,), (0,)), ((), ()))
exact = lax.Precision.HIGHEST
f32 = jnp.float32
bf16 = jnp.bfloat16


def params():
    return pltpu.CompilerParams(vmem_limit_bytes=vmem_limit)


def vmem():
    return pl.BlockSpec(memory_space=pltpu.VMEM)


def smem():
    return pl.BlockSpec(memory_space=pltpu.SMEM)


def moved_along(value, axis, by):
    peers = lax.axis_size(axis)
    return lax.ppermute(value, axis, [(i, (i + by) % peers) for i in range(peers)])


class Cells:
    def __init__(self, size_x, size_y, size_z):
        self.nx, self.ny, self.nz = size_x + 1, size_y + 1, size_z
        self.planes = self.nx * self.ny
        self.rows = -(-self.planes // 16) * 16
        self.middle = self.rows // 2


def levels_of(position, meta):
    return [
        jnp.floor(jnp.floor(position[d] * UNITS + meta[d].astype(f32)) * (1.0 / UNITS))
        - meta[3 + d].astype(f32)
        for d in range(3)
    ]


def plane_of(levels, cells):
    return levels[0] * cells.ny + levels[1] - cells.middle


def wide(row):
    return jnp.broadcast_to(row, (16, LANES)).astype(bf16)


def plane_hot(plane, cells):
    ids = lax.broadcasted_iota(jnp.int32, (cells.rows, LANES), 0) - cells.middle
    ids = ids.astype(f32).astype(bf16).reshape(cells.rows // 16, 16, LANES)
    one, zero = jnp.ones((), bf16), jnp.zeros((), bf16)
    pieces = [
        jnp.where(ids == wide(plane[r : r + 1])[None], one, zero).reshape(cells.rows, LANES)
        for r in range(plane.shape[0])
    ]
    return jnp.concatenate(pieces, axis=1)


def split(value):
    high = value.astype(bf16).astype(f32)
    return high, value - high


def spread_moments(depth, weight, velocity, cells):
    nz = cells.nz
    ids = lax.broadcasted_iota(jnp.int32, (nz, LANES), 0).astype(f32).astype(bf16)
    ids = ids.reshape(nz // 16, 16, LANES)
    row_ids = lax.broadcasted_iota(jnp.int32, (16, LANES), 0).astype(f32).astype(bf16)
    zero = jnp.zeros((), bf16)
    parts = [split(weight * velocity[d]) for d in range(3)]
    channels = [weight] + [p[0] for p in parts] + [p[1] for p in parts]
    pieces = []
    for r in range(depth.shape[0]):
        at = wide(depth[r : r + 1])
        here = ids == at[None]
        values = [wide(c[r : r + 1]) for c in channels]
        tiles = [jnp.where(here, v[None], zero).reshape(nz, LANES) for v in values]
        top = jnp.zeros((16, LANES), bf16)
        for c, v in enumerate(values):
            top = jnp.where(row_ids == c, v, top)
        top = jnp.where(at == nz, top, zero)
        pieces.append(
            jnp.concatenate(
                tiles[:4] + [top, jnp.zeros((nz - 16, LANES), bf16)] + tiles[4:], axis=0
            )
        )
    return jnp.concatenate(pieces, axis=1)


def bin_group(total_ref, position, velocity, weight, meta, cells):
    levels = levels_of(position, meta)
    hot = plane_hot(plane_of(levels, cells), cells)
    spread = spread_moments(levels[2], weight, velocity, cells)
    total_ref[...] += lax.dot_general(hot, spread, NT, preferred_element_type=f32)


def row_iota():
    return lax.broadcasted_iota(jnp.int32, (GROUP, LANES), 0)


def bin_residents(cells, meta_ref, pos_ref, vel_ref, total_ref):
    meta = [meta_ref[k] for k in range(8)]
    total_ref[...] = jnp.zeros_like(total_ref)
    live_rows = meta[6]

    @pl.loop(0, (live_rows + GROUP - 1) // GROUP)
    def _(step):
        rows = pl.ds(pl.multiple_of(step * GROUP, GROUP), GROUP)
        position = [pos_ref[d, rows, :] for d in range(3)]
        velocity = [vel_ref[d, rows, :] for d in range(3)]
        weight = jnp.where(row_iota() + step * GROUP < live_rows, 1.0, 0.0)
        bin_group(total_ref, position, velocity, weight, meta, cells)


def arrival_group(ref, step, face_rows):
    offset = pl.multiple_of(step * GROUP, GROUP)
    comps = [ref[pl.ds(c * face_rows + offset, GROUP), :] for c in range(6)]
    live = (row_iota() + offset).astype(f32) < ref[pl.ds(6 * face_rows, GROUP), :]
    return comps[:3], comps[3:], live


def face_count(ref, face_rows):
    return jnp.max(ref[pl.ds(6 * face_rows, GROUP), :]).astype(jnp.int32)


def bead_mask(chains):
    slot = row_iota() * LANES + lax.broadcasted_iota(jnp.int32, (GROUP, LANES), 1)
    return slot < CHAIN * chains


def bin_arrivals(cells, face_rows, meta_ref, *refs):
    faces, (bead_pos_ref, bead_vel_ref, start_ref, total_ref, low_ref, high_ref, sums) = (
        refs[:6],
        refs[6:],
    )
    meta = [meta_ref[k] for k in range(8)]
    sums[...] = start_ref[...]
    weight = jnp.where(bead_mask(meta[7]), bead_mass, 0.0)
    bin_group(
        sums,
        [bead_pos_ref[d] for d in range(3)],
        [bead_vel_ref[d] for d in range(3)],
        weight,
        meta,
        cells,
    )
    for ref in faces:

        @pl.loop(0, (face_count(ref, face_rows) + GROUP - 1) // GROUP)
        def _(step):
            position, velocity, live = arrival_group(ref, step, face_rows)
            bin_group(sums, position, velocity, jnp.where(live, 1.0, 0.0), meta, cells)

    lane = lax.broadcasted_iota(jnp.int32, (cells.rows, LANES), 1)
    main, rest = sums[:, :LANES], sums[:, LANES:]
    main = main + jnp.where(lane < cells.nz, 0.0, rest)
    top = jnp.where(lane == 0, rest, rest + pltpu.roll(rest, LANES - 3, axis=1))
    top = jnp.where(lane < 4, top, 0.0)
    ny, edge = cells.ny, (cells.nx - 1) * cells.ny
    low_ref[...] = jnp.zeros_like(low_ref)
    high_ref[...] = jnp.zeros_like(high_ref)
    for half, value in enumerate([main, top]):
        total_ref[half] = value
        low_ref[half, :ny, :] = value[:ny]
        high_ref[half, :ny, :] = value[edge : edge + ny]


def add_faces_x(cells, total_ref, below_ref, above_ref, out_ref, low_ref, high_ref):
    nx, ny, edge = cells.nx, cells.ny, (cells.nx - 1) * cells.ny
    out_ref[...] = total_ref[...]
    low_ref[...] = jnp.zeros_like(low_ref)
    high_ref[...] = jnp.zeros_like(high_ref)
    for half in range(2):
        out_ref[half, :ny, :] += below_ref[half, :ny, :]
        out_ref[half, edge : edge + ny, :] += above_ref[half, :ny, :]
        low_ref[half, :nx, :] = out_ref[half, pl.ds(0, nx, stride=ny), :]
        high_ref[half, :nx, :] = out_ref[half, pl.ds(ny - 1, nx, stride=ny), :]


def add_faces_y(cells, total_ref, below_ref, above_ref, out_ref, face_ref, sums):
    nx, ny, nz = cells.nx, cells.ny, cells.nz
    sums[...] = total_ref[...]
    for half in range(2):
        sums[half, pl.ds(0, nx, stride=ny), :] += below_ref[half, :nx, :]
        sums[half, pl.ds(ny - 1, nx, stride=ny), :] += above_ref[half, :nx, :]
    main = sums[0].T
    top = sums[1].T[:GROUP]
    out_ref[:LANES, :] = main
    out_ref[LANES:, :] = top
    for c in range(4):
        face_ref[c : c + 1, :] = main[c * nz : c * nz + 1]
        face_ref[4 + c : 5 + c, :] = top[c : c + 1]


def cell_table(cells, total, faces_below, faces_above, axis_index):
    nz = cells.nz
    row_ids = lax.broadcasted_iota(jnp.int32, (nz, cells.rows), 0)
    sums = []
    tops = []
    for c in range(4):
        part = total[c * nz : (c + 1) * nz]
        sums.append(part + jnp.where(row_ids == 0, faces_below[4 + c : 5 + c], 0.0))
        tops.append(total[LANES + c : LANES + c + 1] + faces_above[c : c + 1])
    mass = jnp.maximum(sums[0], 1.0)
    top_mass = jnp.maximum(tops[0], 1.0)
    mean = [split(s / mass) for s in sums[1:]]
    top_mean = [split(t / top_mass) for t in tops[1:]]
    top_rows = (
        [axis_index[nz : nz + 1]] + [t[0] for t in top_mean] + [t[1] for t in top_mean]
    )
    top_tile = jnp.zeros((nz, cells.rows), f32)
    for c, value in enumerate(top_rows):
        top_tile = jnp.where(row_ids == c, value, top_tile)
    return jnp.concatenate(
        [axis_index[:nz]] + [m[0] for m in mean] + [top_tile] + [m[1] for m in mean], axis=0
    ).astype(bf16)


def direction_table():
    counter = jnp.arange(LANES).astype(f32)
    height = 1.0 - (2.0 * counter + 1.0) / NAXES
    radius = jnp.sqrt(jnp.maximum(1.0 - height * height, 0.0))
    rows = jnp.stack([radius * jnp.cos(golden * counter), radius * jnp.sin(golden * counter)])
    return jnp.broadcast_to(rows[:, None], (2, GROUP, LANES))


def collide(position, velocity, meta, table, dirs_ref, cells):
    nz = cells.nz
    levels = levels_of(position, meta)
    depth = levels[2]
    count = depth.shape[0]
    found = lax.dot_general(
        table, plane_hot(plane_of(levels, cells), cells), NN, preferred_element_type=f32
    )
    ids = lax.broadcasted_iota(jnp.int32, (nz, LANES), 0).astype(f32)
    rows = lax.broadcasted_iota(jnp.int32, (GROUP, LANES), 0)
    picked = [jnp.zeros((count, LANES), f32) for _ in range(4)]
    for r in range(count):
        block = found[:, r * LANES : (r + 1) * LANES]
        at = depth[r : r + 1]
        here = ids == at
        top = jnp.where(at == nz, block[4 * nz : 4 * nz + GROUP], 0.0)
        tops = top + pltpu.roll(top, GROUP - 3, axis=0)
        for c in range(4):
            value = block[c * nz : (c + 1) * nz]
            if c > 0:
                value = value + block[(4 + c) * nz : (5 + c) * nz]
            value = jnp.where(here, value, 0.0)
            value = jnp.sum(value.reshape(nz // GROUP, GROUP, LANES), axis=0)
            value = value + jnp.where(rows == c, tops if c > 0 else top, 0.0)
            value = jnp.sum(value, axis=0, keepdims=True)
            picked[c] = jnp.where(rows == r, value, picked[c])
    axis, flow = picked[0].astype(jnp.int32), picked[1:]
    normal = [
        jnp.take_along_axis(dirs_ref[0], axis, axis=1, mode="promise_in_bounds"),
        jnp.take_along_axis(dirs_ref[1], axis, axis=1, mode="promise_in_bounds"),
        1.0 - (2.0 * picked[0] + 1.0) * (1.0 / NAXES),
    ]
    rel = [velocity[d] - flow[d] for d in range(3)]
    along = (1.0 - turn_cosine) * (
        normal[0] * rel[0] + normal[1] * rel[1] + normal[2] * rel[2]
    )
    result = []
    for d in range(3):
        e, f = (d + 1) % 3, (d + 2) % 3
        crossed = normal[e] * rel[f] - normal[f] * rel[e]
        result.append(
            flow[d] + (turn_cosine * rel[d] + turn_sine * crossed + along * normal[d])
        )
    return result


def passed(position, speed):
    return position - jnp.floor(position) - 0.5 + 3.0 * step_size * speed


def copy_out(pairs, sems):
    copies = [pltpu.make_async_copy(a, b, sems.at[k]) for k, (a, b) in enumerate(pairs)]
    for copy in copies:
        copy.start()
    for copy in copies:
        copy.wait()


def collide_residents(
    cells, first, count, meta_ref, dirs_ref, table_ref, pos_ref, vel_ref, *refs
):
    out_pos, out_vel, held_pos, held_vel, sems = refs[-5:]
    meta = [meta_ref[k] for k in range(8)]
    table = table_ref[...]
    live_rows = meta[6] - first
    held_pos[...] = jnp.zeros_like(held_pos)
    held_vel[...] = jnp.zeros_like(held_vel)

    @pl.loop(0, jnp.clip((live_rows + GROUP - 1) // GROUP, 0, count // GROUP))
    def _(step):
        rows = pl.ds(pl.multiple_of(step * GROUP, GROUP), GROUP)
        position = [pos_ref[d, rows, :] for d in range(3)]
        velocity = [vel_ref[d, rows, :] for d in range(3)]
        live = row_iota() + step * GROUP < live_rows
        speed = collide(position, velocity, meta, table, dirs_ref, cells)
        for d in range(3):
            held_vel[d, rows, :] = jnp.where(live, speed[d], 0.0)
            held_pos[d, rows, :] = jnp.where(live, passed(position[d], speed[d]), 0.0)

    span = pl.ds(first, count)
    copy_out([(held_pos, out_pos.at[:, span, :]), (held_vel, out_vel.at[:, span, :])], sems)


def collide_arrivals(cells, first, face_rows, meta_ref, dirs_ref, table_ref, *refs):
    faces = refs[:6]
    out_pos, out_vel, held_pos, held_vel, sems = refs[-5:]
    meta = [meta_ref[k] for k in range(8)]
    table = table_ref[...]
    held_pos[...] = jnp.zeros_like(held_pos)
    held_vel[...] = jnp.zeros_like(held_vel)
    for face, ref in enumerate(faces):

        @pl.loop(0, (face_count(ref, face_rows) + GROUP - 1) // GROUP)
        def _(step):
            position, velocity, live = arrival_group(ref, step, face_rows)
            speed = collide(position, velocity, meta, table, dirs_ref, cells)
            rows = pl.ds(face * face_rows + pl.multiple_of(step * GROUP, GROUP), GROUP)
            for d in range(3):
                held_vel[d, rows, :] = jnp.where(live, speed[d], 0.0)
                held_pos[d, rows, :] = jnp.where(live, passed(position[d], speed[d]), 0.0)

    span = pl.ds(first, 6 * face_rows)
    copy_out([(held_pos, out_pos.at[:, span, :]), (held_vel, out_vel.at[:, span, :])], sems)


def pack_faces(face_rows, pos_ref, vel_ref, rows_ref, *out_refs):
    for face, out_ref in enumerate(out_refs):
        for c in range(6):
            source = pos_ref if c < 3 else vel_ref
            for k in range(face_rows):
                out_ref[c * face_rows + k : c * face_rows + k + 1, :] = source[
                    c % 3, face : face + 1, k * LANES : (k + 1) * LANES
                ]
        out_ref[6 * face_rows :, :] = jnp.full((GROUP, LANES), rows_ref[face], jnp.int32).astype(
            f32
        )


def bead_rows(parts):
    return jnp.concatenate(parts, axis=0)


def slot_live(slots, chains, rows):
    return lax.broadcasted_iota(jnp.int32, (rows, slots), 1) < CHAIN * chains


def payload(position, live):
    slots = position.shape[1]
    row_ids = lax.broadcasted_iota(jnp.int32, (GROUP, slots), 0)
    flag = jnp.where(live, 1.0, 0.0)
    return jnp.where(row_ids == 3, flag, jnp.where(row_ids < 3, position, 0.0))


def forces(own, chains, bonds_ref, blocks, centre, lengths):
    slots = own.shape[1]
    bond_slots = bonds_ref.shape[0]
    row_ids = lax.broadcasted_iota(jnp.int32, (GROUP, slots), 0)
    mid = jnp.zeros((GROUP, slots), f32)
    length = jnp.ones((GROUP, slots), f32)
    for d in range(3):
        mid = jnp.where(row_ids == d, centre[d], mid)
        length = jnp.where(row_ids == d, lengths[d], length)
    local = jnp.where(row_ids < 3, own - mid, 0.0)
    live = slot_live(slots, chains, GROUP)
    here = jnp.where(live, local, far_own)
    mine = [here[d : d + 1] for d in range(3)]
    total = [jnp.zeros((32, slots), f32) for _ in range(3)]
    for ref in blocks:
        for b in range(ref.shape[0] // GROUP):
            block = ref[b * GROUP : (b + 1) * GROUP, :]
            near = block - mid
            near = near - length * jnp.floor(near / length + 0.5)
            near = jnp.where(block[3:4] > 0.5, near, far_ghost)
            columns = near.T

            for k in range(slots // 32):
                differ = [mine[d] - columns[k * 32 : (k + 1) * 32, d : d + 1] for d in range(3)]
                square = (
                    differ[0] * differ[0] + differ[1] * differ[1] + differ[2] * differ[2]
                )
                inside = (square < cut_square) & (square > 0.25)
                inverse = 1.0 / jnp.where(inside, square, 1.0)
                sixth = inverse * inverse * inverse
                weight = jnp.where(
                    inside, 24.0 * (2.0 * sixth * sixth - sixth) * inverse, 0.0
                )
                total = [total[d] + weight * differ[d] for d in range(3)]
    pair = jnp.zeros((GROUP, slots), f32)
    for d in range(3):
        pair = jnp.where(row_ids == d, jnp.sum(total[d], axis=0, keepdims=True), pair)
    slot_ids = lax.broadcasted_iota(jnp.int32, (bond_slots, slots), 1)
    bond_ids = lax.broadcasted_iota(jnp.int32, (bond_slots, slots), 0)
    ends = bonds_ref[...]
    first = jnp.where(slot_ids == ends[:, 0:1], 1.0, 0.0)
    second = jnp.where(slot_ids == ends[:, 1:2], 1.0, 0.0)
    joins = jnp.where(bond_ids < (CHAIN - 1) * chains, first - second, 0.0)
    stretch = lax.dot_general(
        jnp.where(live, local, 0.0), joins, NT, precision=exact, preferred_element_type=f32
    )
    square = (
        stretch[0:1] * stretch[0:1] + stretch[1:2] * stretch[1:2] + stretch[2:3] * stretch[2:3]
    )
    bond_live = (
        lax.broadcasted_iota(jnp.int32, (1, bond_slots), 1) < (CHAIN - 1) * chains
    )
    pull = jnp.where(bond_live, -spring / (1.0 - square / reach_square), 0.0) * stretch
    return pair + lax.dot_general(pull, joins, NN, precision=exact, preferred_element_type=f32)


def centre_of(meta, sizes):
    return [meta[3 + d].astype(f32) + 0.5 * sizes[d] for d in range(3)]


def first_forces(sizes, lengths, meta_ref, start_ref, bonds_ref, a_ref, b_ref, c_ref, push_ref):
    meta = [meta_ref[k] for k in range(8)]
    push_ref[...] = forces(
        start_ref[...],
        meta[7],
        bonds_ref,
        [a_ref, b_ref, c_ref],
        centre_of(meta, sizes),
        lengths,
    )


def finish_cells(
    cells,
    meta_ref,
    dirs_ref,
    total_ref,
    below_ref,
    above_ref,
    axis_ref,
    bead_pos_ref,
    bead_vel_ref,
    start_ref,
    push_ref,
    table_ref,
    speed_ref,
    moved_ref,
    pay_ref,
):
    meta = [meta_ref[k] for k in range(8)]
    table_ref[...] = cell_table(
        cells, total_ref[...], below_ref[...], above_ref[...], axis_ref[...].astype(f32)
    )
    fresh = collide(
        [bead_pos_ref[d] for d in range(3)],
        [bead_vel_ref[d] for d in range(3)],
        meta,
        table_ref[...],
        dirs_ref,
        cells,
    )
    start = start_ref[...]
    slots = start.shape[1]
    row_ids = lax.broadcasted_iota(jnp.int32, (GROUP, slots), 0)
    speed = jnp.zeros((GROUP, slots), f32)
    for d in range(3):
        line = jnp.concatenate([fresh[d][k : k + 1] for k in range(slots // LANES)], axis=1)
        speed = jnp.where(row_ids == d, line, speed)
    speed = speed + half_kick * push_ref[...]
    moved = step_size * speed
    live = slot_live(slots, meta[7], GROUP)
    speed_ref[...] = speed
    moved_ref[...] = moved
    pay_ref[...] = payload(start + moved, live)


def substep(
    sizes,
    lengths,
    last,
    meta_ref,
    start_ref,
    bonds_ref,
    speed_ref,
    moved_ref,
    a_ref,
    b_ref,
    c_ref,
    speed_out,
    moved_out,
    *pay_refs,
):
    meta = [meta_ref[k] for k in range(8)]
    start = start_ref[...]
    moved = moved_ref[...]
    push = forces(
        start + moved, meta[7], bonds_ref, [a_ref, b_ref, c_ref], centre_of(meta, sizes), lengths
    )
    live = slot_live(start.shape[1], meta[7], GROUP)
    speed = speed_ref[...] + half_kick * push
    if last:
        speed_out[...] = jnp.where(live, speed, 0.0)
        moved_out[...] = jnp.where(live, moved, 0.0)
        return
    speed = speed + half_kick * push
    moved = moved + step_size * speed
    speed_out[...] = speed
    moved_out[...] = moved
    pay_refs[0][...] = payload(start + moved, live)


def neighbours(value, axis):
    peers = lax.axis_size(axis)
    if peers == 2:
        return [moved_along(value, axis, 1)]
    return [moved_along(value, axis, 1), moved_along(value, axis, -1)]


def halo(block):
    row = jnp.concatenate([block] + neighbours(block, "gz"), axis=0)
    plane = jnp.concatenate([row] + neighbours(row, "gy"), axis=0)
    sides = neighbours(plane, "gx")
    return [plane] + sides + sides[: 2 - len(sides)]


def like(*shape, dtype=f32):
    return jax.ShapeDtypeStruct(shape, dtype)


def with_upper(value, axis, dim):
    first = lax.slice_in_dim(value, 0, 1, axis=dim)
    return jnp.concatenate([value, moved_along(first, axis, -1)], axis=dim)


def shards(
    sol_pos,
    sol_vel,
    sol_rows,
    mig_pos,
    mig_vel,
    mig_rows,
    bead_pos,
    bead_vel,
    bead_chains,
    bond_list,
    cell_axis,
    shift,
):
    sizes = cell_axis.shape
    cells = Cells(*sizes)
    names = ("gx", "gy", "gz")
    lengths = tuple(float(sizes[d] * lax.axis_size(names[d])) for d in range(3))
    slots_here = sol_pos.shape[-1]
    buffer_slots = mig_pos.shape[-1]
    bead_slots = bead_pos.shape[-1]
    bond_slots = bond_list.shape[-1]
    rows_here = slots_here // LANES
    face_rows = buffer_slots // LANES
    rows_all = rows_here + 6 * face_rows
    anchor = jnp.stack([lax.axis_index(names[d]) * sizes[d] for d in range(3)])
    meta = jnp.concatenate(
        [shift, anchor.astype(jnp.int32), sol_rows.reshape(1), bead_chains.reshape(1)]
    )
    dirs = direction_table()
    position = sol_pos.reshape(3, rows_here, LANES)
    velocity = sol_vel.reshape(3, rows_here, LANES)

    packed = pl.pallas_call(
        functools.partial(pack_faces, face_rows),
        out_shape=[like(6 * face_rows + GROUP, LANES)] * 6,
        in_specs=[vmem(), vmem(), smem()],
        out_specs=[vmem()] * 6,
        compiler_params=params(),
        name="pack_faces",
    )(
        mig_pos.reshape(3, 6, buffer_slots),
        mig_vel.reshape(3, 6, buffer_slots),
        mig_rows.reshape(6),
    )
    arriving = [
        moved_along(packed[1], "gx", 1),
        moved_along(packed[0], "gx", -1),
        moved_along(packed[3], "gy", 1),
        moved_along(packed[2], "gy", -1),
        moved_along(packed[5], "gz", 1),
        moved_along(packed[4], "gz", -1),
    ]

    start = jnp.pad(bead_pos.reshape(3, bead_slots), ((0, GROUP - 3), (0, 0)))
    bead_rows_pos = jnp.pad(
        bead_pos.reshape(3, bead_slots // LANES, LANES),
        ((0, 0), (0, GROUP - bead_slots // LANES), (0, 0)),
    )
    bead_rows_vel = jnp.pad(
        bead_vel.reshape(3, bead_slots // LANES, LANES),
        ((0, 0), (0, GROUP - bead_slots // LANES), (0, 0)),
    )
    bonds = bond_list.reshape(2, bond_slots).T
    bead_live = jnp.arange(bead_slots, dtype=jnp.int32) < CHAIN * bead_chains.reshape(())
    first_pay = jnp.concatenate(
        [
            bead_pos.reshape(3, bead_slots),
            bead_live.astype(f32)[None],
            jnp.zeros((GROUP - 4, bead_slots), f32),
        ],
        axis=0,
    )
    ghosts = halo(first_pay)

    axis_index = with_upper(with_upper(with_upper(cell_axis, "gx", 0), "gy", 1), "gz", 2)
    axis_index = axis_index.transpose(2, 0, 1).reshape(cells.nz + 1, cells.planes)
    axis_index = jnp.pad(
        axis_index, ((0, GROUP - 1), (0, cells.rows - cells.planes))
    )

    totals = pl.pallas_call(
        functools.partial(bin_residents, cells),
        out_shape=like(cells.rows, 2 * LANES),
        in_specs=[smem(), vmem(), vmem()],
        out_specs=vmem(),
        compiler_params=params(),
        name="bin_residents",
    )(meta, position, velocity)

    push = pl.pallas_call(
        functools.partial(first_forces, sizes, lengths),
        out_shape=like(GROUP, bead_slots),
        in_specs=[smem()] + [vmem()] * 5,
        out_specs=vmem(),
        compiler_params=params(),
        name="first_forces",
    )(meta, start, bonds, *ghosts)

    face_x = like(2, -(-cells.ny // GROUP) * GROUP, LANES)
    face_y = like(2, -(-cells.nx // GROUP) * GROUP, LANES)
    totals, low, high = pl.pallas_call(
        functools.partial(bin_arrivals, cells, face_rows),
        out_shape=[like(2, cells.rows, LANES), face_x, face_x],
        in_specs=[smem()] + [vmem()] * 9,
        out_specs=[vmem()] * 3,
        scratch_shapes=[pltpu.VMEM((cells.rows, 2 * LANES), f32)],
        compiler_params=params(),
        name="bin_arrivals",
    )(meta, *arriving, bead_rows_pos, bead_rows_vel, totals)

    below, above = moved_along(high, "gx", 1), moved_along(low, "gx", -1)
    totals, low, high = pl.pallas_call(
        functools.partial(add_faces_x, cells),
        out_shape=[like(2, cells.rows, LANES), face_y, face_y],
        in_specs=[vmem()] * 3,
        out_specs=[vmem()] * 3,
        compiler_params=params(),
        name="add_faces_x",
    )(totals, below, above)
    below, above = moved_along(high, "gy", 1), moved_along(low, "gy", -1)
    totals, faces = pl.pallas_call(
        functools.partial(add_faces_y, cells),
        out_shape=[like(LANES + GROUP, cells.rows), like(GROUP, cells.rows)],
        in_specs=[vmem()] * 3,
        out_specs=[vmem()] * 2,
        scratch_shapes=[pltpu.VMEM((2, cells.rows, LANES), f32)],
        compiler_params=params(),
        name="add_faces_y",
    )(totals, below, above)
    sides = neighbours(faces, "gz")
    below, above = sides[0], sides[-1]

    bead_shape = like(GROUP, bead_slots)
    table, speed, moved, pay = pl.pallas_call(
        functools.partial(finish_cells, cells),
        out_shape=[like(2 * LANES, cells.rows, dtype=bf16), bead_shape, bead_shape, bead_shape],
        in_specs=[smem()] + [vmem()] * 9,
        out_specs=[vmem()] * 4,
        compiler_params=params(),
        name="finish_cells",
    )(
        meta,
        dirs,
        totals,
        below,
        above,
        axis_index,
        bead_rows_pos,
        bead_rows_vel,
        start,
        push,
    )

    any_spec = pl.BlockSpec(memory_space=pl.ANY)
    solvent_shape = like(3, rows_all, LANES)
    results = []
    cuts = 4
    count = rows_here // cuts
    for piece in range(cuts):
        earlier = results
        results = pl.pallas_call(
            functools.partial(collide_residents, cells, piece * count, count),
            out_shape=[solvent_shape] * 2,
            grid=(1,),
            in_specs=[smem(), vmem(), vmem()]
            + [pl.BlockSpec((3, count, LANES), lambda i, p=piece: (0, p, 0))] * 2
            + [any_spec] * len(earlier),
            out_specs=[any_spec] * 2,
            scratch_shapes=[pltpu.VMEM((3, count, LANES), f32)] * 2
            + [pltpu.SemaphoreType.DMA((2,))],
            input_output_aliases={5: 0, 6: 1} if earlier else {},
            compiler_params=params(),
            name=f"collide_residents_{piece}",
        )(meta, dirs, table, position, velocity, *earlier)
    results = pl.pallas_call(
        functools.partial(collide_arrivals, cells, rows_here, face_rows),
        out_shape=[solvent_shape] * 2,
        in_specs=[smem()] + [vmem()] * 8 + [any_spec] * 2,
        out_specs=[any_spec] * 2,
        scratch_shapes=[pltpu.VMEM((3, 6 * face_rows, LANES), f32)] * 2
        + [pltpu.SemaphoreType.DMA((2,))],
        input_output_aliases={9: 0, 10: 1},
        compiler_params=params(),
        name="collide_arrivals",
    )(meta, dirs, table, *arriving, *results)

    for step in range(3):
        last = step == 2
        outcome = pl.pallas_call(
            functools.partial(substep, sizes, lengths, last),
            out_shape=[bead_shape] * (2 if last else 3),
            in_specs=[smem()] + [vmem()] * 7,
            out_specs=[vmem()] * (2 if last else 3),
            compiler_params=params(),
            name=f"substep_{step}",
        )(meta, start, bonds, speed, moved, *halo(pay))
        speed, moved = outcome[:2]
        pay = outcome[-1]

    count_solvent = rows_all * LANES
    return (
        results[0].reshape(3, 1, 1, 1, count_solvent),
        results[1].reshape(3, 1, 1, 1, count_solvent),
        moved[:3].reshape(3, 1, 1, 1, bead_slots),
        speed[:3].reshape(3, 1, 1, 1, bead_slots),
    )


def solution(mesh):
    return jax.shard_map(
        shards,
        mesh=mesh,
        in_specs=(
            P(None, "gx", "gy", "gz", None),
            P(None, "gx", "gy", "gz", None),
            P("gx", "gy", "gz"),
            P(None, "gx", "gy", "gz", None, None),
            P(None, "gx", "gy", "gz", None, None),
            P("gx", "gy", "gz", None),
            P(None, "gx", "gy", "gz", None),
            P(None, "gx", "gy", "gz", None),
            P("gx", "gy", "gz"),
            P(None, "gx", "gy", "gz", None),
            P("gx", "gy", "gz"),
            P(),
        ),
        out_specs=(
            P(None, "gx", "gy", "gz", None),
            P(None, "gx", "gy", "gz", None),
            P(None, "gx", "gy", "gz", None),
            P(None, "gx", "gy", "gz", None),
        ),
        check_vma=False,
    )
```

profile of v0, /device:TPU:1, one launch (start us, length us, event | category | flops | bytes accessed | tf_op | source)
XLA Modules:
  0.0 166.5 jit_solution(11797830324524601817)
XLA Ops:
  1.3 0.7 copy-done.4
  2.0 2.1 %collective-permute-start.14 = (f32[8,256]{1,0:T(8,128)S(1)}, f32[8,256]{1,0:T(8,128)S(1)}, u32[]{:S(2)}, u32[]{:S(2)}) collective-permute-start(f32[8,256]{1,0:T(8,128)S(1)} %get-tuple-element.96), channel_id=1, source_target_pairs={{0,1},{1,0},{2,3},{3,2},{4,5},{5,4},{6,7},{7,6},{8,9},{9,8},{10,11... | collective-permute-start | bytes 24584 | tf_op jit(solution)/shard_map/ppermute | solution.py:50
  4.1 0.7 slice.15
  4.8 3.3 %collective-permute-start.11 = (s32[1,16,32]{2,1,0:T(8,128)S(1)}, s32[1,16,32]{2,1,0:T(8,128)S(1)}, u32[]{:S(2)}, u32[]{:S(2)}) collective-permute-start(s32[1,16,32]{2,1,0:T(8,128)S(1)} %slice.15), channel_id=1, source_target_pairs={{0,24},{8,0},{16,8},{24,16},{1,25},{9,1},{17,9},{25,17},{2,26},{10... | collective-permute-start | bytes 6152 | tf_op jit(solution)/shard_map/ppermute | solution.py:50
  8.1 1.2 copy_bitcast_fusion
  9.4 0.8 pack_faces.1
  10.3 3.3 %collective-permute-start.1 = (f32[152,128]{1,0:T(8,128)S(1)}, f32[152,128]{1,0:T(8,128)S(1)}, u32[]{:S(2)}, u32[]{:S(2)}) collective-permute-start(f32[152,128]{1,0:T(8,128)S(1)} %get-tuple-element.41), channel_id=1, source_target_pairs={{0,24},{8,0},{16,8},{24,16},{1,25},{9,1},{17,9},{25,17},{2,26},{10... | collective-permute-start | bytes 233480 | tf_op jit(solution)/shard_map/ppermute | solution.py:50
  13.5 2.9 %collective-permute-start.2 = (f32[152,128]{1,0:T(8,128)S(1)}, f32[152,128]{1,0:T(8,128)S(1)}, u32[]{:S(2)}, u32[]{:S(2)}) collective-permute-start(f32[152,128]{1,0:T(8,128)S(1)} %get-tuple-element.42), channel_id=1, source_target_pairs={{0,2},{2,4},{4,6},{6,0},{1,3},{3,5},{5,7},{7,1},{8,10},{10,12},{12... | collective-permute-start | bytes 233480 | tf_op jit(solution)/shard_map/ppermute | solution.py:50
  17.4 0.6 copy-done.7
  18.0 0.1 concatenate.44.meta_ref
  18.1 17.6 %bin_residents.1.refs_8_ = f32[304,256]{1,0:T(8,128)S(1)} custom-call(s32[8]{0:T(128)S(1)} %concatenate.44.meta_ref, f32[3,384,128]{2,1,0:T(8,128)S(1)} %bitcast.33, f32[3,384,128]{2,1,0:T(8,128)S(1)} %bitcast.38), custom_call_target="tpu_custom_call" | custom-call | tf_op jit(solution)/shard_map/bin_residents/pallas_call | solution.py:644
  35.8 0.1 collective-permute-start.4
  35.9 1.4 collective-permute-start.5
  37.4 0.2 collective-permute-start.13
  37.5 2.4 %collective-permute-done.3.refs_3_ = f32[152,128]{1,0:T(8,128)S(1)} collective-permute-done((f32[152,128]{1,0:T(8,128)S(1)}, f32[152,128]{1,0:T(8,128)S(1)}, u32[]{:S(2)}, u32[]{:S(2)}) %collective-permute-start.3) | collective-permute-done | bytes 77856 | tf_op jit(solution)/shard_map/ppermute | solution.py:50
  39.9 0.1 collective-permute-done.4.refs_4_
  40.0 1.4 collective-permute-done.5.refs_5_
  41.4 7.7 %bin_arrivals.1 = (f32[2,304,128]{2,1,0:T(8,128)S(1)}, f32[2,24,128]{2,1,0:T(8,128)S(1)}, f32[2,24,128]{2,1,0:T(8,128)S(1)}) custom-call(s32[8]{0:T(128)S(1)} %concatenate.44.meta_ref, f32[152,128]{1,0:T(8,128)S(1)} %collective-permute-done.refs_0_, f32[152,128]{1,0:T(8,128)S(1)} %collective-permute-done.1.refs_1_, ...), custom_call_target="tpu_custom_call" | custom-call | tf_op jit(solution)/shard_map/bin_arrivals/pallas_call | solution.py:664
  49.2 3.3 %collective-permute-start.7 = (f32[2,24,128]{2,1,0:T(8,128)S(1)}, f32[2,24,128]{2,1,0:T(8,128)S(1)}, u32[]{:S(2)}, u32[]{:S(2)}) collective-permute-start(f32[2,24,128]{2,1,0:T(8,128)S(1)} %get-tuple-element.48), channel_id=1, source_target_pairs={{0,24},{8,0},{16,8},{24,16},{1,25},{9,1},{17,9},{25,17},{2,26},{10... | collective-permute-start | bytes 73736 | tf_op jit(solution)/shard_map/ppermute | solution.py:50
  52.5 1.7 %collective-permute-start.15 = (f32[16,256]{1,0:T(8,128)S(1)}, f32[16,256]{1,0:T(8,128)S(1)}, u32[]{:S(2)}, u32[]{:S(2)}) collective-permute-start(f32[16,256]{1,0:T(8,128)S(1)} %pad_maximum_fusion), channel_id=1, source_target_pairs={{0,2},{2,4},{4,6},{6,0},{1,3},{3,5},{5,7},{7,1},{8,10},{10,12},{12... | collective-permute-start | bytes 49160 | tf_op jit(solution)/shard_map/ppermute | solution.py:50
  54.3 1.3 collective-permute-start.8
  55.6 0.7 copy-done.6
  56.3 0.1 copy.31
  56.5 3.6 %collective-permute-start.18 = (f32[48,256]{1,0:T(8,128)S(1)}, f32[48,256]{1,0:T(8,128)S(1)}, u32[]{:S(2)}, u32[]{:S(2)}) collective-permute-start(f32[48,256]{1,0:T(8,128)S(1)} %concatenate.50.a_ref), channel_id=1, source_target_pairs={{0,24},{8,0},{16,8},{24,16},{1,25},{9,1},{17,9},{25,17},{2,26},{10... | collective-permute-start | bytes 147464 | tf_op jit(solution)/shard_map/ppermute | solution.py:50
  60.1 0.2 add_faces_y.1
  60.3 1.4 collective-permute-start.10
  61.7 0.1 add_bitcast_fusion
  61.8 0.1 copy.30
  62.0 2.9 %collective-permute-done.17.b_ref = f32[48,256]{1,0:T(8,128)S(1)} collective-permute-done((f32[48,256]{1,0:T(8,128)S(1)}, f32[48,256]{1,0:T(8,128)S(1)}, u32[]{:S(2)}, u32[]{:S(2)}) %collective-permute-start.17) | collective-permute-done | bytes 49184 | tf_op jit(solution)/shard_map/ppermute | solution.py:50
  64.8 5.7 %first_forces.1.push_ref = f32[8,256]{1,0:T(8,128)S(1)} custom-call(s32[8]{0:T(128)S(1)} %concatenate.44.meta_ref, f32[8,256]{1,0:T(8,128)S(1)} %get-tuple-element.97.start_ref, s32[224,2]{1,0:T(8,128)S(1)} %bitcast.43, f32[48,256]{1,0:T(8,128)S(1)} %concatenate.50.a_ref, f32[48,256]{1,0:T(8,128)S(1)} %collective-permute-done.17.b_ref, ...), custom_call_target="tpu_custom_call" | custom-call | tf_op jit(solution)/shard_map/first_forces/pallas_call | solution.py:653
  70.6 1.1 finish_cells.1
  71.7 1.4 collective-permute-start.19
  73.1 1.2 collective-permute-done.19
  74.2 4.3 %collective-permute-start.20 = (f32[16,256]{1,0:T(8,128)S(1)}, f32[16,256]{1,0:T(8,128)S(1)}, u32[]{:S(2)}, u32[]{:S(2)}) collective-permute-start(f32[16,256]{1,0:T(8,128)S(1)} %get-tuple-element.92), channel_id=1, source_target_pairs={{0,2},{2,4},{4,6},{6,0},{1,3},{3,5},{5,7},{7,1},{8,10},{10,12},{12... | collective-permute-start | bytes 49160 | tf_op jit(solution)/shard_map/ppermute | solution.py:50
  78.6 0.9 collective-permute-done.20
  79.4 2.3 %collective-permute-done.21 = f32[16,256]{1,0:T(8,128)S(1)} collective-permute-done((f32[16,256]{1,0:T(8,128)S(1)}, f32[16,256]{1,0:T(8,128)S(1)}, u32[]{:S(2)}, u32[]{:S(2)}) %collective-permute-start.21) | collective-permute-done | bytes 16416 | tf_op jit(solution)/shard_map/ppermute | solution.py:50
  81.7 1.5 collective-permute-start.22
  83.2 1.5 collective-permute-done.23.c_ref
  84.7 1.9 %collective-permute-done.22.b_ref = f32[48,256]{1,0:T(8,128)S(1)} collective-permute-done((f32[48,256]{1,0:T(8,128)S(1)}, f32[48,256]{1,0:T(8,128)S(1)}, u32[]{:S(2)}, u32[]{:S(2)}) %collective-permute-start.22) | collective-permute-done | bytes 49184 | tf_op jit(solution)/shard_map/ppermute | solution.py:50
  86.6 5.6 %substep_0.1 = (f32[8,256]{1,0:T(8,128)S(1)}, f32[8,256]{1,0:T(8,128)S(1)}, f32[8,256]{1,0:T(8,128)S(1)}) custom-call(s32[8]{0:T(128)S(1)} %concatenate.44.meta_ref, f32[8,256]{1,0:T(8,128)S(1)} %get-tuple-element.97.start_ref, s32[224,2]{1,0:T(8,128)S(1)} %bitcast.44, f32[8,256]{1,0:T(8,128)S(1)} %get-tuple-element.65.speed_ref, ...), custom_call_target="tpu_custom_call" | custom-call | tf_op jit(solution)/shard_map/substep_0/pallas_call | solution.py:752
  92.2 1.6 collective-permute-start.24
  93.8 1.0 collective-permute-done.24
  94.8 2.5 %collective-permute-start.25 = (f32[16,256]{1,0:T(8,128)S(1)}, f32[16,256]{1,0:T(8,128)S(1)}, u32[]{:S(2)}, u32[]{:S(2)}) collective-permute-start(f32[16,256]{1,0:T(8,128)S(1)} %get-tuple-element.88), channel_id=1, source_target_pairs={{0,2},{2,4},{4,6},{6,0},{1,3},{3,5},{5,7},{7,1},{8,10},{10,12},{12... | collective-permute-start | bytes 49160 | tf_op jit(solution)/shard_map/ppermute | solution.py:50
  97.3 0.9 collective-permute-done.25
  98.1 2.3 %collective-permute-done.26 = f32[16,256]{1,0:T(8,128)S(1)} collective-permute-done((f32[16,256]{1,0:T(8,128)S(1)}, f32[16,256]{1,0:T(8,128)S(1)}, u32[]{:S(2)}, u32[]{:S(2)}) %collective-permute-start.26) | collective-permute-done | bytes 16416 | tf_op jit(solution)/shard_map/ppermute | solution.py:50
  100.4 1.5 collective-permute-start.27
  101.9 1.5 collective-permute-done.28.c_ref
  103.4 1.9 %collective-permute-done.27.b_ref = f32[48,256]{1,0:T(8,128)S(1)} collective-permute-done((f32[48,256]{1,0:T(8,128)S(1)}, f32[48,256]{1,0:T(8,128)S(1)}, u32[]{:S(2)}, u32[]{:S(2)}) %collective-permute-start.27) | collective-permute-done | bytes 49184 | tf_op jit(solution)/shard_map/ppermute | solution.py:50
  105.3 5.6 %substep_1.1 = (f32[8,256]{1,0:T(8,128)S(1)}, f32[8,256]{1,0:T(8,128)S(1)}, f32[8,256]{1,0:T(8,128)S(1)}) custom-call(s32[8]{0:T(128)S(1)} %concatenate.44.meta_ref, f32[8,256]{1,0:T(8,128)S(1)} %get-tuple-element.97.start_ref, s32[224,2]{1,0:T(8,128)S(1)} %bitcast.45, f32[8,256]{1,0:T(8,128)S(1)} %get-tuple-element.68.speed_ref, ...), custom_call_target="tpu_custom_call" | custom-call | tf_op jit(solution)/shard_map/substep_1/pallas_call | solution.py:752
  110.9 1.7 collective-permute-start.29
  112.6 1.0 collective-permute-done.29
  113.6 2.4 %collective-permute-start.30 = (f32[16,256]{1,0:T(8,128)S(1)}, f32[16,256]{1,0:T(8,128)S(1)}, u32[]{:S(2)}, u32[]{:S(2)}) collective-permute-start(f32[16,256]{1,0:T(8,128)S(1)} %get-tuple-element.84), channel_id=1, source_target_pairs={{0,2},{2,4},{4,6},{6,0},{1,3},{3,5},{5,7},{7,1},{8,10},{10,12},{12... | collective-permute-start | bytes 49160 | tf_op jit(solution)/shard_map/ppermute | solution.py:50
  116.0 0.9 collective-permute-done.30
  116.8 2.3 %collective-permute-done.31 = f32[16,256]{1,0:T(8,128)S(1)} collective-permute-done((f32[16,256]{1,0:T(8,128)S(1)}, f32[16,256]{1,0:T(8,128)S(1)}, u32[]{:S(2)}, u32[]{:S(2)}) %collective-permute-start.31) | collective-permute-done | bytes 16416 | tf_op jit(solution)/shard_map/ppermute | solution.py:50
  119.1 0.4 collective-permute-start.33
  119.6 1.0 collective-permute-start.32
  120.6 7.5 %collide_residents_0.1 = (f32[3,528,128]{2,1,0:T(8,128)}, f32[3,528,128]{2,1,0:T(8,128)}) custom-call(s32[8]{0:T(128)S(1)} %concatenate.44.meta_ref, f32[2,8,128]{2,1,0:T(8,128)S(1)} %broadcast_in_dim.4.dirs_ref, bf16[256,304]{1,0:T(8,128)(2,1)S(1)} %get-tuple-element.54.table_ref, f32[3,384,128]{2,1,0:T(8,128)S(1)} %bitcast.34, f32[3,384,128]{2,1,0:T(8,128)S(1)} %bitcast.39), custom_call_target="tpu_custom_call" | custom-call | tf_op jit(solution)/shard_map/collide_residents_0/pallas_call | solution.py:724
  128.1 7.5 %collide_residents_1.1 = (f32[3,528,128]{2,1,0:T(8,128)}, f32[3,528,128]{2,1,0:T(8,128)}) custom-call(s32[8]{0:T(128)S(1)} %concatenate.44.meta_ref, f32[2,8,128]{2,1,0:T(8,128)S(1)} %broadcast_in_dim.4.dirs_ref, bf16[256,304]{1,0:T(8,128)(2,1)S(1)} %get-tuple-element.54.table_ref, ...), custom_call_target="tpu_custom_call", output_to_operand_aliasing={{0}: (5, {}), {1}: (6, {})} | custom-call | tf_op jit(solution)/shard_map/collide_residents_1/pallas_call | solution.py:724
  135.6 7.7 %collide_residents_2.1 = (f32[3,528,128]{2,1,0:T(8,128)}, f32[3,528,128]{2,1,0:T(8,128)}) custom-call(s32[8]{0:T(128)S(1)} %concatenate.44.meta_ref, f32[2,8,128]{2,1,0:T(8,128)S(1)} %broadcast_in_dim.4.dirs_ref, bf16[256,304]{1,0:T(8,128)(2,1)S(1)} %get-tuple-element.54.table_ref, ...), custom_call_target="tpu_custom_call", output_to_operand_aliasing={{0}: (5, {}), {1}: (6, {})} | custom-call | tf_op jit(solution)/shard_map/collide_residents_2/pallas_call | solution.py:724
  143.4 6.0 %collide_residents_3.1 = (f32[3,528,128]{2,1,0:T(8,128)}, f32[3,528,128]{2,1,0:T(8,128)}) custom-call(s32[8]{0:T(128)S(1)} %concatenate.44.meta_ref, f32[2,8,128]{2,1,0:T(8,128)S(1)} %broadcast_in_dim.4.dirs_ref, bf16[256,304]{1,0:T(8,128)(2,1)S(1)} %get-tuple-element.54.table_ref, ...), custom_call_target="tpu_custom_call", output_to_operand_aliasing={{0}: (5, {}), {1}: (6, {})} | custom-call | tf_op jit(solution)/shard_map/collide_residents_3/pallas_call | solution.py:724
  149.3 10.4 %collide_arrivals.1 = (f32[3,528,128]{2,1,0:T(8,128)}, f32[3,528,128]{2,1,0:T(8,128)}) custom-call(s32[8]{0:T(128)S(1)} %concatenate.44.meta_ref, f32[2,8,128]{2,1,0:T(8,128)S(1)} %broadcast_in_dim.4.dirs_ref, bf16[256,304]{1,0:T(8,128)(2,1)S(1)} %get-tuple-element.54.table_ref, ...), custom_call_target="tpu_custom_call", output_to_operand_aliasing={{0}: (9, {}), {1}: (10, {})} | custom-call | tf_op jit(solution)/shard_map/collide_arrivals/pallas_call | solution.py:738
  159.7 5.6 %substep_2.1 = (f32[8,256]{1,0:T(8,128)S(1)}, f32[8,256]{1,0:T(8,128)S(1)}) custom-call(s32[8]{0:T(128)S(1)} %concatenate.44.meta_ref, f32[8,256]{1,0:T(8,128)S(1)} %get-tuple-element.97.start_ref, s32[224,2]{1,0:T(8,128)S(1)} %bitcast.46, f32[8,256]{1,0:T(8,128)S(1)} %get-tuple-element.71.speed_ref, f32[8,256]{1,0:T(8,128)S(1)} %get-tuple-element.72.moved_ref, ...), custom_call_target="tpu_custom_call" | custom-call | tf_op jit(solution)/shard_map/substep_2/pallas_call | solution.py:752
  165.4 0.6 copy.34
  165.9 0.6 copy.35
  (74 shorter events, 0.7 us)
Async XLA Ops:
  1.3 0.7 copy-start.4
  2.0 50.4 %collective-permute-start.14 = (f32[8,256]{1,0:T(8,128)S(1)}, f32[8,256]{1,0:T(8,128)S(1)}, u32[]{:S(2)}, u32[]{:S(2)}) collective-permute-start(f32[8,256]{1,0:T(8,128)S(1)} %get-tuple-element.96), channel_id=1, source_target_pairs={{0,1},{1,0},{2,3},{3,2},{4,5},{5,4},{6,7},{7,6},{8,9},{9,8},{10,11... | collective-permute-start | bytes 24584 | tf_op jit(solution)/shard_map/ppermute | solution.py:50
  4.8 11.7 %collective-permute-start.11 = (s32[1,16,32]{2,1,0:T(8,128)S(1)}, s32[1,16,32]{2,1,0:T(8,128)S(1)}, u32[]{:S(2)}, u32[]{:S(2)}) collective-permute-start(s32[1,16,32]{2,1,0:T(8,128)S(1)} %slice.15), channel_id=1, source_target_pairs={{0,24},{8,0},{16,8},{24,16},{1,25},{9,1},{17,9},{25,17},{2,26},{10... | collective-permute-start | bytes 6152 | tf_op jit(solution)/shard_map/ppermute | solution.py:50
  8.1 1.3 copy-start.2
  8.1 8.4 %copy-start.3 = (s32[16,16,32]{2,1,0:T(8,128)S(1)}, s32[16,16,32]{2,1,0:T(8,128)}, u32[]{:S(2)}) copy-start(s32[16,16,32]{2,1,0:T(8,128)} %param.22) | copy-start | bytes 98308
  8.1 10.0 %copy-start.1 = (f32[3,1,1,1,49152]{4,3,2,1,0:T(1,128)S(1)}, f32[3,1,1,1,49152]{4,3,2,1,0:T(1,128)}, u32[]{:S(2)}) copy-start(f32[3,1,1,1,49152]{4,3,2,1,0:T(1,128)} %param.13) | copy-start | bytes 1769476
  9.3 8.7 %copy-start = (f32[3,1,1,1,49152]{4,3,2,1,0:T(1,128)S(1)}, f32[3,1,1,1,49152]{4,3,2,1,0:T(1,128)}, u32[]{:S(2)}) copy-start(f32[3,1,1,1,49152]{4,3,2,1,0:T(1,128)} %param.12) | copy-start | bytes 1769476
  10.2 25.6 %collective-permute-start = (f32[152,128]{1,0:T(8,128)S(1)}, f32[152,128]{1,0:T(8,128)S(1)}, u32[]{:S(2)}, u32[]{:S(2)}) collective-permute-start(f32[152,128]{1,0:T(8,128)S(1)} %get-tuple-element.40), channel_id=1, source_target_pairs={{0,8},{8,16},{16,24},{24,0},{1,9},{9,17},{17,25},{25,1},{2,10},{10... | collective-permute-start | bytes 233480 | tf_op jit(solution)/shard_map/ppermute | solution.py:50
  10.3 25.6 %collective-permute-start.1 = (f32[152,128]{1,0:T(8,128)S(1)}, f32[152,128]{1,0:T(8,128)S(1)}, u32[]{:S(2)}, u32[]{:S(2)}) collective-permute-start(f32[152,128]{1,0:T(8,128)S(1)} %get-tuple-element.41), channel_id=1, source_target_pairs={{0,24},{8,0},{16,8},{24,16},{1,25},{9,1},{17,9},{25,17},{2,26},{10... | collective-permute-start | bytes 233480 | tf_op jit(solution)/shard_map/ppermute | solution.py:50
  13.5 23.8 %collective-permute-start.2 = (f32[152,128]{1,0:T(8,128)S(1)}, f32[152,128]{1,0:T(8,128)S(1)}, u32[]{:S(2)}, u32[]{:S(2)}) collective-permute-start(f32[152,128]{1,0:T(8,128)S(1)} %get-tuple-element.42), channel_id=1, source_target_pairs={{0,2},{2,4},{4,6},{6,0},{1,3},{3,5},{5,7},{7,1},{8,10},{10,12},{12... | collective-permute-start | bytes 233480 | tf_op jit(solution)/shard_map/ppermute | solution.py:50
  16.5 19.2 %collective-permute-start.12 = (s32[17,1,32]{2,1,0:T(1,128)S(1)}, s32[17,1,32]{2,1,0:T(1,128)S(1)}, u32[]{:S(2)}, u32[]{:S(2)}) collective-permute-start(s32[17,1,32]{2,1,0:T(1,128)S(1)} %slice.20), channel_id=1, source_target_pairs={{0,6},{2,0},{4,2},{6,4},{1,7},{3,1},{5,3},{7,5},{8,14},{10,8},{12,... | collective-permute-start | bytes 6536 | tf_op jit(solution)/shard_map/ppermute | solution.py:50
  16.6 0.7 copy-start.5
  17.3 0.7 copy-start.7
  35.7 4.2 %collective-permute-start.3 = (f32[152,128]{1,0:T(8,128)S(1)}, f32[152,128]{1,0:T(8,128)S(1)}, u32[]{:S(2)}, u32[]{:S(2)}) collective-permute-start(f32[152,128]{1,0:T(8,128)S(1)} %get-tuple-element.43), channel_id=1, source_target_pairs={{0,6},{2,0},{4,2},{6,4},{1,7},{3,1},{5,3},{7,5},{8,14},{10,8},{12,... | collective-permute-start | bytes 233480 | tf_op jit(solution)/shard_map/ppermute | solution.py:50
  35.8 4.2 %collective-permute-start.4 = (f32[152,128]{1,0:T(8,128)S(1)}, f32[152,128]{1,0:T(8,128)S(1)}, u32[]{:S(2)}, u32[]{:S(2)}) collective-permute-start(f32[152,128]{1,0:T(8,128)S(1)} %get-tuple-element.44), channel_id=1, source_target_pairs={{0,1},{1,0},{2,3},{3,2},{4,5},{5,4},{6,7},{7,6},{8,9},{9,8},{10,11... | collective-permute-start | bytes 233480 | tf_op jit(solution)/shard_map/ppermute | solution.py:50
  35.9 5.5 %collective-permute-start.5 = (f32[152,128]{1,0:T(8,128)S(1)}, f32[152,128]{1,0:T(8,128)S(1)}, u32[]{:S(2)}, u32[]{:S(2)}) collective-permute-start(f32[152,128]{1,0:T(8,128)S(1)} %get-tuple-element.45), channel_id=1, source_target_pairs={{0,1},{1,0},{2,3},{3,2},{4,5},{5,4},{6,7},{7,6},{8,9},{9,8},{10,11... | collective-permute-start | bytes 233480 | tf_op jit(solution)/shard_map/ppermute | solution.py:50
  37.4 24.3 %collective-permute-start.13 = (s32[17,17,1]{2,1,0:T(8,128)S(1)}, s32[17,17,1]{2,1,0:T(8,128)S(1)}, u32[]{:S(2)}, u32[]{:S(2)}) collective-permute-start(s32[17,17,1]{2,1,0:T(8,128)S(1)} %pad_add_fusion), channel_id=1, source_target_pairs={{0,1},{1,0},{2,3},{3,2},{4,5},{5,4},{6,7},{7,6},{8,9},{9,8},{10,11... | collective-permute-start | bytes 3476 | tf_op jit(solution)/shard_map/ppermute | solution.py:50
  49.1 5.1 %collective-permute-start.6 = (f32[2,24,128]{2,1,0:T(8,128)S(1)}, f32[2,24,128]{2,1,0:T(8,128)S(1)}, u32[]{:S(2)}, u32[]{:S(2)}) collective-permute-start(f32[2,24,128]{2,1,0:T(8,128)S(1)} %get-tuple-element.47), channel_id=1, source_target_pairs={{0,8},{8,16},{16,24},{24,0},{1,9},{9,17},{17,25},{25,1},{2,10},{10... | collective-permute-start | bytes 73736 | tf_op jit(solution)/shard_map/ppermute | solution.py:50
  49.2 5.1 %collective-permute-start.7 = (f32[2,24,128]{2,1,0:T(8,128)S(1)}, f32[2,24,128]{2,1,0:T(8,128)S(1)}, u32[]{:S(2)}, u32[]{:S(2)}) collective-permute-start(f32[2,24,128]{2,1,0:T(8,128)S(1)} %get-tuple-element.48), channel_id=1, source_target_pairs={{0,24},{8,0},{16,8},{24,16},{1,25},{9,1},{17,9},{25,17},{2,26},{10... | collective-permute-start | bytes 73736 | tf_op jit(solution)/shard_map/ppermute | solution.py:50
  52.4 4.0 %collective-permute-start.16 = (f32[16,256]{1,0:T(8,128)S(1)}, f32[16,256]{1,0:T(8,128)S(1)}, u32[]{:S(2)}, u32[]{:S(2)}) collective-permute-start(f32[16,256]{1,0:T(8,128)S(1)} %pad_maximum_fusion), channel_id=1, source_target_pairs={{0,6},{2,0},{4,2},{6,4},{1,7},{3,1},{5,3},{7,5},{8,14},{10,8},{12,... | collective-permute-start | bytes 49160 | tf_op jit(solution)/shard_map/ppermute | solution.py:50
  52.5 4.0 %collective-permute-start.15 = (f32[16,256]{1,0:T(8,128)S(1)}, f32[16,256]{1,0:T(8,128)S(1)}, u32[]{:S(2)}, u32[]{:S(2)}) collective-permute-start(f32[16,256]{1,0:T(8,128)S(1)} %pad_maximum_fusion), channel_id=1, source_target_pairs={{0,2},{2,4},{4,6},{6,0},{1,3},{3,5},{5,7},{7,1},{8,10},{10,12},{12... | collective-permute-start | bytes 49160 | tf_op jit(solution)/shard_map/ppermute | solution.py:50
  54.3 5.8 %collective-permute-start.8 = (f32[2,24,128]{2,1,0:T(8,128)S(1)}, f32[2,24,128]{2,1,0:T(8,128)S(1)}, u32[]{:S(2)}, u32[]{:S(2)}) collective-permute-start(f32[2,24,128]{2,1,0:T(8,128)S(1)} %get-tuple-element.50), channel_id=1, source_target_pairs={{0,2},{2,4},{4,6},{6,0},{1,3},{3,5},{5,7},{7,1},{8,10},{10,12},{12... | collective-permute-start | bytes 73736 | tf_op jit(solution)/shard_map/ppermute | solution.py:50
  55.6 4.5 %collective-permute-start.9 = (f32[2,24,128]{2,1,0:T(8,128)S(1)}, f32[2,24,128]{2,1,0:T(8,128)S(1)}, u32[]{:S(2)}, u32[]{:S(2)}) collective-permute-start(f32[2,24,128]{2,1,0:T(8,128)S(1)} %get-tuple-element.51), channel_id=1, source_target_pairs={{0,6},{2,0},{4,2},{6,4},{1,7},{3,1},{5,3},{7,5},{8,14},{10,8},{12,... | collective-permute-start | bytes 73736 | tf_op jit(solution)/shard_map/ppermute | solution.py:50
  55.6 0.7 copy-start.6
  56.5 5.5 %collective-permute-start.18 = (f32[48,256]{1,0:T(8,128)S(1)}, f32[48,256]{1,0:T(8,128)S(1)}, u32[]{:S(2)}, u32[]{:S(2)}) collective-permute-start(f32[48,256]{1,0:T(8,128)S(1)} %concatenate.50.a_ref), channel_id=1, source_target_pairs={{0,24},{8,0},{16,8},{24,16},{1,25},{9,1},{17,9},{25,17},{2,26},{10... | collective-permute-start | bytes 147464 | tf_op jit(solution)/shard_map/ppermute | solution.py:50
  60.1 4.7 %collective-permute-start.17 = (f32[48,256]{1,0:T(8,128)S(1)}, f32[48,256]{1,0:T(8,128)S(1)}, u32[]{:S(2)}, u32[]{:S(2)}) collective-permute-start(f32[48,256]{1,0:T(8,128)S(1)} %concatenate.50.a_ref), channel_id=1, source_target_pairs={{0,8},{8,16},{16,24},{24,0},{1,9},{9,17},{17,25},{25,1},{2,10},{10... | collective-permute-start | bytes 147464 | tf_op jit(solution)/shard_map/ppermute | solution.py:50
  60.3 10.3 %collective-permute-start.10 = (f32[8,304]{1,0:T(8,128)S(1)}, f32[8,304]{1,0:T(8,128)S(1)}, u32[]{:S(2)}, u32[]{:S(2)}) collective-permute-start(f32[8,304]{1,0:T(8,128)S(1)} %get-tuple-element.53), channel_id=1, source_target_pairs={{0,1},{1,0},{2,3},{3,2},{4,5},{5,4},{6,7},{7,6},{8,9},{9,8},{10,11... | collective-permute-start | bytes 29192 | tf_op jit(solution)/shard_map/ppermute | solution.py:50
  71.7 2.6 %collective-permute-start.19 = (f32[8,256]{1,0:T(8,128)S(1)}, f32[8,256]{1,0:T(8,128)S(1)}, u32[]{:S(2)}, u32[]{:S(2)}) collective-permute-start(f32[8,256]{1,0:T(8,128)S(1)} %get-tuple-element.67), channel_id=1, source_target_pairs={{0,1},{1,0},{2,3},{3,2},{4,5},{5,4},{6,7},{7,6},{8,9},{9,8},{10,11... | collective-permute-start | bytes 24584 | tf_op jit(solution)/shard_map/ppermute | solution.py:50
  74.2 5.2 %collective-permute-start.20 = (f32[16,256]{1,0:T(8,128)S(1)}, f32[16,256]{1,0:T(8,128)S(1)}, u32[]{:S(2)}, u32[]{:S(2)}) collective-permute-start(f32[16,256]{1,0:T(8,128)S(1)} %get-tuple-element.92), channel_id=1, source_target_pairs={{0,2},{2,4},{4,6},{6,0},{1,3},{3,5},{5,7},{7,1},{8,10},{10,12},{12... | collective-permute-start | bytes 49160 | tf_op jit(solution)/shard_map/ppermute | solution.py:50
  78.5 3.2 %collective-permute-start.21 = (f32[16,256]{1,0:T(8,128)S(1)}, f32[16,256]{1,0:T(8,128)S(1)}, u32[]{:S(2)}, u32[]{:S(2)}) collective-permute-start(f32[16,256]{1,0:T(8,128)S(1)} %get-tuple-element.92), channel_id=1, source_target_pairs={{0,6},{2,0},{4,2},{6,4},{1,7},{3,1},{5,3},{7,5},{8,14},{10,8},{12,... | collective-permute-start | bytes 49160 | tf_op jit(solution)/shard_map/ppermute | solution.py:50
  81.7 2.9 %collective-permute-start.23 = (f32[48,256]{1,0:T(8,128)S(1)}, f32[48,256]{1,0:T(8,128)S(1)}, u32[]{:S(2)}, u32[]{:S(2)}) collective-permute-start(f32[48,256]{1,0:T(8,128)S(1)} %constant_dynamic-update-slice_fusion.4.a_ref), channel_id=1, source_target_pairs={{0,24},{8,0},{16,8},{24,16},{1,25},{9,1},{17,9},{25,17},{2,26},{10... | collective-permute-start | bytes 147464 | tf_op jit(solution)/shard_map/ppermute | solution.py:50
  81.7 4.8 %collective-permute-start.22 = (f32[48,256]{1,0:T(8,128)S(1)}, f32[48,256]{1,0:T(8,128)S(1)}, u32[]{:S(2)}, u32[]{:S(2)}) collective-permute-start(f32[48,256]{1,0:T(8,128)S(1)} %constant_dynamic-update-slice_fusion.4.a_ref), channel_id=1, source_target_pairs={{0,8},{8,16},{16,24},{24,0},{1,9},{9,17},{17,25},{25,1},{2,10},{10... | collective-permute-start | bytes 147464 | tf_op jit(solution)/shard_map/ppermute | solution.py:50
  92.2 2.6 %collective-permute-start.24 = (f32[8,256]{1,0:T(8,128)S(1)}, f32[8,256]{1,0:T(8,128)S(1)}, u32[]{:S(2)}, u32[]{:S(2)}) collective-permute-start(f32[8,256]{1,0:T(8,128)S(1)} %get-tuple-element.70), channel_id=1, source_target_pairs={{0,1},{1,0},{2,3},{3,2},{4,5},{5,4},{6,7},{7,6},{8,9},{9,8},{10,11... | collective-permute-start | bytes 24584 | tf_op jit(solution)/shard_map/ppermute | solution.py:50
  94.8 3.3 %collective-permute-start.25 = (f32[16,256]{1,0:T(8,128)S(1)}, f32[16,256]{1,0:T(8,128)S(1)}, u32[]{:S(2)}, u32[]{:S(2)}) collective-permute-start(f32[16,256]{1,0:T(8,128)S(1)} %get-tuple-element.88), channel_id=1, source_target_pairs={{0,2},{2,4},{4,6},{6,0},{1,3},{3,5},{5,7},{7,1},{8,10},{10,12},{12... | collective-permute-start | bytes 49160 | tf_op jit(solution)/shard_map/ppermute | solution.py:50
  97.3 3.2 %collective-permute-start.26 = (f32[16,256]{1,0:T(8,128)S(1)}, f32[16,256]{1,0:T(8,128)S(1)}, u32[]{:S(2)}, u32[]{:S(2)}) collective-permute-start(f32[16,256]{1,0:T(8,128)S(1)} %get-tuple-element.88), channel_id=1, source_target_pairs={{0,6},{2,0},{4,2},{6,4},{1,7},{3,1},{5,3},{7,5},{8,14},{10,8},{12,... | collective-permute-start | bytes 49160 | tf_op jit(solution)/shard_map/ppermute | solution.py:50
  100.4 3.0 %collective-permute-start.28 = (f32[48,256]{1,0:T(8,128)S(1)}, f32[48,256]{1,0:T(8,128)S(1)}, u32[]{:S(2)}, u32[]{:S(2)}) collective-permute-start(f32[48,256]{1,0:T(8,128)S(1)} %constant_dynamic-update-slice_fusion.10.a_ref), channel_id=1, source_target_pairs={{0,24},{8,0},{16,8},{24,16},{1,25},{9,1},{17,9},{25,17},{2,26},{10... | collective-permute-start | bytes 147464 | tf_op jit(solution)/shard_map/ppermute | solution.py:50
  100.4 4.8 %collective-permute-start.27 = (f32[48,256]{1,0:T(8,128)S(1)}, f32[48,256]{1,0:T(8,128)S(1)}, u32[]{:S(2)}, u32[]{:S(2)}) collective-permute-start(f32[48,256]{1,0:T(8,128)S(1)} %constant_dynamic-update-slice_fusion.10.a_ref), channel_id=1, source_target_pairs={{0,8},{8,16},{16,24},{24,0},{1,9},{9,17},{17,25},{25,1},{2,10},{10... | collective-permute-start | bytes 147464 | tf_op jit(solution)/shard_map/ppermute | solution.py:50
  110.9 2.7 %collective-permute-start.29 = (f32[8,256]{1,0:T(8,128)S(1)}, f32[8,256]{1,0:T(8,128)S(1)}, u32[]{:S(2)}, u32[]{:S(2)}) collective-permute-start(f32[8,256]{1,0:T(8,128)S(1)} %get-tuple-element.73), channel_id=1, source_target_pairs={{0,1},{1,0},{2,3},{3,2},{4,5},{5,4},{6,7},{7,6},{8,9},{9,8},{10,11... | collective-permute-start | bytes 24584 | tf_op jit(solution)/shard_map/ppermute | solution.py:50
  113.6 3.2 %collective-permute-start.30 = (f32[16,256]{1,0:T(8,128)S(1)}, f32[16,256]{1,0:T(8,128)S(1)}, u32[]{:S(2)}, u32[]{:S(2)}) collective-permute-start(f32[16,256]{1,0:T(8,128)S(1)} %get-tuple-element.84), channel_id=1, source_target_pairs={{0,2},{2,4},{4,6},{6,0},{1,3},{3,5},{5,7},{7,1},{8,10},{10,12},{12... | collective-permute-start | bytes 49160 | tf_op jit(solution)/shard_map/ppermute | solution.py:50
  116.0 3.2 %collective-permute-start.31 = (f32[16,256]{1,0:T(8,128)S(1)}, f32[16,256]{1,0:T(8,128)S(1)}, u32[]{:S(2)}, u32[]{:S(2)}) collective-permute-start(f32[16,256]{1,0:T(8,128)S(1)} %get-tuple-element.84), channel_id=1, source_target_pairs={{0,6},{2,0},{4,2},{6,4},{1,7},{3,1},{5,3},{7,5},{8,14},{10,8},{12,... | collective-permute-start | bytes 49160 | tf_op jit(solution)/shard_map/ppermute | solution.py:50
  119.1 40.6 %collective-permute-start.33 = (f32[48,256]{1,0:T(8,128)S(1)}, f32[48,256]{1,0:T(8,128)S(1)}, u32[]{:S(2)}, u32[]{:S(2)}) collective-permute-start(f32[48,256]{1,0:T(8,128)S(1)} %constant_dynamic-update-slice_fusion.16.a_ref), channel_id=1, source_target_pairs={{0,24},{8,0},{16,8},{24,16},{1,25},{9,1},{17,9},{25,17},{2,26},{10... | collective-permute-start | bytes 147464 | tf_op jit(solution)/shard_map/ppermute | solution.py:50
  119.6 40.1 %collective-permute-start.32 = (f32[48,256]{1,0:T(8,128)S(1)}, f32[48,256]{1,0:T(8,128)S(1)}, u32[]{:S(2)}, u32[]{:S(2)}) collective-permute-start(f32[48,256]{1,0:T(8,128)S(1)} %constant_dynamic-update-slice_fusion.16.a_ref), channel_id=1, source_target_pairs={{0,8},{8,16},{16,24},{24,0},{1,9},{9,17},{17,25},{25,1},{2,10},{10... | collective-permute-start | bytes 147464 | tf_op jit(solution)/shard_map/ppermute | solution.py:50
where the time goes:
time: 166 us; the launch traced here: 167 us
  Pallas kernels  89.1 us (54%)
  starting transfers between devices  43.1 us (26%)
  waiting for transfers between devices  26.2 us (16%)
  local copies, waits for them, and re-layouts  5.55 us (3%)
  between operations  2.37 us (1%)
    ppermute x34, starting transfers between devices, moved_along(): lax.ppermute(value, axis, [(i, (i + by) % peers) for i in range(peers)])  43.1 us
    pallas_call x4, Pallas kernels, shards(): pl.pallas_call(functools.partial(collide_residents, cells, piece * count,...  28.7 us
    ppermute x34, waiting for transfers between devices, moved_along(): lax.ppermute(value, axis, [(i, (i + by) % peers) for i in range(peers)])  26.2 us
    pallas_call x1, Pallas kernels, shards(): pl.pallas_call(functools.partial(bin_residents, cells), out_shape=like(ce...  17.6 us
    pallas_call x3, Pallas kernels, shards(): pl.pallas_call(functools.partial(substep, sizes, lengths, last), out_shap...  16.9 us
    pallas_call x1, Pallas kernels, shards(): pl.pallas_call(functools.partial(collide_arrivals, cells, rows_here, face...  10.4 us
    pallas_call x1, Pallas kernels, shards(): pl.pallas_call(functools.partial(bin_arrivals, cells, face_rows), out_sha...  7.74 us
    pallas_call x1, Pallas kernels, shards(): pl.pallas_call(functools.partial(first_forces, sizes, lengths), out_shape...  5.72 us
  transfers between devices with their start and end apart: 34, of which 17 were waited for; matrix products, arithmetic and copies ran while one was open for 2% of the time, Pallas kernels for 43%

commit v1 on v0

v1 whole, which is shorter than its diff:
```python
import functools
import math

import jax
import jax.numpy as jnp
from jax import lax
from jax.experimental import pallas as pl
from jax.experimental.pallas import tpu as pltpu
from jax.sharding import PartitionSpec as P

UNITS = 16
NAXES = 32
CHAIN = 8
LANES = 128
GROUP = 8
TWIN = 2

bead_mass = 5.0
step_size = 0.02
spring = 30.0
reach_square = 2.25
cut_square = 2.0 ** (1.0 / 3.0)
turn_cosine = math.cos(130.0 * math.pi / 180.0)
turn_sine = math.sin(130.0 * math.pi / 180.0)
golden = math.pi * (3.0 - math.sqrt(5.0))
half_kick = 0.5 * step_size / bead_mass
far_own = 3000.0
far_ghost = 9000.0
vmem_limit = 48 * 1024 * 1024
NT = (((1,), (1,)), ((), ()))
NN = (((1,), (0,)), ((), ()))
exact = lax.Precision.HIGHEST
f32 = jnp.float32
bf16 = jnp.bfloat16


def params():
    return pltpu.CompilerParams(vmem_limit_bytes=vmem_limit)


def vmem():
    return pl.BlockSpec(memory_space=pltpu.VMEM)


def smem():
    return pl.BlockSpec(memory_space=pltpu.SMEM)


def moved_along(value, axis, by):
    peers = lax.axis_size(axis)
    return lax.ppermute(value, axis, [(i, (i + by) % peers) for i in range(peers)])


class Cells:
    def __init__(self, size_x, size_y, size_z):
        self.sx, self.sy, self.nz = size_x, size_y, size_z
        self.inner = size_x * size_y
        self.edges = size_x + size_y + 1
        self.rows = -(-(self.inner + self.edges) // 16) * 16
        self.middle = self.rows // 2
        self.per = self.inner // self.edges
        self.depths = size_z + 1
        self.extra = -(-self.depths // self.per)
        self.height = -(-(self.depths + self.extra) // GROUP) * GROUP


def levels_of(position, meta):
    return [
        jnp.floor(jnp.floor(position[d] * UNITS + meta[d].astype(f32)) * (1.0 / UNITS))
        - meta[3 + d].astype(f32)
        for d in range(3)
    ]


def edge_of(levels, cells):
    outer = (levels[0] == cells.sx) | (levels[1] == cells.sy)
    return outer, jnp.where(levels[0] == cells.sx, levels[1], cells.sy + 1 + levels[0])


def plane_of(levels, cells):
    outer, edge = edge_of(levels, cells)
    return jnp.where(outer, cells.inner + edge, levels[0] * cells.sy + levels[1])


def place_of(levels, cells):
    outer, edge = edge_of(levels, cells)
    fold = jnp.floor((levels[2] + 0.5) * (1.0 / cells.per))
    row = jnp.where(outer, cells.depths + fold, levels[2])
    column = jnp.where(
        outer,
        (levels[2] - fold * cells.per) * cells.edges + edge,
        levels[0] * cells.sy + levels[1],
    )
    return row, column


def wide(row):
    return jnp.broadcast_to(row, (16, LANES)).astype(bf16)


def one_hot(column, height):
    middle = height // 2
    ids = lax.broadcasted_iota(jnp.int32, (height, LANES), 0) - middle
    ids = ids.astype(f32).astype(bf16).reshape(height // 16, 16, LANES)
    column = column - middle
    one, zero = jnp.ones((), bf16), jnp.zeros((), bf16)
    pieces = [
        jnp.where(ids == wide(column[r : r + 1])[None], one, zero).reshape(height, LANES)
        for r in range(column.shape[0])
    ]
    return jnp.concatenate(pieces, axis=1)


def split(value):
    high = value.astype(bf16).astype(f32)
    return high, value - high


def spread_moments(depth, weight, velocity, cells):
    nz = cells.nz
    ids = lax.broadcasted_iota(jnp.int32, (nz, LANES), 0).astype(f32).astype(bf16)
    ids = ids.reshape(nz // 16, 16, LANES)
    row_ids = lax.broadcasted_iota(jnp.int32, (16, LANES), 0).astype(f32).astype(bf16)
    zero = jnp.zeros((), bf16)
    parts = [split(weight * velocity[d]) for d in range(3)]
    channels = [weight] + [p[0] for p in parts] + [p[1] for p in parts]
    pieces = []
    for r in range(depth.shape[0]):
        at = wide(depth[r : r + 1])
        here = ids == at[None]
        values = [wide(c[r : r + 1]) for c in channels]
        tiles = [jnp.where(here, v[None], zero).reshape(nz, LANES) for v in values]
        top = jnp.zeros((16, LANES), bf16)
        for c, v in enumerate(values):
            top = jnp.where(row_ids == c, v, top)
        top = jnp.where(at == nz, top, zero)
        pieces.append(
            jnp.concatenate(
                tiles[:4] + [top, jnp.zeros((nz - 16, LANES), bf16)] + tiles[4:], axis=0
            )
        )
    return jnp.concatenate(pieces, axis=1)


def bin_group(total_ref, position, velocity, weight, meta, cells):
    levels = levels_of(position, meta)
    hot = one_hot(plane_of(levels, cells), cells.rows)
    spread = spread_moments(levels[2], weight, velocity, cells)
    total_ref[...] += lax.dot_general(hot, spread, NT, preferred_element_type=f32)


def row_iota():
    return lax.broadcasted_iota(jnp.int32, (GROUP, LANES), 0)


def bin_residents(cells, first, count, meta_ref, pos_ref, vel_ref, *refs):
    total_ref = refs[-1]
    meta = [meta_ref[k] for k in range(8)]
    if first == 0:
        total_ref[...] = jnp.zeros_like(total_ref)
    else:
        total_ref[...] = refs[0][...]
    live_rows = meta[6] - first
    stride = GROUP * TWIN

    @pl.loop(0, jnp.clip((live_rows + stride - 1) // stride, 0, count // stride))
    def _(step):
        for part in range(TWIN):
            offset = pl.multiple_of(step * stride + part * GROUP, GROUP)
            rows = pl.ds(offset, GROUP)
            position = [pos_ref[d, rows, :] for d in range(3)]
            velocity = [vel_ref[d, rows, :] for d in range(3)]
            weight = jnp.where(row_iota() + offset < live_rows, 1.0, 0.0)
            bin_group(total_ref, position, velocity, weight, meta, cells)


def arrival_group(ref, first, step, face_rows):
    offset = pl.multiple_of(step * GROUP, GROUP)
    comps = [ref[pl.ds(first + c * face_rows + offset, GROUP), :] for c in range(6)]
    live = (row_iota() + offset).astype(f32) < ref[pl.ds(first + 6 * face_rows, GROUP), :]
    return comps[:3], comps[3:], live


def face_count(ref, first, face_rows):
    return jnp.max(ref[pl.ds(first + 6 * face_rows, GROUP), :]).astype(jnp.int32)


def bead_mask(chains):
    slot = row_iota() * LANES + lax.broadcasted_iota(jnp.int32, (GROUP, LANES), 1)
    return slot < CHAIN * chains


def bin_arrivals(cells, face_rows, places, meta_ref, *refs):
    count = len(refs) - 8
    sources = refs[:count]
    bead_pos_ref, bead_vel_ref, axis_ref, start_ref, total_ref, low_ref, high_ref, sums = refs[
        count:
    ]
    meta = [meta_ref[k] for k in range(8)]
    sums[...] = start_ref[...]
    weight = jnp.where(bead_mask(meta[7]), bead_mass, 0.0)
    bin_group(
        sums,
        [bead_pos_ref[d] for d in range(3)],
        [bead_vel_ref[d] for d in range(3)],
        weight,
        meta,
        cells,
    )
    for which, first in places:
        ref = sources[which]

        @pl.loop(0, (face_count(ref, first, face_rows) + GROUP - 1) // GROUP)
        def _(step):
            position, velocity, live = arrival_group(ref, first, step, face_rows)
            bin_group(sums, position, velocity, jnp.where(live, 1.0, 0.0), meta, cells)

    nz, inner = cells.nz, cells.inner
    lane = lax.broadcasted_iota(jnp.int32, (cells.rows, LANES), 1)
    main, rest = sums[:, :LANES], sums[:, LANES:]
    main = main + jnp.where(lane < nz, 0.0, rest)
    top = jnp.where(lane == 0, rest, rest + pltpu.roll(rest, LANES - 3, axis=1))
    total_ref[0] = main
    total_ref[1] = jnp.where(lane < 4, top, 0.0)
    axis = axis_ref[...].astype(f32)
    total_ref[1, :inner, nz : 2 * nz] = axis
    sx, sy = cells.sx, cells.sy
    low_ref[...] = jnp.zeros_like(low_ref)
    high_ref[...] = jnp.zeros_like(high_ref)
    for half in range(2):
        corner = inner + sy + 1
        low_ref[half, :sy, :] = total_ref[half, :sy, :]
        low_ref[half, sy : sy + 1, :] = total_ref[half, corner : corner + 1, :]
        high_ref[half, : sy + 1, :] = total_ref[half, inner : inner + sy + 1, :]


def add_faces_x(cells, total_ref, below_ref, above_ref, out_ref, low_ref, high_ref):
    sx, sy, inner = cells.sx, cells.sy, cells.inner
    corner = inner + sy + 1
    out_ref[...] = total_ref[...]
    low_ref[...] = jnp.zeros_like(low_ref)
    high_ref[...] = jnp.zeros_like(high_ref)
    for half in range(2):
        out_ref[half, :sy, :] += below_ref[half, :sy, :]
        out_ref[half, corner : corner + 1, :] += below_ref[half, sy : sy + 1, :]
        out_ref[half, inner : inner + sy + 1, :] += above_ref[half, : sy + 1, :]
        low_ref[half, :sx, :] = out_ref[half, pl.ds(0, sx, stride=sy), :]
        low_ref[half, sx : sx + 1, :] = out_ref[half, inner : inner + 1, :]
        high_ref[half, :sx, :] = out_ref[half, corner : corner + sx, :]
        high_ref[half, sx : sx + 1, :] = out_ref[half, inner + sy : inner + sy + 1, :]


def add_faces_y(cells, total_ref, below_ref, above_ref, out_ref, face_ref, sums):
    sx, sy, nz, inner = cells.sx, cells.sy, cells.nz, cells.inner
    corner = inner + sy + 1
    sums[...] = total_ref[...]
    for half in range(2):
        sums[half, pl.ds(0, sx, stride=sy), :] += below_ref[half, :sx, :]
        sums[half, inner : inner + 1, :] += below_ref[half, sx : sx + 1, :]
        sums[half, corner : corner + sx, :] += above_ref[half, :sx, :]
        sums[half, inner + sy : inner + sy + 1, :] += above_ref[half, sx : sx + 1, :]
    main = sums[0].T
    rest = sums[1].T
    out_ref[:LANES, :] = main
    out_ref[LANES : LANES + nz, :] = rest[nz : 2 * nz]
    out_ref[LANES + nz :, :] = jnp.zeros((GROUP, cells.rows), f32)
    out_ref[LANES + nz : LANES + nz + 4, :] = rest[:4]
    face_ref[...] = jnp.zeros_like(face_ref)
    for c in range(5):
        face_ref[c : c + 1, :] = out_ref[c * nz : c * nz + 1, :]
        face_ref[GROUP + c : GROUP + c + 1, :] = out_ref[5 * nz + c : 5 * nz + c + 1, :]


def cell_table(cells, total_ref, below_ref, above_ref, table_ref, sheet, edge):
    nz, inner, height = cells.nz, cells.inner, cells.height
    row_ids = lax.broadcasted_iota(jnp.int32, (nz, cells.rows), 0)
    parts = []
    tops = []
    for c in range(5):
        face = jnp.where(row_ids == 0, below_ref[GROUP + c : GROUP + c + 1, :], 0.0)
        parts.append(total_ref[c * nz : (c + 1) * nz, :] + face)
        tops.append(
            total_ref[5 * nz + c : 5 * nz + c + 1, :] + above_ref[c : c + 1, :]
        )
    mass = jnp.maximum(parts[0], 1.0)
    top_mass = jnp.maximum(tops[0], 1.0)
    values = [parts[4]] + [p / mass for p in parts[1:4]]
    top_values = [tops[4]] + [t / top_mass for t in tops[1:4]]
    sheet[...] = jnp.zeros_like(sheet)
    edge[...] = jnp.zeros_like(edge)
    lane = lax.broadcasted_iota(jnp.int32, (cells.extra, LANES), 1)
    spare = LANES - (cells.rows - inner)
    for c in range(4):
        base = c * height
        sheet[base : base + nz, :] = values[c][:, :inner]
        sheet[base + nz : base + nz + 1, :] = top_values[c][:, :inner]
        edge[base : base + nz, :] = jnp.concatenate(
            [values[c][:, inner:], jnp.zeros((nz, spare), f32)], axis=1
        )
        edge[base + nz : base + nz + 1, :] = jnp.concatenate(
            [top_values[c][:, inner:], jnp.zeros((1, spare), f32)], axis=1
        )
        folded = [jnp.zeros((cells.extra, LANES), f32) for _ in range(inner // LANES)]
        for m in range(cells.per):
            begin = m * cells.edges
            piece = edge[pl.ds(base + m, cells.extra, stride=cells.per), :]
            piece = pltpu.roll(piece, begin % LANES, axis=1) if begin % LANES else piece
            for t in range(inner // LANES):
                low, high = begin - t * LANES, begin + cells.edges - t * LANES
                if high > 0 and low < LANES:
                    folded[t] = jnp.where((lane >= low) & (lane < high), piece, folded[t])
        sheet[base + nz + 1 : base + nz + 1 + cells.extra, :] = jnp.concatenate(folded, axis=1)
    whole = sheet[...]
    high = whole.astype(bf16).astype(f32)
    low = (whole - high)[height:]
    table_ref[...] = jnp.concatenate([high, low], axis=0).astype(bf16)


def direction_table():
    counter = jnp.arange(LANES).astype(f32)
    height = 1.0 - (2.0 * counter + 1.0) / NAXES
    radius = jnp.sqrt(jnp.maximum(1.0 - height * height, 0.0))
    rows = jnp.stack([radius * jnp.cos(golden * counter), radius * jnp.sin(golden * counter)])
    return jnp.broadcast_to(rows[:, None], (2, GROUP, LANES))


def fold_rows(values):
    sub = lax.broadcasted_iota(jnp.int32, (GROUP, LANES), 0)
    step = GROUP // 2
    while step:
        upper = (sub & step) == 0
        half = len(values) // 2
        joined = []
        for a, b in zip(values[:half], values[half:]):
            a = a + pltpu.roll(a, GROUP - step, axis=0)
            b = b + pltpu.roll(b, step, axis=0)
            joined.append(jnp.where(upper, a, b))
        values = joined
        step //= 2
    return values[0]


def collide(position, velocity, meta, table, dirs_ref, cells):
    height = cells.height
    row, column = place_of(levels_of(position, meta), cells)
    found = lax.dot_general(
        table, one_hot(column, cells.inner), NN, preferred_element_type=f32
    )
    ids = lax.broadcasted_iota(jnp.int32, (height, LANES), 0).astype(f32)
    picked = [[] for _ in range(4)]
    for r in range(GROUP):
        block = found[:, r * LANES : (r + 1) * LANES]
        here = ids == row[r : r + 1]
        for c in range(4):
            value = block[c * height : (c + 1) * height]
            if c > 0:
                value = value + block[(3 + c) * height : (4 + c) * height]
            value = jnp.where(here, value, 0.0)
            picked[c].append(
                jnp.sum(value.reshape(height // GROUP, GROUP, LANES), axis=0)
            )
    picked = [fold_rows(p) for p in picked]
    axis, flow = picked[0].astype(jnp.int32), picked[1:]
    normal = [
        jnp.take_along_axis(dirs_ref[0], axis, axis=1, mode="promise_in_bounds"),
        jnp.take_along_axis(dirs_ref[1], axis, axis=1, mode="promise_in_bounds"),
        1.0 - (2.0 * picked[0] + 1.0) * (1.0 / NAXES),
    ]
    rel = [velocity[d] - flow[d] for d in range(3)]
    along = (1.0 - turn_cosine) * (
        normal[0] * rel[0] + normal[1] * rel[1] + normal[2] * rel[2]
    )
    result = []
    for d in range(3):
        e, f = (d + 1) % 3, (d + 2) % 3
        crossed = normal[e] * rel[f] - normal[f] * rel[e]
        result.append(
            flow[d] + (turn_cosine * rel[d] + turn_sine * crossed + along * normal[d])
        )
    return result


def passed(position, speed):
    return position - jnp.floor(position) - 0.5 + 3.0 * step_size * speed


def copy_out(pairs, sems):
    copies = [pltpu.make_async_copy(a, b, sems.at[k]) for k, (a, b) in enumerate(pairs)]
    for copy in copies:
        copy.start()
    for copy in copies:
        copy.wait()


def collide_residents(
    cells, first, count, meta_ref, dirs_ref, table_ref, pos_ref, vel_ref, *refs
):
    out_pos, out_vel, held_pos, held_vel, sems = refs[-5:]
    meta = [meta_ref[k] for k in range(8)]
    table = table_ref[...]
    live_rows = meta[6] - first
    held_pos[...] = jnp.zeros_like(held_pos)
    held_vel[...] = jnp.zeros_like(held_vel)
    stride = GROUP * TWIN

    @pl.loop(0, jnp.clip((live_rows + stride - 1) // stride, 0, count // stride))
    def _(step):
        for part in range(TWIN):
            offset = pl.multiple_of(step * stride + part * GROUP, GROUP)
            rows = pl.ds(offset, GROUP)
            position = [pos_ref[d, rows, :] for d in range(3)]
            velocity = [vel_ref[d, rows, :] for d in range(3)]
            live = row_iota() + offset < live_rows
            speed = collide(position, velocity, meta, table, dirs_ref, cells)
            for d in range(3):
                held_vel[d, rows, :] = jnp.where(live, speed[d], 0.0)
                held_pos[d, rows, :] = jnp.where(live, passed(position[d], speed[d]), 0.0)

    span = pl.ds(first, count)
    copy_out([(held_pos, out_pos.at[:, span, :]), (held_vel, out_vel.at[:, span, :])], sems)


def collide_arrivals(cells, first, face_rows, places, meta_ref, dirs_ref, table_ref, *refs):
    out_pos, out_vel, held_pos, held_vel, sems = refs[-5:]
    meta = [meta_ref[k] for k in range(8)]
    table = table_ref[...]
    held_pos[...] = jnp.zeros_like(held_pos)
    held_vel[...] = jnp.zeros_like(held_vel)
    for k, (which, begin) in enumerate(places):
        ref = refs[which]

        @pl.loop(0, (face_count(ref, begin, face_rows) + GROUP - 1) // GROUP)
        def _(step):
            position, velocity, live = arrival_group(ref, begin, step, face_rows)
            speed = collide(position, velocity, meta, table, dirs_ref, cells)
            rows = pl.ds(k * face_rows + pl.multiple_of(step * GROUP, GROUP), GROUP)
            for d in range(3):
                held_vel[d, rows, :] = jnp.where(live, speed[d], 0.0)
                held_pos[d, rows, :] = jnp.where(live, passed(position[d], speed[d]), 0.0)

    span = pl.ds(first, len(places) * face_rows)
    copy_out([(held_pos, out_pos.at[:, span, :]), (held_vel, out_vel.at[:, span, :])], sems)


def pack_faces(face_rows, pos_ref, vel_ref, rows_ref, *out_refs):
    for face, out_ref in enumerate(out_refs):
        for c in range(6):
            source = pos_ref if c < 3 else vel_ref
            for k in range(face_rows):
                out_ref[c * face_rows + k : c * face_rows + k + 1, :] = source[
                    c % 3, face : face + 1, k * LANES : (k + 1) * LANES
                ]
        out_ref[6 * face_rows :, :] = jnp.full((GROUP, LANES), rows_ref[face], jnp.int32).astype(
            f32
        )


def stack_rows(parts, *refs):
    out_ref = refs[-1]
    at = 0
    for which, begin, count in parts:
        out_ref[at : at + count, :] = refs[which][begin : begin + count, :]
        at += count


def slot_live(slots, chains, rows):
    return lax.broadcasted_iota(jnp.int32, (rows, slots), 1) < CHAIN * chains


def payload(position, live):
    slots = position.shape[1]
    row_ids = lax.broadcasted_iota(jnp.int32, (GROUP, slots), 0)
    flag = jnp.where(live, 1.0, 0.0)
    return jnp.where(row_ids == 3, flag, jnp.where(row_ids < 3, position, 0.0))


def forces(own, chains, bonds_ref, blocks, centre, lengths):
    slots = own.shape[1]
    bond_slots = bonds_ref.shape[0]
    row_ids = lax.broadcasted_iota(jnp.int32, (GROUP, slots), 0)
    mid = jnp.zeros((GROUP, slots), f32)
    length = jnp.ones((GROUP, slots), f32)
    for d in range(3):
        mid = jnp.where(row_ids == d, centre[d], mid)
        length = jnp.where(row_ids == d, lengths[d], length)
    local = jnp.where(row_ids < 3, own - mid, 0.0)
    live = slot_live(slots, chains, GROUP)
    here = jnp.where(live, local, far_own)
    mine = [here[d : d + 1] for d in range(3)]
    total = [jnp.zeros((32, slots), f32) for _ in range(3)]
    for ref in blocks:
        for b in range(ref.shape[0] // GROUP):
            block = ref[b * GROUP : (b + 1) * GROUP, :]
            near = block - mid
            near = near - length * jnp.floor(near / length + 0.5)
            near = jnp.where(block[3:4] > 0.5, near, far_ghost)
            columns = near.T

            for k in range(slots // 32):
                differ = [mine[d] - columns[k * 32 : (k + 1) * 32, d : d + 1] for d in range(3)]
                square = (
                    differ[0] * differ[0] + differ[1] * differ[1] + differ[2] * differ[2]
                )
                inside = (square < cut_square) & (square > 0.25)
                inverse = 1.0 / jnp.where(inside, square, 1.0)
                sixth = inverse * inverse * inverse
                weight = jnp.where(
                    inside, 24.0 * (2.0 * sixth * sixth - sixth) * inverse, 0.0
                )
                total = [total[d] + weight * differ[d] for d in range(3)]
    pair = jnp.zeros((GROUP, slots), f32)
    for d in range(3):
        pair = jnp.where(row_ids == d, jnp.sum(total[d], axis=0, keepdims=True), pair)
    slot_ids = lax.broadcasted_iota(jnp.int32, (bond_slots, slots), 1)
    bond_ids = lax.broadcasted_iota(jnp.int32, (bond_slots, slots), 0)
    ends = bonds_ref[...]
    first = jnp.where(slot_ids == ends[:, 0:1], 1.0, 0.0)
    second = jnp.where(slot_ids == ends[:, 1:2], 1.0, 0.0)
    joins = jnp.where(bond_ids < (CHAIN - 1) * chains, first - second, 0.0)
    stretch = lax.dot_general(
        jnp.where(live, local, 0.0), joins, NT, precision=exact, preferred_element_type=f32
    )
    square = (
        stretch[0:1] * stretch[0:1] + stretch[1:2] * stretch[1:2] + stretch[2:3] * stretch[2:3]
    )
    bond_live = (
        lax.broadcasted_iota(jnp.int32, (1, bond_slots), 1) < (CHAIN - 1) * chains
    )
    pull = jnp.where(bond_live, -spring / (1.0 - square / reach_square), 0.0) * stretch
    return pair + lax.dot_general(pull, joins, NN, precision=exact, preferred_element_type=f32)


def centre_of(meta, sizes):
    return [meta[3 + d].astype(f32) + 0.5 * sizes[d] for d in range(3)]


def first_forces(sizes, lengths, meta_ref, start_ref, bonds_ref, a_ref, b_ref, c_ref, push_ref):
    meta = [meta_ref[k] for k in range(8)]
    push_ref[...] = forces(
        start_ref[...],
        meta[7],
        bonds_ref,
        [a_ref, b_ref, c_ref],
        centre_of(meta, sizes),
        lengths,
    )


def finish_cells(
    cells,
    meta_ref,
    dirs_ref,
    total_ref,
    below_ref,
    above_ref,
    bead_pos_ref,
    bead_vel_ref,
    start_ref,
    push_ref,
    table_ref,
    speed_ref,
    moved_ref,
    pay_ref,
    sheet,
    edge,
):
    meta = [meta_ref[k] for k in range(8)]
    cell_table(cells, total_ref, below_ref, above_ref, table_ref, sheet, edge)
    fresh = collide(
        [bead_pos_ref[d] for d in range(3)],
        [bead_vel_ref[d] for d in range(3)],
        meta,
        table_ref[...],
        dirs_ref,
        cells,
    )
    start = start_ref[...]
    slots = start.shape[1]
    row_ids = lax.broadcasted_iota(jnp.int32, (GROUP, slots), 0)
    speed = jnp.zeros((GROUP, slots), f32)
    for d in range(3):
        line = jnp.concatenate([fresh[d][k : k + 1] for k in range(slots // LANES)], axis=1)
        speed = jnp.where(row_ids == d, line, speed)
    speed = speed + half_kick * push_ref[...]
    moved = step_size * speed
    live = slot_live(slots, meta[7], GROUP)
    speed_ref[...] = speed
    moved_ref[...] = moved
    pay_ref[...] = payload(start + moved, live)


def substep(
    sizes,
    lengths,
    last,
    meta_ref,
    start_ref,
    bonds_ref,
    speed_ref,
    moved_ref,
    a_ref,
    b_ref,
    c_ref,
    order_ref,
    speed_out,
    moved_out,
    *pay_refs,
):
    meta = [meta_ref[k] for k in range(8)]
    start = start_ref[...]
    moved = moved_ref[...]
    push = forces(
        start + moved, meta[7], bonds_ref, [a_ref, b_ref, c_ref], centre_of(meta, sizes), lengths
    )
    live = slot_live(start.shape[1], meta[7], GROUP)
    speed = speed_ref[...] + half_kick * push
    if last:
        speed_out[...] = jnp.where(live, speed, 0.0)[:3]
        moved_out[...] = jnp.where(live, moved, 0.0)[:3]
        return
    speed = speed + half_kick * push
    moved = moved + step_size * speed
    speed_out[...] = speed
    moved_out[...] = moved
    pay_refs[0][...] = payload(start + moved, live)


def neighbours(value, axis):
    peers = lax.axis_size(axis)
    if peers == 2:
        return [moved_along(value, axis, 1)]
    return [moved_along(value, axis, 1), moved_along(value, axis, -1)]


def stacked(parts, operands, order=()):
    rows = sum(count for _, _, count in parts)
    width = operands[0].shape[1]
    return pl.pallas_call(
        functools.partial(stack_rows, tuple(parts)),
        out_shape=like(rows, width),
        in_specs=[vmem()] * len(operands) + [pl.BlockSpec(memory_space=pl.ANY)] * len(order),
        out_specs=vmem(),
        compiler_params=params(),
        name="stack_rows",
    )(*operands, *order)


def whole_rows(operands):
    return [(k, 0, value.shape[0]) for k, value in enumerate(operands)]


def halo(block, pieces):
    parts = [block] + neighbours(block, "gz")
    row = stacked(whole_rows(parts), parts, [pieces[0]()])
    parts = [row] + neighbours(row, "gy")
    plane = stacked(whole_rows(parts), parts, [pieces[1]()])
    sides = neighbours(plane, "gx")
    return [plane] + sides + sides[: 2 - len(sides)], pieces[2]()


def like(*shape, dtype=f32):
    return jax.ShapeDtypeStruct(shape, dtype)


def shards(
    sol_pos,
    sol_vel,
    sol_rows,
    mig_pos,
    mig_vel,
    mig_rows,
    bead_pos,
    bead_vel,
    bead_chains,
    bond_list,
    cell_axis,
    shift,
):
    sizes = cell_axis.shape
    cells = Cells(*sizes)
    names = ("gx", "gy", "gz")
    lengths = tuple(float(sizes[d] * lax.axis_size(names[d])) for d in range(3))
    slots_here = sol_pos.shape[-1]
    buffer_slots = mig_pos.shape[-1]
    bead_slots = bead_pos.shape[-1]
    bond_slots = bond_list.shape[-1]
    rows_here = slots_here // LANES
    face_rows = buffer_slots // LANES
    rows_all = rows_here + 6 * face_rows
    anchor = jnp.stack([lax.axis_index(names[d]) * sizes[d] for d in range(3)])
    meta = jnp.concatenate(
        [shift, anchor.astype(jnp.int32), sol_rows.reshape(1), bead_chains.reshape(1)]
    )
    dirs = direction_table()
    position = sol_pos.reshape(3, rows_here, LANES)
    velocity = sol_vel.reshape(3, rows_here, LANES)

    any_spec = pl.BlockSpec(memory_space=pl.ANY)
    face_height = 6 * face_rows + GROUP
    packed = pl.pallas_call(
        functools.partial(pack_faces, face_rows),
        out_shape=[like(face_height, LANES)] * 6,
        in_specs=[vmem(), vmem(), smem()],
        out_specs=[vmem()] * 6,
        compiler_params=params(),
        name="pack_faces",
    )(
        mig_pos.reshape(3, 6, buffer_slots),
        mig_vel.reshape(3, 6, buffer_slots),
        mig_rows.reshape(6),
    )

    bead_flat = bead_pos.reshape(3, bead_slots)
    start = jnp.pad(bead_flat, ((0, GROUP - 3), (0, 0)))
    tiles = bead_slots // LANES
    bead_pad = ((0, 0), (0, GROUP - tiles), (0, 0))
    bead_rows_pos = jnp.pad(bead_pos.reshape(3, tiles, LANES), bead_pad)
    bead_rows_vel = jnp.pad(bead_vel.reshape(3, tiles, LANES), bead_pad)
    bonds = bond_list.reshape(2, bond_slots).T
    bead_live = jnp.arange(bead_slots, dtype=jnp.int32) < CHAIN * bead_chains.reshape(())
    first_pay = jnp.concatenate(
        [bead_flat, bead_live.astype(f32)[None], jnp.zeros((GROUP - 4, bead_slots), f32)], axis=0
    )
    block = first_pay.reshape(GROUP, tiles, LANES).transpose(1, 0, 2).reshape(-1, LANES)

    thirds = 3
    count = rows_here // thirds
    axis_rows = cell_axis.reshape(cells.inner, sizes[2])

    def bin_piece(piece, earlier, order):
        return pl.pallas_call(
            functools.partial(bin_residents, cells, piece * count, count),
            out_shape=like(cells.rows, 2 * LANES),
            grid=(1,),
            in_specs=[smem()]
            + [pl.BlockSpec((3, count, LANES), lambda i, p=piece: (0, p, 0))] * 2
            + [vmem()] * len(earlier)
            + [any_spec] * len(order),
            out_specs=vmem(),
            compiler_params=params(),
            name=f"bin_residents_{piece}",
        )(meta, position, velocity, *earlier, *order)

    def swap(axis, low, high, body):
        if lax.axis_size(axis) == 2:
            both = [packed[low], packed[high], body]
            came = moved_along(stacked(whole_rows(both), both), axis, 1)
            return [came], [(0, face_height), (0, 0)], [(0, 2 * face_height)]
        up = stacked(whole_rows([packed[high], body]), [packed[high], body])
        down = stacked(whole_rows([packed[low], body]), [packed[low], body])
        came = [moved_along(up, axis, 1), moved_along(down, axis, -1)]
        return came, [(0, 0), (1, 0)], [(0, face_height), (1, face_height)]

    arrived, places, blocks = {}, {}, block
    totals = None
    for piece, (axis, low) in enumerate((("gz", 4), ("gy", 2), ("gx", 0))):
        came, spots, bodies = swap(axis, low, low + 1, blocks)
        totals = bin_piece(piece, [] if totals is None else [totals], [blocks])
        height = blocks.shape[0]
        arrived[axis], places[axis] = came, spots
        if axis != "gx":
            parts = [(0, 0, height)] + [(1 + w, at, height) for w, at in bodies]
            blocks = stacked(parts, [blocks] + came, [totals])
        else:
            around = [blocks] + [
                stacked([(0, at, height)], [came[w]]) for w, at in bodies
            ]
            around = around + around[1 : 1 + 3 - len(around)]

    def as_blocks(value):
        n = value.shape[0] // (GROUP * tiles)
        return (
            value.reshape(n, tiles, GROUP, LANES)
            .transpose(0, 2, 1, 3)
            .reshape(n * GROUP, bead_slots)
        )

    arriving, spots = [], []
    for axis in names:
        spots += [(len(arriving) + w, at) for w, at in places[axis]]
        arriving += arrived[axis]

    face_x = like(2, -(-(sizes[1] + 1) // GROUP) * GROUP, LANES)
    face_y = like(2, -(-(sizes[0] + 1) // GROUP) * GROUP, LANES)
    totals, low, high = pl.pallas_call(
        functools.partial(bin_arrivals, cells, face_rows, tuple(spots)),
        out_shape=[like(2, cells.rows, LANES), face_x, face_x],
        in_specs=[smem()] + [vmem()] * (len(arriving) + 4),
        out_specs=[vmem()] * 3,
        scratch_shapes=[pltpu.VMEM((cells.rows, 2 * LANES), f32)],
        compiler_params=params(),
        name="bin_arrivals",
    )(meta, *arriving, bead_rows_pos, bead_rows_vel, axis_rows, totals)

    push = pl.pallas_call(
        functools.partial(first_forces, sizes, lengths),
        out_shape=like(GROUP, bead_slots),
        in_specs=[smem()] + [vmem()] * 5,
        out_specs=vmem(),
        compiler_params=params(),
        name="first_forces",
    )(meta, start, bonds, *[as_blocks(value) for value in around])

    below, above = moved_along(high, "gx", 1), moved_along(low, "gx", -1)
    totals, low, high = pl.pallas_call(
        functools.partial(add_faces_x, cells),
        out_shape=[like(2, cells.rows, LANES), face_y, face_y],
        in_specs=[vmem()] * 3,
        out_specs=[vmem()] * 3,
        compiler_params=params(),
        name="add_faces_x",
    )(totals, below, above)
    below, above = moved_along(high, "gy", 1), moved_along(low, "gy", -1)
    totals, faces = pl.pallas_call(
        functools.partial(add_faces_y, cells),
        out_shape=[like(LANES + cells.nz + GROUP, cells.rows), like(2 * GROUP, cells.rows)],
        in_specs=[vmem()] * 3,
        out_specs=[vmem()] * 2,
        scratch_shapes=[pltpu.VMEM((2, cells.rows, LANES), f32)],
        compiler_params=params(),
        name="add_faces_y",
    )(totals, below, above)
    sides = neighbours(faces, "gz")
    below, above = sides[0], sides[-1]

    bead_shape = like(GROUP, bead_slots)
    table, speed, moved, pay = pl.pallas_call(
        functools.partial(finish_cells, cells),
        out_shape=[
            like(7 * cells.height, cells.inner, dtype=bf16),
            bead_shape,
            bead_shape,
            bead_shape,
        ],
        in_specs=[smem()] + [vmem()] * 8,
        out_specs=[vmem()] * 4,
        scratch_shapes=[
            pltpu.VMEM((4 * cells.height, cells.inner), f32),
            pltpu.VMEM((4 * cells.height, LANES), f32),
        ],
        compiler_params=params(),
        name="finish_cells",
    )(meta, dirs, totals, below, above, bead_rows_pos, bead_rows_vel, start, push)

    solvent_shape = like(3, rows_all, LANES)
    results = []
    cuts = 6
    span = rows_here // cuts

    def collide_piece(piece):
        earlier = list(results)
        if piece < cuts:
            body = functools.partial(collide_residents, cells, piece * span, span)
            rows = span
            sources = [position, velocity]
            specs = [pl.BlockSpec((3, span, LANES), lambda i: (0, piece, 0))] * 2
        else:
            begin = 2 * (piece - cuts)
            body = functools.partial(
                collide_arrivals,
                cells,
                rows_here + begin * face_rows,
                face_rows,
                tuple(spots[begin : begin + 2]),
            )
            rows = 2 * face_rows
            sources = arriving
            specs = [vmem()] * len(arriving)
        at = 3 + len(sources)
        results[:] = pl.pallas_call(
            body,
            out_shape=[solvent_shape] * 2,
            grid=(1,),
            in_specs=[smem(), vmem(), vmem()] + specs + [any_spec] * len(earlier),
            out_specs=[any_spec] * 2,
            scratch_shapes=[pltpu.VMEM((3, rows, LANES), f32)] * 2
            + [pltpu.SemaphoreType.DMA((2,))],
            input_output_aliases={at: 0, at + 1: 1} if earlier else {},
            compiler_params=params(),
            name=f"collide_{piece}",
        )(meta, dirs, table, *sources, *earlier)
        return results[1]

    for step in range(3):
        last = step == 2
        thunks = [functools.partial(collide_piece, 3 * step + k) for k in range(3)]
        ghosts, order = halo(pay, thunks)
        outcome = pl.pallas_call(
            functools.partial(substep, sizes, lengths, last),
            out_shape=[like(3, bead_slots)] * 2 if last else [bead_shape] * 3,
            in_specs=[smem()] + [vmem()] * 7 + [any_spec],
            out_specs=[vmem()] * (2 if last else 3),
            compiler_params=params(),
            name=f"substep_{step}",
        )(meta, start, bonds, speed, moved, *ghosts, order)
        speed, moved = outcome[:2]
        pay = outcome[-1]

    count_solvent = rows_all * LANES
    return (
        results[0].reshape(3, 1, 1, 1, count_solvent),
        results[1].reshape(3, 1, 1, 1, count_solvent),
        moved.reshape(3, 1, 1, 1, bead_slots),
        speed.reshape(3, 1, 1, 1, bead_slots),
    )


def solution(mesh):
    return jax.shard_map(
        shards,
        mesh=mesh,
        in_specs=(
            P(None, "gx", "gy", "gz", None),
            P(None, "gx", "gy", "gz", None),
            P("gx", "gy", "gz"),
            P(None, "gx", "gy", "gz", None, None),
            P(None, "gx", "gy", "gz", None, None),
            P("gx", "gy", "gz", None),
            P(None, "gx", "gy", "gz", None),
            P(None, "gx", "gy", "gz", None),
            P("gx", "gy", "gz"),
            P(None, "gx", "gy", "gz", None),
            P("gx", "gy", "gz"),
            P(),
        ),
        out_specs=(
            P(None, "gx", "gy", "gz", None),
            P(None, "gx", "gy", "gz", None),
            P(None, "gx", "gy", "gz", None),
            P(None, "gx", "gy", "gz", None),
        ),
        check_vma=False,
    )
```

time: 166 us -> 133 us (0.80)
  the two profiles are of different devices: /device:TPU:1 before, /device:TPU:0 now
where the time goes in v1:
time: 133 us; the launch traced here: 132 us
  Pallas kernels  69.8 us (52%)
  starting transfers between devices  28.9 us (22%)
  waiting for transfers between devices  16.2 us (12%)
  local copies, waits for them, and re-layouts  14.9 us (11%)
  between operations  2.45 us (2%)
    ppermute x25, starting transfers between devices, moved_along(): lax.ppermute(value, axis, [(i, (i + by) % peers) for i in range(peers)])  28.9 us
    pallas_call x9, Pallas kernels, collide_piece(): pl.pallas_call(body, out_shape=[solvent_shape] * 2, grid=(1,), in_specs=[...  26.9 us
    pallas_call x3, Pallas kernels, shards(): pl.pallas_call(functools.partial(substep, sizes, lengths, last), out_shap...  16.9 us
    ppermute x25, waiting for transfers between devices, moved_along(): lax.ppermute(value, axis, [(i, (i + by) % peers) for i in range(peers)])  16.2 us
    unnamed x39, local copies, waits for them, and re-layouts  14.8 us
    pallas_call x3, Pallas kernels, bin_piece(): pl.pallas_call(functools.partial(bin_residents, cells, piece * count, cou...  11.5 us
    pallas_call x1, Pallas kernels, shards(): pl.pallas_call(functools.partial(bin_arrivals, cells, face_rows, tuple(sp...  6.57 us
    pallas_call x1, Pallas kernels, shards(): pl.pallas_call(functools.partial(first_forces, sizes, lengths), out_shape...  5.73 us
  transfers between devices with their start and end apart: 25, of which 10 were waited for; matrix products, arithmetic and copies ran while one was open for 0% of the time, Pallas kernels for 33%

profile of v1, /device:TPU:0, one launch (start us, length us, event | category | flops | bytes accessed | tf_op | source)
XLA Modules:
  0.0 132.5 jit_solution(11409468132664187818)
XLA Ops:
  1.3 0.7 copy-done.13
  2.0 1.2 copy_bitcast_fusion
  3.4 0.8 pack_faces.1
  4.2 3.0 %collective-permute-start = (f32[320,128]{1,0:T(8,128)S(1)}, f32[320,128]{1,0:T(8,128)S(1)}, u32[]{:S(2)}, u32[]{:S(2)}) collective-permute-start(f32[320,128]{1,0:T(8,128)S(1)} %stack_rows.15), channel_id=1, source_target_pairs={{0,1},{1,0},{2,3},{3,2},{4,5},{5,4},{6,7},{7,6},{8,9},{9,8},{10,11... | collective-permute-start | bytes 491528 | tf_op jit(solution)/shard_map/ppermute | solution.py:51
  7.9 0.6 copy-done.16
  8.6 4.9 %bin_residents_0.1.refs_2_.refs_0_ = f32[304,256]{1,0:T(8,128)S(1)} custom-call(s32[8]{0:T(128)S(1)} %concatenate.9.meta_ref, f32[3,384,128]{2,1,0:T(8,128)S(1)} %bitcast.48, f32[3,384,128]{2,1,0:T(8,128)S(1)} %bitcast.57, f32[16,128]{1,0:T(8,128)S(1)} %maximum_bitcast_fusion.refs_2_.refs_0_), custom_call_target="tpu_custom_call" | custom-call | tf_op jit(solution)/shard_map/bin_residents_0/pallas_call | solution.py:731
  13.7 1.7 %collective-permute-start.2 = (f32[184,128]{1,0:T(8,128)S(1)}, f32[184,128]{1,0:T(8,128)S(1)}, u32[]{:S(2)}, u32[]{:S(2)}) collective-permute-start(f32[184,128]{1,0:T(8,128)S(1)} %stack_rows.18), channel_id=1, source_target_pairs={{0,6},{2,0},{4,2},{6,4},{1,7},{3,1},{5,3},{7,5},{8,14},{10,8},{12,... | collective-permute-start | bytes 282632 | tf_op jit(solution)/shard_map/ppermute | solution.py:51
  15.4 4.9 %bin_residents_1.1.refs_3_.refs_0_ = f32[304,256]{1,0:T(8,128)S(1)} custom-call(s32[8]{0:T(128)S(1)} %concatenate.9.meta_ref, f32[3,384,128]{2,1,0:T(8,128)S(1)} %bitcast.49, f32[3,384,128]{2,1,0:T(8,128)S(1)} %bitcast.58, f32[304,256]{1,0:T(8,128)S(1)} %bin_residents_0.1.refs_2_.refs_0_, f32[32,128]{1,0:T(8,128)S(1)} %stack_rows.16.refs_1_.refs_0_), custom_call_target="tpu_custom_call" | custom-call | tf_op jit(solution)/shard_map/bin_residents_1/pallas_call | solution.py:731
  20.5 3.8 %collective-permute-start.4 = (f32[248,128]{1,0:T(8,128)S(1)}, f32[248,128]{1,0:T(8,128)S(1)}, u32[]{:S(2)}, u32[]{:S(2)}) collective-permute-start(f32[248,128]{1,0:T(8,128)S(1)} %stack_rows.21), channel_id=1, source_target_pairs={{0,24},{8,0},{16,8},{24,16},{1,25},{9,1},{17,9},{25,17},{2,26},{10... | collective-permute-start | bytes 380936 | tf_op jit(solution)/shard_map/ppermute | solution.py:51
  24.4 1.7 %bin_residents_2.1.refs_8_ = f32[304,256]{1,0:T(8,128)S(1)} custom-call(s32[8]{0:T(128)S(1)} %concatenate.9.meta_ref, f32[3,384,128]{2,1,0:T(8,128)S(1)} %bitcast.50, f32[3,384,128]{2,1,0:T(8,128)S(1)} %bitcast.59, f32[304,256]{1,0:T(8,128)S(1)} %bin_residents_1.1.refs_3_.refs_0_, f32[96,128]{1,0:T(8,128)S(1)} %stack_rows.19.refs_1_), custom_call_target="tpu_custom_call" | custom-call | tf_op jit(solution)/shard_map/bin_residents_2/pallas_call | solution.py:731
  26.0 2.6 %collective-permute-done.3.refs_0_ = f32[248,128]{1,0:T(8,128)S(1)} collective-permute-done((f32[248,128]{1,0:T(8,128)S(1)}, f32[248,128]{1,0:T(8,128)S(1)}, u32[]{:S(2)}, u32[]{:S(2)}) %collective-permute-start.3) | collective-permute-done | bytes 127008 | tf_op jit(solution)/shard_map/ppermute | solution.py:51
  28.6 0.9 collective-permute-done.4.refs_1_.refs_0_
  29.4 6.6 %bin_arrivals.1 = (f32[2,304,128]{2,1,0:T(8,128)S(1)}, f32[2,24,128]{2,1,0:T(8,128)S(1)}, f32[2,24,128]{2,1,0:T(8,128)S(1)}) custom-call(s32[8]{0:T(128)S(1)} %concatenate.9.meta_ref, f32[248,128]{1,0:T(8,128)S(1)} %collective-permute-done.3.refs_0_, f32[248,128]{1,0:T(8,128)S(1)} %collective-permute-done.4.refs_1_.refs_0_, ...), custom_call_target="tpu_custom_call" | custom-call | tf_op jit(solution)/shard_map/bin_arrivals/pallas_call | solution.py:785
  36.0 1.8 %collective-permute-start.5 = (f32[2,24,128]{2,1,0:T(8,128)S(1)}, f32[2,24,128]{2,1,0:T(8,128)S(1)}, u32[]{:S(2)}, u32[]{:S(2)}) collective-permute-start(f32[2,24,128]{2,1,0:T(8,128)S(1)} %get-tuple-element.55), channel_id=1, source_target_pairs={{0,8},{8,16},{16,24},{24,0},{1,9},{9,17},{17,25},{25,1},{2,10},{10... | collective-permute-start | bytes 73736 | tf_op jit(solution)/shard_map/ppermute | solution.py:51
  37.9 2.0 %collective-permute-start.6 = (f32[2,24,128]{2,1,0:T(8,128)S(1)}, f32[2,24,128]{2,1,0:T(8,128)S(1)}, u32[]{:S(2)}, u32[]{:S(2)}) collective-permute-start(f32[2,24,128]{2,1,0:T(8,128)S(1)} %get-tuple-element.56), channel_id=1, source_target_pairs={{0,24},{8,0},{16,8},{24,16},{1,25},{9,1},{17,9},{25,17},{2,26},{10... | collective-permute-start | bytes 73736 | tf_op jit(solution)/shard_map/ppermute | solution.py:51
  39.9 1.9 %collective-permute-done.5.below_ref = f32[2,24,128]{2,1,0:T(8,128)S(1)} collective-permute-done((f32[2,24,128]{2,1,0:T(8,128)S(1)}, f32[2,24,128]{2,1,0:T(8,128)S(1)}, u32[]{:S(2)}, u32[]{:S(2)}) %collective-permute-start.5) | collective-permute-done | bytes 24608 | tf_op jit(solution)/shard_map/ppermute | solution.py:51
  42.1 1.7 %collective-permute-start.8 = (f32[2,24,128]{2,1,0:T(8,128)S(1)}, f32[2,24,128]{2,1,0:T(8,128)S(1)}, u32[]{:S(2)}, u32[]{:S(2)}) collective-permute-start(f32[2,24,128]{2,1,0:T(8,128)S(1)} %get-tuple-element.59), channel_id=1, source_target_pairs={{0,6},{2,0},{4,2},{6,4},{1,7},{3,1},{5,3},{7,5},{8,14},{10,8},{12,... | collective-permute-start | bytes 73736 | tf_op jit(solution)/shard_map/ppermute | solution.py:51
  43.8 1.5 %collective-permute-done.7.below_ref = f32[2,24,128]{2,1,0:T(8,128)S(1)} collective-permute-done((f32[2,24,128]{2,1,0:T(8,128)S(1)}, f32[2,24,128]{2,1,0:T(8,128)S(1)}, u32[]{:S(2)}, u32[]{:S(2)}) %collective-permute-start.7) | collective-permute-done | bytes 24608 | tf_op jit(solution)/shard_map/ppermute | solution.py:51
  45.3 0.2 add_faces_y.1
  45.5 1.3 %collective-permute-start.9 = (f32[16,304]{1,0:T(8,128)S(1)}, f32[16,304]{1,0:T(8,128)S(1)}, u32[]{:S(2)}, u32[]{:S(2)}) collective-permute-start(f32[16,304]{1,0:T(8,128)S(1)} %get-tuple-element.61), channel_id=1, source_target_pairs={{0,1},{1,0},{2,3},{3,2},{4,5},{5,4},{6,7},{7,6},{8,9},{9,8},{10,11... | collective-permute-start | bytes 58376 | tf_op jit(solution)/shard_map/ppermute | solution.py:51
  46.9 0.7 copy-done.15
  47.7 5.7 %first_forces.1.push_ref = f32[8,256]{1,0:T(8,128)S(1)} custom-call(s32[8]{0:T(128)S(1)} %concatenate.9.meta_ref, f32[8,256]{1,0:T(8,128)S(1)} %pad.13.start_ref, s32[224,2]{1,0:T(8,128)S(1)} %bitcast.66, f32[48,256]{1,0:T(8,128)S(1)} %bitcast.70, f32[48,256]{1,0:T(8,128)S(1)} %bitcast.71, f32[48,256]{1,0:T(8,128)S(1)} %bitcast.72), custom_call_target="tpu_custom_call" | custom-call | tf_op jit(solution)/shard_map/first_forces/pallas_call | solution.py:795
  53.5 1.0 finish_cells.1
  54.4 0.8 collective-permute-start.10
  55.3 3.4 %collide_0.1 = (f32[3,528,128]{2,1,0:T(8,128)}, f32[3,528,128]{2,1,0:T(8,128)}) custom-call(s32[8]{0:T(128)S(1)} %concatenate.9.meta_ref, f32[2,8,128]{2,1,0:T(8,128)S(1)} %broadcast_in_dim.4.dirs_ref, bf16[280,256]{1,0:T(8,128)(2,1)S(1)} %get-tuple-element.62.table_ref, f32[3,384,128]{2,1,0:T(8,128)S(1)} %bitcast.51, f32[3,384,128]{2,1,0:T(8,128)S(1)} %bitcast.60), custom_call_target="tpu_custom_call" | custom-call | tf_op jit(solution)/shard_map/collide_0/pallas_call | solution.py:870
  58.7 1.1 copy-done
  59.8 1.6 %collective-permute-start.12 = (f32[16,256]{1,0:T(8,128)S(1)}, f32[16,256]{1,0:T(8,128)S(1)}, u32[]{:S(2)}, u32[]{:S(2)}) collective-permute-start(f32[16,256]{1,0:T(8,128)S(1)} %stack_rows.24.refs_0_), channel_id=1, source_target_pairs={{0,6},{2,0},{4,2},{6,4},{1,7},{3,1},{5,3},{7,5},{8,14},{10,8},{12,... | collective-permute-start | bytes 49160 | tf_op jit(solution)/shard_map/ppermute | solution.py:51
  61.4 0.2 collective-permute-start.11
  61.6 3.6 %collide_1.1 = (f32[3,528,128]{2,1,0:T(8,128)}, f32[3,528,128]{2,1,0:T(8,128)}) custom-call(s32[8]{0:T(128)S(1)} %concatenate.9.meta_ref, f32[2,8,128]{2,1,0:T(8,128)S(1)} %broadcast_in_dim.4.dirs_ref, bf16[280,256]{1,0:T(8,128)(2,1)S(1)} %get-tuple-element.62.table_ref, f32[3,384,128]{2,1,0:T(8,128)S(1)} %bitcast.52, ...), custom_call_target="tpu_custom_call", output_to_operand_aliasing={{0}: (5, {}), {1}: (6, {})} | custom-call | tf_op jit(solution)/shard_map/collide_1/pallas_call | solution.py:870
  65.2 1.1 copy-done.1
  66.3 3.8 %collective-permute-start.14 = (f32[48,256]{1,0:T(8,128)S(1)}, f32[48,256]{1,0:T(8,128)S(1)}, u32[]{:S(2)}, u32[]{:S(2)}) collective-permute-start(f32[48,256]{1,0:T(8,128)S(1)} %stack_rows.25.a_ref), channel_id=1, source_target_pairs={{0,24},{8,0},{16,8},{24,16},{1,25},{9,1},{17,9},{25,17},{2,26},{10... | collective-permute-start | bytes 147464 | tf_op jit(solution)/shard_map/ppermute | solution.py:51
  70.1 3.4 %collide_2.1 = (f32[3,528,128]{2,1,0:T(8,128)}, f32[3,528,128]{2,1,0:T(8,128)}) custom-call(s32[8]{0:T(128)S(1)} %concatenate.9.meta_ref, f32[2,8,128]{2,1,0:T(8,128)S(1)} %broadcast_in_dim.4.dirs_ref, bf16[280,256]{1,0:T(8,128)(2,1)S(1)} %get-tuple-element.62.table_ref, f32[3,384,128]{2,1,0:T(8,128)S(1)} %bitcast.53, ...), custom_call_target="tpu_custom_call", output_to_operand_aliasing={{0}: (5, {}), {1}: (6, {})} | custom-call | tf_op jit(solution)/shard_map/collide_2/pallas_call | solution.py:870
  73.5 2.6 %collective-permute-done.13.b_ref = f32[48,256]{1,0:T(8,128)S(1)} collective-permute-done((f32[48,256]{1,0:T(8,128)S(1)}, f32[48,256]{1,0:T(8,128)S(1)}, u32[]{:S(2)}, u32[]{:S(2)}) %collective-permute-start.13) | collective-permute-done | bytes 49184 | tf_op jit(solution)/shard_map/ppermute | solution.py:51
  76.1 1.1 copy-done.2
  77.3 5.6 %substep_0.1 = (f32[8,256]{1,0:T(8,128)S(1)}, f32[8,256]{1,0:T(8,128)S(1)}, f32[8,256]{1,0:T(8,128)S(1)}) custom-call(s32[8]{0:T(128)S(1)} %concatenate.9.meta_ref, f32[8,256]{1,0:T(8,128)S(1)} %pad.13.start_ref, s32[224,2]{1,0:T(8,128)S(1)} %bitcast.67, f32[8,256]{1,0:T(8,128)S(1)} %get-tuple-element.81.speed_ref, ...), custom_call_target="tpu_custom_call" | custom-call | tf_op jit(solution)/shard_map/substep_0/pallas_call | solution.py:888
  82.9 1.0 collective-permute-start.15
  83.9 3.4 %collide_3.1 = (f32[3,528,128]{2,1,0:T(8,128)}, f32[3,528,128]{2,1,0:T(8,128)}) custom-call(s32[8]{0:T(128)S(1)} %concatenate.9.meta_ref, f32[2,8,128]{2,1,0:T(8,128)S(1)} %broadcast_in_dim.4.dirs_ref, bf16[280,256]{1,0:T(8,128)(2,1)S(1)} %get-tuple-element.62.table_ref, f32[3,384,128]{2,1,0:T(8,128)S(1)} %bitcast.54, ...), custom_call_target="tpu_custom_call", output_to_operand_aliasing={{0}: (5, {}), {1}: (6, {})} | custom-call | tf_op jit(solution)/shard_map/collide_3/pallas_call | solution.py:870
  87.3 1.1 copy-done.3
  88.5 0.2 collective-permute-start.17
  88.7 0.3 collective-permute-start.16
  89.0 2.3 %collide_4.1 = (f32[3,528,128]{2,1,0:T(8,128)}, f32[3,528,128]{2,1,0:T(8,128)}) custom-call(s32[8]{0:T(128)S(1)} %concatenate.9.meta_ref, f32[2,8,128]{2,1,0:T(8,128)S(1)} %broadcast_in_dim.4.dirs_ref, bf16[280,256]{1,0:T(8,128)(2,1)S(1)} %get-tuple-element.62.table_ref, f32[3,384,128]{2,1,0:T(8,128)S(1)} %bitcast.55, ...), custom_call_target="tpu_custom_call", output_to_operand_aliasing={{0}: (5, {}), {1}: (6, {})} | custom-call | tf_op jit(solution)/shard_map/collide_4/pallas_call | solution.py:870
  91.3 0.5 collective-permute-done.16.refs_1_
  91.8 1.1 copy-done.4
  93.0 1.7 %collective-permute-start.19 = (f32[48,256]{1,0:T(8,128)S(1)}, f32[48,256]{1,0:T(8,128)S(1)}, u32[]{:S(2)}, u32[]{:S(2)}) collective-permute-start(f32[48,256]{1,0:T(8,128)S(1)} %stack_rows.27.a_ref), channel_id=1, source_target_pairs={{0,24},{8,0},{16,8},{24,16},{1,25},{9,1},{17,9},{25,17},{2,26},{10... | collective-permute-start | bytes 147464 | tf_op jit(solution)/shard_map/ppermute | solution.py:51
  94.6 0.3 collective-permute-start.18
  95.0 1.5 %collide_5.1 = (f32[3,528,128]{2,1,0:T(8,128)}, f32[3,528,128]{2,1,0:T(8,128)}) custom-call(s32[8]{0:T(128)S(1)} %concatenate.9.meta_ref, f32[2,8,128]{2,1,0:T(8,128)S(1)} %broadcast_in_dim.4.dirs_ref, bf16[280,256]{1,0:T(8,128)(2,1)S(1)} %get-tuple-element.62.table_ref, f32[3,384,128]{2,1,0:T(8,128)S(1)} %bitcast.56, ...), custom_call_target="tpu_custom_call", output_to_operand_aliasing={{0}: (5, {}), {1}: (6, {})} | custom-call | tf_op jit(solution)/shard_map/collide_5/pallas_call | solution.py:870
  96.5 0.6 collective-permute-done.19.c_ref
  97.1 3.7 %collective-permute-done.18.b_ref = f32[48,256]{1,0:T(8,128)S(1)} collective-permute-done((f32[48,256]{1,0:T(8,128)S(1)}, f32[48,256]{1,0:T(8,128)S(1)}, u32[]{:S(2)}, u32[]{:S(2)}) %collective-permute-start.18) | collective-permute-done | bytes 49184 | tf_op jit(solution)/shard_map/ppermute | solution.py:51
  100.8 1.1 copy-done.5
  101.9 5.6 %substep_1.1 = (f32[8,256]{1,0:T(8,128)S(1)}, f32[8,256]{1,0:T(8,128)S(1)}, f32[8,256]{1,0:T(8,128)S(1)}) custom-call(s32[8]{0:T(128)S(1)} %concatenate.9.meta_ref, f32[8,256]{1,0:T(8,128)S(1)} %pad.13.start_ref, s32[224,2]{1,0:T(8,128)S(1)} %bitcast.68, f32[8,256]{1,0:T(8,128)S(1)} %get-tuple-element.84.speed_ref, ...), custom_call_target="tpu_custom_call" | custom-call | tf_op jit(solution)/shard_map/substep_1/pallas_call | solution.py:888
  107.6 0.7 collective-permute-start.20
  108.3 3.7 %collide_6.1 = (f32[3,528,128]{2,1,0:T(8,128)}, f32[3,528,128]{2,1,0:T(8,128)}) custom-call(s32[8]{0:T(128)S(1)} %concatenate.9.meta_ref, f32[2,8,128]{2,1,0:T(8,128)S(1)} %broadcast_in_dim.4.dirs_ref, bf16[280,256]{1,0:T(8,128)(2,1)S(1)} %get-tuple-element.62.table_ref, ...), custom_call_target="tpu_custom_call", output_to_operand_aliasing={{0}: (8, {}), {1}: (9, {})} | custom-call | tf_op jit(solution)/shard_map/collide_6/pallas_call | solution.py:870
  112.0 1.1 copy-done.6
  113.1 0.5 collective-permute-start.21
  113.7 2.9 %collide_7.1 = (f32[3,528,128]{2,1,0:T(8,128)}, f32[3,528,128]{2,1,0:T(8,128)}) custom-call(s32[8]{0:T(128)S(1)} %concatenate.9.meta_ref, f32[2,8,128]{2,1,0:T(8,128)S(1)} %broadcast_in_dim.4.dirs_ref, bf16[280,256]{1,0:T(8,128)(2,1)S(1)} %get-tuple-element.62.table_ref, ...), custom_call_target="tpu_custom_call", output_to_operand_aliasing={{0}: (8, {}), {1}: (9, {})} | custom-call | tf_op jit(solution)/shard_map/collide_7/pallas_call | solution.py:870
  116.6 1.1 copy-done.7
  117.8 0.9 collective-permute-start.24
  118.6 1.2 collective-permute-start.23
  119.8 2.8 %collide_8.1 = (f32[3,528,128]{2,1,0:T(8,128)}, f32[3,528,128]{2,1,0:T(8,128)}) custom-call(s32[8]{0:T(128)S(1)} %concatenate.9.meta_ref, f32[2,8,128]{2,1,0:T(8,128)S(1)} %broadcast_in_dim.4.dirs_ref, bf16[280,256]{1,0:T(8,128)(2,1)S(1)} %get-tuple-element.62.table_ref, ...), custom_call_target="tpu_custom_call", output_to_operand_aliasing={{0}: (8, {}), {1}: (9, {})} | custom-call | tf_op jit(solution)/shard_map/collide_8/pallas_call | solution.py:870
  122.7 1.9 %collective-permute-done.23.b_ref = f32[48,256]{1,0:T(8,128)S(1)} collective-permute-done((f32[48,256]{1,0:T(8,128)S(1)}, f32[48,256]{1,0:T(8,128)S(1)}, u32[]{:S(2)}, u32[]{:S(2)}) %collective-permute-start.23) | collective-permute-done | bytes 49184 | tf_op jit(solution)/shard_map/ppermute | solution.py:51
  124.5 1.1 copy-done.8
  125.7 5.6 %substep_2.1 = (f32[3,256]{1,0:T(4,128)S(1)}, f32[3,256]{1,0:T(4,128)S(1)}) custom-call(s32[8]{0:T(128)S(1)} %concatenate.9.meta_ref, f32[8,256]{1,0:T(8,128)S(1)} %pad.13.start_ref, s32[224,2]{1,0:T(8,128)S(1)} %bitcast.69, f32[8,256]{1,0:T(8,128)S(1)} %get-tuple-element.87.speed_ref, f32[8,256]{1,0:T(8,128)S(1)} %get-tuple-element.88.moved_ref, ...), custom_call_target="tpu_custom_call" | custom-call | tf_op jit(solution)/shard_map/substep_2/pallas_call | solution.py:888
  131.3 0.6 copy.42
  131.9 0.6 copy.43
  (73 shorter events, 1.0 us)
Async XLA Ops:
  1.3 0.7 copy-start.13
  2.0 1.3 copy-start.12
  2.0 6.6 %copy-start.10 = (f32[3,1,1,1,49152]{4,3,2,1,0:T(1,128)S(1)}, f32[3,1,1,1,49152]{4,3,2,1,0:T(1,128)}, u32[]{:S(2)}) copy-start(f32[3,1,1,1,49152]{4,3,2,1,0:T(1,128)} %param.13) | copy-start | bytes 1769476
  3.3 5.4 %copy-start.9 = (f32[3,1,1,1,49152]{4,3,2,1,0:T(1,128)S(1)}, f32[3,1,1,1,49152]{4,3,2,1,0:T(1,128)}, u32[]{:S(2)}) copy-start(f32[3,1,1,1,49152]{4,3,2,1,0:T(1,128)} %param.12) | copy-start | bytes 1769476
  4.2 9.3 %collective-permute-start = (f32[320,128]{1,0:T(8,128)S(1)}, f32[320,128]{1,0:T(8,128)S(1)}, u32[]{:S(2)}, u32[]{:S(2)}) collective-permute-start(f32[320,128]{1,0:T(8,128)S(1)} %stack_rows.15), channel_id=1, source_target_pairs={{0,1},{1,0},{2,3},{3,2},{4,5},{5,4},{6,7},{7,6},{8,9},{9,8},{10,11... | collective-permute-start | bytes 491528 | tf_op jit(solution)/shard_map/ppermute | solution.py:51
  7.9 0.7 copy-start.16
  13.6 6.7 %collective-permute-start.1 = (f32[184,128]{1,0:T(8,128)S(1)}, f32[184,128]{1,0:T(8,128)S(1)}, u32[]{:S(2)}, u32[]{:S(2)}) collective-permute-start(f32[184,128]{1,0:T(8,128)S(1)} %stack_rows.17), channel_id=1, source_target_pairs={{0,2},{2,4},{4,6},{6,0},{1,3},{3,5},{5,7},{7,1},{8,10},{10,12},{12... | collective-permute-start | bytes 282632 | tf_op jit(solution)/shard_map/ppermute | solution.py:51
  13.7 6.7 %collective-permute-start.2 = (f32[184,128]{1,0:T(8,128)S(1)}, f32[184,128]{1,0:T(8,128)S(1)}, u32[]{:S(2)}, u32[]{:S(2)}) collective-permute-start(f32[184,128]{1,0:T(8,128)S(1)} %stack_rows.18), channel_id=1, source_target_pairs={{0,6},{2,0},{4,2},{6,4},{1,7},{3,1},{5,3},{7,5},{8,14},{10,8},{12,... | collective-permute-start | bytes 282632 | tf_op jit(solution)/shard_map/ppermute | solution.py:51
  20.4 3.9 %copy-start.14 = (f32[3,1,1,1,256]{4,3,2,1,0:T(1,128)S(1)}, f32[3,1,1,1,256]{4,3,2,1,0:T(1,128)}, u32[]{:S(2)}) copy-start(f32[3,1,1,1,256]{4,3,2,1,0:T(1,128)} %param.19) | copy-start | bytes 9220
  20.4 8.1 %collective-permute-start.3 = (f32[248,128]{1,0:T(8,128)S(1)}, f32[248,128]{1,0:T(8,128)S(1)}, u32[]{:S(2)}, u32[]{:S(2)}) collective-permute-start(f32[248,128]{1,0:T(8,128)S(1)} %stack_rows.20), channel_id=1, source_target_pairs={{0,8},{8,16},{16,24},{24,0},{1,9},{9,17},{17,25},{25,1},{2,10},{10... | collective-permute-start | bytes 380936 | tf_op jit(solution)/shard_map/ppermute | solution.py:51
  20.5 8.9 %collective-permute-start.4 = (f32[248,128]{1,0:T(8,128)S(1)}, f32[248,128]{1,0:T(8,128)S(1)}, u32[]{:S(2)}, u32[]{:S(2)}) collective-permute-start(f32[248,128]{1,0:T(8,128)S(1)} %stack_rows.21), channel_id=1, source_target_pairs={{0,24},{8,0},{16,8},{24,16},{1,25},{9,1},{17,9},{25,17},{2,26},{10... | collective-permute-start | bytes 380936 | tf_op jit(solution)/shard_map/ppermute | solution.py:51
  24.3 5.1 %copy-start.11 = (s32[16,16,32]{2,1,0:T(8,128)S(1)}, s32[16,16,32]{2,1,0:T(8,128)}, u32[]{:S(2)}) copy-start(s32[16,16,32]{2,1,0:T(8,128)} %param.22) | copy-start | bytes 98308
  36.0 5.8 %collective-permute-start.5 = (f32[2,24,128]{2,1,0:T(8,128)S(1)}, f32[2,24,128]{2,1,0:T(8,128)S(1)}, u32[]{:S(2)}, u32[]{:S(2)}) collective-permute-start(f32[2,24,128]{2,1,0:T(8,128)S(1)} %get-tuple-element.55), channel_id=1, source_target_pairs={{0,8},{8,16},{16,24},{24,0},{1,9},{9,17},{17,25},{25,1},{2,10},{10... | collective-permute-start | bytes 73736 | tf_op jit(solution)/shard_map/ppermute | solution.py:51
  37.9 4.1 %collective-permute-start.6 = (f32[2,24,128]{2,1,0:T(8,128)S(1)}, f32[2,24,128]{2,1,0:T(8,128)S(1)}, u32[]{:S(2)}, u32[]{:S(2)}) collective-permute-start(f32[2,24,128]{2,1,0:T(8,128)S(1)} %get-tuple-element.56), channel_id=1, source_target_pairs={{0,24},{8,0},{16,8},{24,16},{1,25},{9,1},{17,9},{25,17},{2,26},{10... | collective-permute-start | bytes 73736 | tf_op jit(solution)/shard_map/ppermute | solution.py:51
  42.0 3.3 %collective-permute-start.7 = (f32[2,24,128]{2,1,0:T(8,128)S(1)}, f32[2,24,128]{2,1,0:T(8,128)S(1)}, u32[]{:S(2)}, u32[]{:S(2)}) collective-permute-start(f32[2,24,128]{2,1,0:T(8,128)S(1)} %get-tuple-element.58), channel_id=1, source_target_pairs={{0,2},{2,4},{4,6},{6,0},{1,3},{3,5},{5,7},{7,1},{8,10},{10,12},{12... | collective-permute-start | bytes 73736 | tf_op jit(solution)/shard_map/ppermute | solution.py:51
  42.1 3.3 %collective-permute-start.8 = (f32[2,24,128]{2,1,0:T(8,128)S(1)}, f32[2,24,128]{2,1,0:T(8,128)S(1)}, u32[]{:S(2)}, u32[]{:S(2)}) collective-permute-start(f32[2,24,128]{2,1,0:T(8,128)S(1)} %get-tuple-element.59), channel_id=1, source_target_pairs={{0,6},{2,0},{4,2},{6,4},{1,7},{3,1},{5,3},{7,5},{8,14},{10,8},{12,... | collective-permute-start | bytes 73736 | tf_op jit(solution)/shard_map/ppermute | solution.py:51
  45.5 7.9 %collective-permute-start.9 = (f32[16,304]{1,0:T(8,128)S(1)}, f32[16,304]{1,0:T(8,128)S(1)}, u32[]{:S(2)}, u32[]{:S(2)}) collective-permute-start(f32[16,304]{1,0:T(8,128)S(1)} %get-tuple-element.61), channel_id=1, source_target_pairs={{0,1},{1,0},{2,3},{3,2},{4,5},{5,4},{6,7},{7,6},{8,9},{9,8},{10,11... | collective-permute-start | bytes 58376 | tf_op jit(solution)/shard_map/ppermute | solution.py:51
  46.9 0.7 copy-start.15
  54.4 4.2 %collective-permute-start.10 = (f32[8,256]{1,0:T(8,128)S(1)}, f32[8,256]{1,0:T(8,128)S(1)}, u32[]{:S(2)}, u32[]{:S(2)}) collective-permute-start(f32[8,256]{1,0:T(8,128)S(1)} %get-tuple-element.83.refs_0_), channel_id=1, source_target_pairs={{0,1},{1,0},{2,3},{3,2},{4,5},{5,4},{6,7},{7,6},{8,9},{9,8},{10,11... | collective-permute-start | bytes 24584 | tf_op jit(solution)/shard_map/ppermute | solution.py:51
  58.7 1.1 copy-start
  59.8 5.3 %collective-permute-start.12 = (f32[16,256]{1,0:T(8,128)S(1)}, f32[16,256]{1,0:T(8,128)S(1)}, u32[]{:S(2)}, u32[]{:S(2)}) collective-permute-start(f32[16,256]{1,0:T(8,128)S(1)} %stack_rows.24.refs_0_), channel_id=1, source_target_pairs={{0,6},{2,0},{4,2},{6,4},{1,7},{3,1},{5,3},{7,5},{8,14},{10,8},{12,... | collective-permute-start | bytes 49160 | tf_op jit(solution)/shard_map/ppermute | solution.py:51
  61.4 3.8 %collective-permute-start.11 = (f32[16,256]{1,0:T(8,128)S(1)}, f32[16,256]{1,0:T(8,128)S(1)}, u32[]{:S(2)}, u32[]{:S(2)}) collective-permute-start(f32[16,256]{1,0:T(8,128)S(1)} %stack_rows.24.refs_0_), channel_id=1, source_target_pairs={{0,2},{2,4},{4,6},{6,0},{1,3},{3,5},{5,7},{7,1},{8,10},{10,12},{12... | collective-permute-start | bytes 49160 | tf_op jit(solution)/shard_map/ppermute | solution.py:51
  65.2 1.1 copy-start.1
  66.3 7.2 %collective-permute-start.14 = (f32[48,256]{1,0:T(8,128)S(1)}, f32[48,256]{1,0:T(8,128)S(1)}, u32[]{:S(2)}, u32[]{:S(2)}) collective-permute-start(f32[48,256]{1,0:T(8,128)S(1)} %stack_rows.25.a_ref), channel_id=1, source_target_pairs={{0,24},{8,0},{16,8},{24,16},{1,25},{9,1},{17,9},{25,17},{2,26},{10... | collective-permute-start | bytes 147464 | tf_op jit(solution)/shard_map/ppermute | solution.py:51
  70.1 6.0 %collective-permute-start.13 = (f32[48,256]{1,0:T(8,128)S(1)}, f32[48,256]{1,0:T(8,128)S(1)}, u32[]{:S(2)}, u32[]{:S(2)}) collective-permute-start(f32[48,256]{1,0:T(8,128)S(1)} %stack_rows.25.a_ref), channel_id=1, source_target_pairs={{0,8},{8,16},{16,24},{24,0},{1,9},{9,17},{17,25},{25,1},{2,10},{10... | collective-permute-start | bytes 147464 | tf_op jit(solution)/shard_map/ppermute | solution.py:51
  76.1 1.1 copy-start.2
  82.9 4.4 %collective-permute-start.15 = (f32[8,256]{1,0:T(8,128)S(1)}, f32[8,256]{1,0:T(8,128)S(1)}, u32[]{:S(2)}, u32[]{:S(2)}) collective-permute-start(f32[8,256]{1,0:T(8,128)S(1)} %get-tuple-element.86.refs_0_), channel_id=1, source_target_pairs={{0,1},{1,0},{2,3},{3,2},{4,5},{5,4},{6,7},{7,6},{8,9},{9,8},{10,11... | collective-permute-start | bytes 24584 | tf_op jit(solution)/shard_map/ppermute | solution.py:51
  87.3 1.1 copy-start.3
  88.5 2.8 %collective-permute-start.17 = (f32[16,256]{1,0:T(8,128)S(1)}, f32[16,256]{1,0:T(8,128)S(1)}, u32[]{:S(2)}, u32[]{:S(2)}) collective-permute-start(f32[16,256]{1,0:T(8,128)S(1)} %stack_rows.26.refs_0_), channel_id=1, source_target_pairs={{0,6},{2,0},{4,2},{6,4},{1,7},{3,1},{5,3},{7,5},{8,14},{10,8},{12,... | collective-permute-start | bytes 49160 | tf_op jit(solution)/shard_map/ppermute | solution.py:51
  88.7 3.2 %collective-permute-start.16 = (f32[16,256]{1,0:T(8,128)S(1)}, f32[16,256]{1,0:T(8,128)S(1)}, u32[]{:S(2)}, u32[]{:S(2)}) collective-permute-start(f32[16,256]{1,0:T(8,128)S(1)} %stack_rows.26.refs_0_), channel_id=1, source_target_pairs={{0,2},{2,4},{4,6},{6,0},{1,3},{3,5},{5,7},{7,1},{8,10},{10,12},{12... | collective-permute-start | bytes 49160 | tf_op jit(solution)/shard_map/ppermute | solution.py:51
  91.8 1.1 copy-start.4
  93.0 4.1 %collective-permute-start.19 = (f32[48,256]{1,0:T(8,128)S(1)}, f32[48,256]{1,0:T(8,128)S(1)}, u32[]{:S(2)}, u32[]{:S(2)}) collective-permute-start(f32[48,256]{1,0:T(8,128)S(1)} %stack_rows.27.a_ref), channel_id=1, source_target_pairs={{0,24},{8,0},{16,8},{24,16},{1,25},{9,1},{17,9},{25,17},{2,26},{10... | collective-permute-start | bytes 147464 | tf_op jit(solution)/shard_map/ppermute | solution.py:51
  94.6 6.1 %collective-permute-start.18 = (f32[48,256]{1,0:T(8,128)S(1)}, f32[48,256]{1,0:T(8,128)S(1)}, u32[]{:S(2)}, u32[]{:S(2)}) collective-permute-start(f32[48,256]{1,0:T(8,128)S(1)} %stack_rows.27.a_ref), channel_id=1, source_target_pairs={{0,8},{8,16},{16,24},{24,0},{1,9},{9,17},{17,25},{25,1},{2,10},{10... | collective-permute-start | bytes 147464 | tf_op jit(solution)/shard_map/ppermute | solution.py:51
  100.8 1.1 copy-start.5
  107.6 4.4 %collective-permute-start.20 = (f32[8,256]{1,0:T(8,128)S(1)}, f32[8,256]{1,0:T(8,128)S(1)}, u32[]{:S(2)}, u32[]{:S(2)}) collective-permute-start(f32[8,256]{1,0:T(8,128)S(1)} %get-tuple-element.89.refs_0_), channel_id=1, source_target_pairs={{0,1},{1,0},{2,3},{3,2},{4,5},{5,4},{6,7},{7,6},{8,9},{9,8},{10,11... | collective-permute-start | bytes 24584 | tf_op jit(solution)/shard_map/ppermute | solution.py:51
  112.0 1.1 copy-start.6
  113.1 3.5 %collective-permute-start.22 = (f32[16,256]{1,0:T(8,128)S(1)}, f32[16,256]{1,0:T(8,128)S(1)}, u32[]{:S(2)}, u32[]{:S(2)}) collective-permute-start(f32[16,256]{1,0:T(8,128)S(1)} %stack_rows.28.refs_0_), channel_id=1, source_target_pairs={{0,6},{2,0},{4,2},{6,4},{1,7},{3,1},{5,3},{7,5},{8,14},{10,8},{12,... | collective-permute-start | bytes 49160 | tf_op jit(solution)/shard_map/ppermute | solution.py:51
  113.1 3.5 %collective-permute-start.21 = (f32[16,256]{1,0:T(8,128)S(1)}, f32[16,256]{1,0:T(8,128)S(1)}, u32[]{:S(2)}, u32[]{:S(2)}) collective-permute-start(f32[16,256]{1,0:T(8,128)S(1)} %stack_rows.28.refs_0_), channel_id=1, source_target_pairs={{0,2},{2,4},{4,6},{6,0},{1,3},{3,5},{5,7},{7,1},{8,10},{10,12},{12... | collective-permute-start | bytes 49160 | tf_op jit(solution)/shard_map/ppermute | solution.py:51
  116.6 1.1 copy-start.7
  117.8 4.9 %collective-permute-start.24 = (f32[48,256]{1,0:T(8,128)S(1)}, f32[48,256]{1,0:T(8,128)S(1)}, u32[]{:S(2)}, u32[]{:S(2)}) collective-permute-start(f32[48,256]{1,0:T(8,128)S(1)} %stack_rows.29.a_ref), channel_id=1, source_target_pairs={{0,24},{8,0},{16,8},{24,16},{1,25},{9,1},{17,9},{25,17},{2,26},{10... | collective-permute-start | bytes 147464 | tf_op jit(solution)/shard_map/ppermute | solution.py:51
  118.6 5.9 %collective-permute-start.23 = (f32[48,256]{1,0:T(8,128)S(1)}, f32[48,256]{1,0:T(8,128)S(1)}, u32[]{:S(2)}, u32[]{:S(2)}) collective-permute-start(f32[48,256]{1,0:T(8,128)S(1)} %stack_rows.29.a_ref), channel_id=1, source_target_pairs={{0,8},{8,16},{16,24},{24,0},{1,9},{9,17},{17,25},{25,1},{2,10},{10... | collective-permute-start | bytes 147464 | tf_op jit(solution)/shard_map/ppermute | solution.py:51
  124.5 1.1 copy-start.8

commit v2 on v1

--- a/solution.py
+++ b/solution.py
@@ -13,7 +13,7 @@
 CHAIN = 8
 LANES = 128
 GROUP = 8
-TWIN = 2
+TWIN = 4
 
 bead_mass = 5.0
 step_size = 0.02
@@ -27,6 +27,7 @@
 far_own = 3000.0
 far_ghost = 9000.0
 vmem_limit = 48 * 1024 * 1024
+vmem_most = 48 * 1024 * 1024
 NT = (((1,), (1,)), ((), ()))
 NN = (((1,), (0,)), ((), ()))
 exact = lax.Precision.HIGHEST
@@ -34,8 +35,8 @@
 bf16 = jnp.bfloat16
 
 
-def params():
-    return pltpu.CompilerParams(vmem_limit_bytes=vmem_limit)
+def params(limit=vmem_limit):
+    return pltpu.CompilerParams(vmem_limit_bytes=limit)
 
 
 def vmem():
@@ -395,7 +396,8 @@
 def collide_residents(
     cells, first, count, meta_ref, dirs_ref, table_ref, pos_ref, vel_ref, *refs
 ):
-    out_pos, out_vel, held_pos, held_vel, sems = refs[-5:]
+    out_pos, out_vel, token, held_pos, held_vel, sems = refs[-6:]
+    token[...] = jnp.zeros_like(token)
     meta = [meta_ref[k] for k in range(8)]
     table = table_ref[...]
     live_rows = meta[6] - first
@@ -421,7 +423,8 @@
 
 
 def collide_arrivals(cells, first, face_rows, places, meta_ref, dirs_ref, table_ref, *refs):
-    out_pos, out_vel, held_pos, held_vel, sems = refs[-5:]
+    out_pos, out_vel, token, held_pos, held_vel, sems = refs[-6:]
+    token[...] = jnp.zeros_like(token)
     meta = [meta_ref[k] for k in range(8)]
     table = table_ref[...]
     held_pos[...] = jnp.zeros_like(held_pos)
@@ -442,17 +445,44 @@
     copy_out([(held_pos, out_pos.at[:, span, :]), (held_vel, out_vel.at[:, span, :])], sems)
 
 
-def pack_faces(face_rows, pos_ref, vel_ref, rows_ref, *out_refs):
+def pack_inputs(
+    meta_ref,
+    pos_ref,
+    vel_ref,
+    bead_pos_ref,
+    bead_vel_ref,
+    start_ref,
+    block_ref,
+    rows_pos_ref,
+    rows_vel_ref,
+    *refs,
+):
+    out_refs, (held_pos, held_vel, sems) = refs[:6], refs[6:]
+    copies = [(bead_pos_ref, held_pos), (bead_vel_ref, held_vel)]
     for face, out_ref in enumerate(out_refs):
-        for c in range(6):
-            source = pos_ref if c < 3 else vel_ref
-            for k in range(face_rows):
-                out_ref[c * face_rows + k : c * face_rows + k + 1, :] = source[
-                    c % 3, face : face + 1, k * LANES : (k + 1) * LANES
-                ]
-        out_ref[6 * face_rows :, :] = jnp.full((GROUP, LANES), rows_ref[face], jnp.int32).astype(
-            f32
-        )
+        copies.append((pos_ref.at[:, face], out_ref.at[0:3]))
+        copies.append((vel_ref.at[:, face], out_ref.at[3:6]))
+    copies = [pltpu.make_async_copy(a, b, sems.at[k]) for k, (a, b) in enumerate(copies)]
+    for copy in copies:
+        copy.start()
+    for face, out_ref in enumerate(out_refs):
+        out_ref[6] = jnp.full(out_ref.shape[1:], meta_ref[8 + face], jnp.int32).astype(f32)
+    slots = start_ref.shape[1]
+    start_ref[...] = jnp.zeros_like(start_ref)
+    rows_pos_ref[...] = jnp.zeros_like(rows_pos_ref)
+    rows_vel_ref[...] = jnp.zeros_like(rows_vel_ref)
+    for copy in copies:
+        copy.wait()
+    for d in range(3):
+        for k in range(slots // LANES):
+            lanes = slice(k * LANES, (k + 1) * LANES)
+            start_ref[d : d + 1, lanes] = held_pos[d, k : k + 1, :]
+            rows_pos_ref[d, k : k + 1, :] = held_pos[d, k : k + 1, :]
+            rows_vel_ref[d, k : k + 1, :] = held_vel[d, k : k + 1, :]
+    start = start_ref[...]
+    whole = payload(start, slot_live(slots, meta_ref[7], GROUP))
+    for k in range(slots // LANES):
+        block_ref[k * GROUP : (k + 1) * GROUP, :] = whole[:, k * LANES : (k + 1) * LANES]
 
 
 def stack_rows(parts, *refs):
@@ -474,7 +504,21 @@
     return jnp.where(row_ids == 3, flag, jnp.where(row_ids < 3, position, 0.0))
 
 
-def forces(own, chains, bonds_ref, blocks, centre, lengths):
+def thirds_of(value):
+    high = value.astype(bf16)
+    rest = value - high.astype(f32)
+    middle = rest.astype(bf16)
+    low = (rest - middle.astype(f32)).astype(bf16)
+    return jnp.concatenate([high.astype(f32), middle.astype(f32), low.astype(f32)], axis=0).astype(
+        bf16
+    )
+
+
+def summed_thirds(value):
+    return value[:GROUP] + (value[GROUP : 2 * GROUP] + value[2 * GROUP :])
+
+
+def forces(own, chains, counts, bonds_ref, blocks, centre, lengths, mine_ref, packed, push):
     slots = own.shape[1]
     bond_slots = bonds_ref.shape[0]
     row_ids = lax.broadcasted_iota(jnp.int32, (GROUP, slots), 0)
@@ -483,42 +527,80 @@
     for d in range(3):
         mid = jnp.where(row_ids == d, centre[d], mid)
         length = jnp.where(row_ids == d, lengths[d], length)
-    local = jnp.where(row_ids < 3, own - mid, 0.0)
     live = slot_live(slots, chains, GROUP)
-    here = jnp.where(live, local, far_own)
-    mine = [here[d : d + 1] for d in range(3)]
-    total = [jnp.zeros((32, slots), f32) for _ in range(3)]
+    local = jnp.where(live & (row_ids < 3), own - mid, 0.0)
+    columns = jnp.where(live, local, far_own).T
+    for d in range(3):
+        mine_ref[d] = jnp.broadcast_to(columns[:, d : d + 1], (slots, LANES))
+
+    packed[...] = jnp.full(packed.shape, far_ghost, f32)
+    lane = lax.broadcasted_iota(jnp.int32, (GROUP, LANES), 1)
+    tiles = slots // LANES
+    offset = jnp.int32(0)
+    index = 0
     for ref in blocks:
         for b in range(ref.shape[0] // GROUP):
-            block = ref[b * GROUP : (b + 1) * GROUP, :]
-            near = block - mid
-            near = near - length * jnp.floor(near / length + 0.5)
-            near = jnp.where(block[3:4] > 0.5, near, far_ghost)
-            columns = near.T
-
-            for k in range(slots // 32):
-                differ = [mine[d] - columns[k * 32 : (k + 1) * 32, d : d + 1] for d in range(3)]
+            near = ref[b * GROUP : (b + 1) * GROUP, :] - mid
+            near = near - length * jnp.floor(near * (1.0 / length) + 0.5)
+            tile, turn = offset // LANES, offset % LANES
+            turned = [
+                pltpu.roll(near[:, k * LANES : (k + 1) * LANES], turn, axis=1)
+                for k in range(tiles)
+            ]
+            for k in range(tiles + 1):
+                if k == 0:
+                    value = turned[0]
+                elif k == tiles:
+                    value = turned[-1]
+                else:
+                    value = jnp.where(lane < turn, turned[k - 1], turned[k])
+                place = (tile + k) * LANES + lane
+                taken = (place >= offset) & (place < offset + counts[index])
+                packed[tile + k] = jnp.where(taken, value, packed[tile + k])
+            offset = offset + counts[index]
+            index += 1
+
+    push[...] = jnp.zeros_like(push)
+    chunk = 64
+    steps = (offset + 2 * LANES - 1) // (2 * LANES)
+
+    @pl.loop(0, (CHAIN * chains + chunk - 1) // chunk)
+    def _(part):
+        rows = pl.ds(pl.multiple_of(part * chunk, chunk), chunk)
+        mine = [mine_ref[d, rows, :] for d in range(3)]
+
+        def add_tiles(step, total):
+            for k in range(2):
+                other = packed[2 * step + k]
+                differ = [mine[d] - other[d : d + 1] for d in range(3)]
                 square = (
                     differ[0] * differ[0] + differ[1] * differ[1] + differ[2] * differ[2]
                 )
                 inside = (square < cut_square) & (square > 0.25)
-                inverse = 1.0 / jnp.where(inside, square, 1.0)
+                inverse = 1.0 / jnp.where(inside, square, 1e30)
                 sixth = inverse * inverse * inverse
-                weight = jnp.where(
-                    inside, 24.0 * (2.0 * sixth * sixth - sixth) * inverse, 0.0
-                )
-                total = [total[d] + weight * differ[d] for d in range(3)]
+                weight = (sixth * inverse) * (48.0 * sixth - 24.0)
+                total = tuple(total[d] + weight * differ[d] for d in range(3))
+            return total
+
+        total = lax.fori_loop(
+            0, steps, add_tiles, tuple(jnp.zeros((chunk, LANES), f32) for _ in range(3))
+        )
+        for d in range(3):
+            push[d, rows, :] = total[d]
+
     pair = jnp.zeros((GROUP, slots), f32)
     for d in range(3):
-        pair = jnp.where(row_ids == d, jnp.sum(total[d], axis=0, keepdims=True), pair)
+        pair = jnp.where(row_ids == d, jnp.sum(push[d].T, axis=0, keepdims=True), pair)
+
     slot_ids = lax.broadcasted_iota(jnp.int32, (bond_slots, slots), 1)
     bond_ids = lax.broadcasted_iota(jnp.int32, (bond_slots, slots), 0)
     ends = bonds_ref[...]
     first = jnp.where(slot_ids == ends[:, 0:1], 1.0, 0.0)
     second = jnp.where(slot_ids == ends[:, 1:2], 1.0, 0.0)
-    joins = jnp.where(bond_ids < (CHAIN - 1) * chains, first - second, 0.0)
-    stretch = lax.dot_general(
-        jnp.where(live, local, 0.0), joins, NT, precision=exact, preferred_element_type=f32
+    joins = jnp.where(bond_ids < (CHAIN - 1) * chains, first - second, 0.0).astype(bf16)
+    stretch = summed_thirds(
+        lax.dot_general(thirds_of(local), joins, NT, preferred_element_type=f32)
     )
     square = (
         stretch[0:1] * stretch[0:1] + stretch[1:2] * stretch[1:2] + stretch[2:3] * stretch[2:3]
@@ -527,22 +609,47 @@
         lax.broadcasted_iota(jnp.int32, (1, bond_slots), 1) < (CHAIN - 1) * chains
     )
     pull = jnp.where(bond_live, -spring / (1.0 - square / reach_square), 0.0) * stretch
-    return pair + lax.dot_general(pull, joins, NN, precision=exact, preferred_element_type=f32)
+    return pair + summed_thirds(
+        lax.dot_general(thirds_of(pull), joins, NN, preferred_element_type=f32)
+    )
+
+
+def force_scratch(slots, blocks):
+    tiles = -(-(blocks * slots // LANES + 2) // 2) * 2
+    return [
+        pltpu.VMEM((3, slots, LANES), f32),
+        pltpu.VMEM((tiles, GROUP, LANES), f32),
+        pltpu.VMEM((3, slots, LANES), f32),
+    ]
 
 
 def centre_of(meta, sizes):
     return [meta[3 + d].astype(f32) + 0.5 * sizes[d] for d in range(3)]
 
 
-def first_forces(sizes, lengths, meta_ref, start_ref, bonds_ref, a_ref, b_ref, c_ref, push_ref):
+def first_forces(sizes, lengths, sources, meta_ref, start_ref, bonds_ref, *refs):
+    blocks, (push_ref, counts_ref), scratch = (
+        refs[:sources],
+        refs[sources : sources + 2],
+        refs[sources + 2 :],
+    )
     meta = [meta_ref[k] for k in range(8)]
+    counts = []
+    for ref in blocks:
+        for b in range(ref.shape[0] // GROUP):
+            live = ref[b * GROUP + 3 : b * GROUP + 4, :]
+            counts.append(jnp.sum(live).astype(jnp.int32))
+    for k, count in enumerate(counts):
+        counts_ref[k] = count
     push_ref[...] = forces(
         start_ref[...],
         meta[7],
+        counts,
         bonds_ref,
-        [a_ref, b_ref, c_ref],
+        blocks,
         centre_of(meta, sizes),
         lengths,
+        *scratch,
     )
 
 
@@ -590,39 +697,37 @@
 
 
 def substep(
-    sizes,
-    lengths,
-    last,
-    meta_ref,
-    start_ref,
-    bonds_ref,
-    speed_ref,
-    moved_ref,
-    a_ref,
-    b_ref,
-    c_ref,
-    order_ref,
-    speed_out,
-    moved_out,
-    *pay_refs,
+    sizes, lengths, last, sources, meta_ref, start_ref, bonds_ref, counts_ref, speed_ref, moved_ref, *refs
 ):
+    blocks, outs, scratch = refs[:sources], refs[sources + 1 : -3], refs[-3:]
     meta = [meta_ref[k] for k in range(8)]
+    counts = [
+        counts_ref[k] for k in range(sum(ref.shape[0] // GROUP for ref in blocks))
+    ]
     start = start_ref[...]
     moved = moved_ref[...]
     push = forces(
-        start + moved, meta[7], bonds_ref, [a_ref, b_ref, c_ref], centre_of(meta, sizes), lengths
+        start + moved,
+        meta[7],
+        counts,
+        bonds_ref,
+        blocks,
+        centre_of(meta, sizes),
+        lengths,
+        *scratch,
     )
     live = slot_live(start.shape[1], meta[7], GROUP)
     speed = speed_ref[...] + half_kick * push
     if last:
-        speed_out[...] = jnp.where(live, speed, 0.0)[:3]
-        moved_out[...] = jnp.where(live, moved, 0.0)[:3]
+        for d in range(3):
+            outs[0][d, 0, 0, :, :] = jnp.where(live, speed, 0.0)[d : d + 1]
+            outs[1][d, 0, 0, :, :] = jnp.where(live, moved, 0.0)[d : d + 1]
         return
     speed = speed + half_kick * push
     moved = moved + step_size * speed
-    speed_out[...] = speed
-    moved_out[...] = moved
-    pay_refs[0][...] = payload(start + moved, live)
+    outs[0][...] = speed
+    outs[1][...] = moved
+    outs[2][...] = payload(start + moved, live)
 
 
 def neighbours(value, axis):
@@ -655,7 +760,7 @@
     parts = [row] + neighbours(row, "gy")
     plane = stacked(whole_rows(parts), parts, [pieces[1]()])
     sides = neighbours(plane, "gx")
-    return [plane] + sides + sides[: 2 - len(sides)], pieces[2]()
+    return [plane] + sides, pieces[2]()
 
 
 def like(*shape, dtype=f32):
@@ -689,39 +794,42 @@
     rows_all = rows_here + 6 * face_rows
     anchor = jnp.stack([lax.axis_index(names[d]) * sizes[d] for d in range(3)])
     meta = jnp.concatenate(
-        [shift, anchor.astype(jnp.int32), sol_rows.reshape(1), bead_chains.reshape(1)]
+        [
+            shift,
+            anchor.astype(jnp.int32),
+            sol_rows.reshape(1),
+            bead_chains.reshape(1),
+            mig_rows.reshape(6),
+        ]
     )
     dirs = direction_table()
     position = sol_pos.reshape(3, rows_here, LANES)
     velocity = sol_vel.reshape(3, rows_here, LANES)
 
     any_spec = pl.BlockSpec(memory_space=pl.ANY)
-    face_height = 6 * face_rows + GROUP
-    packed = pl.pallas_call(
-        functools.partial(pack_faces, face_rows),
-        out_shape=[like(face_height, LANES)] * 6,
-        in_specs=[vmem(), vmem(), smem()],
-        out_specs=[vmem()] * 6,
-        compiler_params=params(),
-        name="pack_faces",
+    face_height = 7 * face_rows
+    bead_shape = like(GROUP, bead_slots)
+    tiles = bead_slots // LANES
+    rows_shape = like(3, GROUP, LANES)
+    start, block, bead_rows_pos, bead_rows_vel, *packed = pl.pallas_call(
+        pack_inputs,
+        out_shape=[bead_shape, like(tiles * GROUP, LANES), rows_shape, rows_shape]
+        + [like(7, face_rows, LANES)] * 6,
+        in_specs=[smem()] + [pl.BlockSpec(memory_space=pltpu.HBM)] * 4,
+        out_specs=[vmem()] * 10,
+        scratch_shapes=[pltpu.VMEM((3, tiles, LANES), f32)] * 2
+        + [pltpu.SemaphoreType.DMA((14,))],
+        compiler_params=params(vmem_most),
+        name="pack_inputs",
     )(
-        mig_pos.reshape(3, 6, buffer_slots),
-        mig_vel.reshape(3, 6, buffer_slots),
-        mig_rows.reshape(6),
-    )
-
-    bead_flat = bead_pos.reshape(3, bead_slots)
-    start = jnp.pad(bead_flat, ((0, GROUP - 3), (0, 0)))
-    tiles = bead_slots // LANES
-    bead_pad = ((0, 0), (0, GROUP - tiles), (0, 0))
-    bead_rows_pos = jnp.pad(bead_pos.reshape(3, tiles, LANES), bead_pad)
-    bead_rows_vel = jnp.pad(bead_vel.reshape(3, tiles, LANES), bead_pad)
+        meta,
+        mig_pos.reshape(3, 6, face_rows, LANES),
+        mig_vel.reshape(3, 6, face_rows, LANES),
+        bead_pos.reshape(3, tiles, LANES),
+        bead_vel.reshape(3, tiles, LANES),
+    )
+    packed = [value.reshape(face_height, LANES) for value in packed]
     bonds = bond_list.reshape(2, bond_slots).T
-    bead_live = jnp.arange(bead_slots, dtype=jnp.int32) < CHAIN * bead_chains.reshape(())
-    first_pay = jnp.concatenate(
-        [bead_flat, bead_live.astype(f32)[None], jnp.zeros((GROUP - 4, bead_slots), f32)], axis=0
-    )
-    block = first_pay.reshape(GROUP, tiles, LANES).transpose(1, 0, 2).reshape(-1, LANES)
 
     thirds = 3
     count = rows_here // thirds
@@ -765,7 +873,6 @@
             around = [blocks] + [
                 stacked([(0, at, height)], [came[w]]) for w, at in bodies
             ]
-            around = around + around[1 : 1 + 3 - len(around)]
 
     def as_blocks(value):
         n = value.shape[0] // (GROUP * tiles)
@@ -792,14 +899,17 @@
         name="bin_arrivals",
     )(meta, *arriving, bead_rows_pos, bead_rows_vel, axis_rows, totals)
 
-    push = pl.pallas_call(
-        functools.partial(first_forces, sizes, lengths),
-        out_shape=like(GROUP, bead_slots),
-        in_specs=[smem()] + [vmem()] * 5,
-        out_specs=vmem(),
+    around = [as_blocks(value) for value in around]
+    many = sum(value.shape[0] // GROUP for value in around)
+    push, counts = pl.pallas_call(
+        functools.partial(first_forces, sizes, lengths, len(around)),
+        out_shape=[bead_shape, like(many, dtype=jnp.int32)],
+        in_specs=[smem()] + [vmem()] * (2 + len(around)),
+        out_specs=[vmem(), smem()],
+        scratch_shapes=force_scratch(bead_slots, many),
         compiler_params=params(),
         name="first_forces",
-    )(meta, start, bonds, *[as_blocks(value) for value in around])
+    )(meta, start, bonds, *around)
 
     below, above = moved_along(high, "gx", 1), moved_along(low, "gx", -1)
     totals, low, high = pl.pallas_call(
@@ -823,7 +933,6 @@
     sides = neighbours(faces, "gz")
     below, above = sides[0], sides[-1]
 
-    bead_shape = like(GROUP, bead_slots)
     table, speed, moved, pay = pl.pallas_call(
         functools.partial(finish_cells, cells),
         out_shape=[
@@ -848,7 +957,7 @@
     span = rows_here // cuts
 
     def collide_piece(piece):
-        earlier = list(results)
+        earlier = results[:2]
         if piece < cuts:
             body = functools.partial(collide_residents, cells, piece * span, span)
             rows = span
@@ -869,30 +978,34 @@
         at = 3 + len(sources)
         results[:] = pl.pallas_call(
             body,
-            out_shape=[solvent_shape] * 2,
+            out_shape=[solvent_shape, solvent_shape, like(GROUP, LANES)],
             grid=(1,),
             in_specs=[smem(), vmem(), vmem()] + specs + [any_spec] * len(earlier),
-            out_specs=[any_spec] * 2,
+            out_specs=[any_spec, any_spec, vmem()],
             scratch_shapes=[pltpu.VMEM((3, rows, LANES), f32)] * 2
             + [pltpu.SemaphoreType.DMA((2,))],
             input_output_aliases={at: 0, at + 1: 1} if earlier else {},
             compiler_params=params(),
             name=f"collide_{piece}",
         )(meta, dirs, table, *sources, *earlier)
-        return results[1]
+        return results[2]
 
     for step in range(3):
         last = step == 2
         thunks = [functools.partial(collide_piece, 3 * step + k) for k in range(3)]
         ghosts, order = halo(pay, thunks)
+        final = like(3, 1, 1, 1, bead_slots)
         outcome = pl.pallas_call(
-            functools.partial(substep, sizes, lengths, last),
-            out_shape=[like(3, bead_slots)] * 2 if last else [bead_shape] * 3,
-            in_specs=[smem()] + [vmem()] * 7 + [any_spec],
+            functools.partial(substep, sizes, lengths, last, len(ghosts)),
+            out_shape=[final] * 2 if last else [bead_shape] * 3,
+            in_specs=[smem(), vmem(), vmem(), smem()]
+            + [vmem()] * (2 + len(ghosts))
+            + [any_spec],
             out_specs=[vmem()] * (2 if last else 3),
+            scratch_shapes=force_scratch(bead_slots, many),
             compiler_params=params(),
             name=f"substep_{step}",
-        )(meta, start, bonds, speed, moved, *ghosts, order)
+        )(meta, start, bonds, counts, speed, moved, *ghosts, order)
         speed, moved = outcome[:2]
         pay = outcome[-1]
 
@@ -900,8 +1013,8 @@
     return (
         results[0].reshape(3, 1, 1, 1, count_solvent),
         results[1].reshape(3, 1, 1, 1, count_solvent),
-        moved.reshape(3, 1, 1, 1, bead_slots),
-        speed.reshape(3, 1, 1, 1, bead_slots),
+        moved,
+        speed,
     )
 
 

time: 133 us -> 112 us (0.84)
  waiting for transfers between devices: 16.2 us -> 5.76 us
  Pallas kernels: 69.8 us -> 60.2 us
  local copies, waits for them, and re-layouts: 14.9 us -> 5.87 us
  starting transfers between devices: 28.9 us -> 35.9 us
    pallas_call x14, Pallas kernels: 50.4 us -> 39.5 us  [the longest x9 27.8 us: collide_piece(): pl.pallas_call(body, out_shape=[solvent_shape, solvent_shape, like(GROUP,...]
    ppermute x25, waiting for transfers between devices: 16.2 us -> 5.76 us  [moved_along(): lax.ppermute(value, axis, [(i, (i + by) % peers) for i in range(peers)])]
    unnamed x39 -> x19, local copies, waits for them, and re-layouts: 14.8 us -> 5.12 us
    ppermute x25, starting transfers between devices: 28.9 us -> 35.9 us  [moved_along(): lax.ppermute(value, axis, [(i, (i + by) % peers) for i in range(peers)])]
  transfers between devices with their start and end apart: 25 -> 25, of which waited for: 10 -> 6; matrix products, arithmetic and copies ran while one was open for 0% -> 0% of each run, Pallas kernels for 33% -> 39%
where the time goes in v2:
time: 112 us; the launch traced here: 110 us
  Pallas kernels  60.2 us (54%)
  starting transfers between devices  35.9 us (32%)
  local copies, waits for them, and re-layouts  5.87 us (5%)
  waiting for transfers between devices  5.76 us (5%)
  between operations  2.47 us (2%)
    ppermute x25, starting transfers between devices, moved_along(): lax.ppermute(value, axis, [(i, (i + by) % peers) for i in range(peers)])  35.9 us
    pallas_call x9, Pallas kernels, collide_piece(): pl.pallas_call(body, out_shape=[solvent_shape, solvent_shape, like(GROUP,...  27.8 us
    pallas_call x3, Pallas kernels, bin_piece(): pl.pallas_call(functools.partial(bin_residents, cells, piece * count, cou...  12.1 us
    pallas_call x3, Pallas kernels, shards(): pl.pallas_call(functools.partial(substep, sizes, lengths, last, len(ghost...  8.14 us
    pallas_call x1, Pallas kernels, shards(): pl.pallas_call(functools.partial(bin_arrivals, cells, face_rows, tuple(sp...  7.32 us
    ppermute x25, waiting for transfers between devices, moved_along(): lax.ppermute(value, axis, [(i, (i + by) % peers) for i in range(peers)])  5.76 us
    unnamed x19, local copies, waits for them, and re-layouts  5.12 us
    pallas_call x1, Pallas kernels, shards(): pl.pallas_call(functools.partial(first_forces, sizes, lengths, len(around...  2.67 us
  transfers between devices with their start and end apart: 25, of which 6 were waited for; matrix products, arithmetic and copies ran while one was open for 0% of the time, Pallas kernels for 39%

profile of v2, /device:TPU:0, one launch (start us, length us, event | category | flops | bytes accessed | tf_op | source)
XLA Modules:
  0.0 110.3 jit_solution(13271016055723815845)
XLA Ops:
  2.0 0.8 concatenate.3.meta_ref
  2.8 0.9 copy-done.3
  3.7 0.9 copy-done.4
  4.6 0.7 copy-done.6
  5.3 0.7 copy-done.7
  6.0 0.9 pack_inputs.1
  6.9 3.0 %collective-permute-start = (f32[352,128]{1,0:T(8,128)S(1)}, f32[352,128]{1,0:T(8,128)S(1)}, u32[]{:S(2)}, u32[]{:S(2)}) collective-permute-start(f32[352,128]{1,0:T(8,128)S(1)} %stack_rows.15), channel_id=1, source_target_pairs={{0,1},{1,0},{2,3},{3,2},{4,5},{5,4},{6,7},{7,6},{8,9},{9,8},{10,11... | collective-permute-start | bytes 540680 | tf_op jit(solution)/shard_map/ppermute | solution.py:52
  9.9 1.1 copy-done.1
  11.0 4.0 %bin_residents_0.1.refs_2_.refs_0_ = f32[304,256]{1,0:T(8,128)S(1)} custom-call(s32[14]{0:T(128)S(1)} %concatenate.3.meta_ref, f32[3,384,128]{2,1,0:T(8,128)S(1)} %bitcast.41, f32[3,384,128]{2,1,0:T(8,128)S(1)} %bitcast.50, f32[16,128]{1,0:T(8,128)S(1)} %get-tuple-element.64.refs_2_.refs_0_), custom_call_target="tpu_custom_call" | custom-call | tf_op jit(solution)/shard_map/bin_residents_0/pallas_call | solution.py:839
  15.0 0.0 copy-start.2
  15.0 0.0 collective-permute-done.refs_1_.refs_4_
  15.1 0.1 collective-permute-start.1
  15.2 1.8 %collective-permute-start.2 = (f32[200,128]{1,0:T(8,128)S(1)}, f32[200,128]{1,0:T(8,128)S(1)}, u32[]{:S(2)}, u32[]{:S(2)}) collective-permute-start(f32[200,128]{1,0:T(8,128)S(1)} %stack_rows.18), channel_id=1, source_target_pairs={{0,6},{2,0},{4,2},{6,4},{1,7},{3,1},{5,3},{7,5},{8,14},{10,8},{12,... | collective-permute-start | bytes 307208 | tf_op jit(solution)/shard_map/ppermute | solution.py:52
  16.9 4.0 %bin_residents_1.1.refs_3_.refs_0_ = f32[304,256]{1,0:T(8,128)S(1)} custom-call(s32[14]{0:T(128)S(1)} %concatenate.3.meta_ref, f32[3,384,128]{2,1,0:T(8,128)S(1)} %bitcast.42, f32[3,384,128]{2,1,0:T(8,128)S(1)} %bitcast.51, f32[304,256]{1,0:T(8,128)S(1)} %bin_residents_0.1.refs_2_.refs_0_, f32[32,128]{1,0:T(8,128)S(1)} %stack_rows.16.refs_1_.refs_0_), custom_call_target="tpu_custom_call" | custom-call | tf_op jit(solution)/shard_map/bin_residents_1/pallas_call | solution.py:839
  21.0 0.0 collective-permute-done.1.refs_1_.refs_2_
  21.0 1.6 %collective-permute-start.3 = (f32[264,128]{1,0:T(8,128)S(1)}, f32[264,128]{1,0:T(8,128)S(1)}, u32[]{:S(2)}, u32[]{:S(2)}) collective-permute-start(f32[264,128]{1,0:T(8,128)S(1)} %stack_rows.20), channel_id=1, source_target_pairs={{0,8},{8,16},{16,24},{24,0},{1,9},{9,17},{17,25},{25,1},{2,10},{10... | collective-permute-start | bytes 405512 | tf_op jit(solution)/shard_map/ppermute | solution.py:52
  22.7 0.0 copy-start.5
  22.7 2.3 %collective-permute-start.4 = (f32[264,128]{1,0:T(8,128)S(1)}, f32[264,128]{1,0:T(8,128)S(1)}, u32[]{:S(2)}, u32[]{:S(2)}) collective-permute-start(f32[264,128]{1,0:T(8,128)S(1)} %stack_rows.21), channel_id=1, source_target_pairs={{0,24},{8,0},{16,8},{24,16},{1,25},{9,1},{17,9},{25,17},{2,26},{10... | collective-permute-start | bytes 405512 | tf_op jit(solution)/shard_map/ppermute | solution.py:52
  25.0 4.0 %bin_residents_2.1.refs_8_ = f32[304,256]{1,0:T(8,128)S(1)} custom-call(s32[14]{0:T(128)S(1)} %concatenate.3.meta_ref, f32[3,384,128]{2,1,0:T(8,128)S(1)} %bitcast.43, f32[3,384,128]{2,1,0:T(8,128)S(1)} %bitcast.52, f32[304,256]{1,0:T(8,128)S(1)} %bin_residents_1.1.refs_3_.refs_0_, f32[96,128]{1,0:T(8,128)S(1)} %stack_rows.19.refs_1_), custom_call_target="tpu_custom_call" | custom-call | tf_op jit(solution)/shard_map/bin_residents_2/pallas_call | solution.py:839
  29.0 0.3 collective-permute-done.3.refs_0_
  29.3 1.4 %collective-permute-done.4.refs_1_.refs_0_ = f32[264,128]{1,0:T(8,128)S(1)} collective-permute-done((f32[264,128]{1,0:T(8,128)S(1)}, f32[264,128]{1,0:T(8,128)S(1)}, u32[]{:S(2)}, u32[]{:S(2)}) %collective-permute-start.4) | collective-permute-done | bytes 135200 | tf_op jit(solution)/shard_map/ppermute | solution.py:52
  30.8 7.3 %bin_arrivals.1 = (f32[2,304,128]{2,1,0:T(8,128)S(1)}, f32[2,24,128]{2,1,0:T(8,128)S(1)}, f32[2,24,128]{2,1,0:T(8,128)S(1)}) custom-call(s32[14]{0:T(128)S(1)} %concatenate.3.meta_ref, f32[264,128]{1,0:T(8,128)S(1)} %collective-permute-done.3.refs_0_, f32[264,128]{1,0:T(8,128)S(1)} %collective-permute-done.4.refs_1_.refs_0_, ...), custom_call_target="tpu_custom_call" | custom-call | tf_op jit(solution)/shard_map/bin_arrivals/pallas_call | solution.py:892
  38.1 0.1 collective-permute-start.5
  38.2 3.8 %collective-permute-start.6 = (f32[2,24,128]{2,1,0:T(8,128)S(1)}, f32[2,24,128]{2,1,0:T(8,128)S(1)}, u32[]{:S(2)}, u32[]{:S(2)}) collective-permute-start(f32[2,24,128]{2,1,0:T(8,128)S(1)} %get-tuple-element.74), channel_id=1, source_target_pairs={{0,24},{8,0},{16,8},{24,16},{1,25},{9,1},{17,9},{25,17},{2,26},{10... | collective-permute-start | bytes 73736 | tf_op jit(solution)/shard_map/ppermute | solution.py:52
  42.0 1.8 %collective-permute-done.5.below_ref = f32[2,24,128]{2,1,0:T(8,128)S(1)} collective-permute-done((f32[2,24,128]{2,1,0:T(8,128)S(1)}, f32[2,24,128]{2,1,0:T(8,128)S(1)}, u32[]{:S(2)}, u32[]{:S(2)}) %collective-permute-start.5) | collective-permute-done | bytes 24608 | tf_op jit(solution)/shard_map/ppermute | solution.py:52
  43.8 0.1 collective-permute-start.7
  43.9 1.7 %collective-permute-start.8 = (f32[2,24,128]{2,1,0:T(8,128)S(1)}, f32[2,24,128]{2,1,0:T(8,128)S(1)}, u32[]{:S(2)}, u32[]{:S(2)}) collective-permute-start(f32[2,24,128]{2,1,0:T(8,128)S(1)} %get-tuple-element.77), channel_id=1, source_target_pairs={{0,6},{2,0},{4,2},{6,4},{1,7},{3,1},{5,3},{7,5},{8,14},{10,8},{12,... | collective-permute-start | bytes 73736 | tf_op jit(solution)/shard_map/ppermute | solution.py:52
  45.7 1.5 %collective-permute-done.7.below_ref = f32[2,24,128]{2,1,0:T(8,128)S(1)} collective-permute-done((f32[2,24,128]{2,1,0:T(8,128)S(1)}, f32[2,24,128]{2,1,0:T(8,128)S(1)}, u32[]{:S(2)}, u32[]{:S(2)}) %collective-permute-start.7) | collective-permute-done | bytes 24608 | tf_op jit(solution)/shard_map/ppermute | solution.py:52
  47.1 0.0 collective-permute-done.8.above_ref
  47.1 0.2 add_faces_y.1
  47.3 1.6 %collective-permute-start.9 = (f32[16,304]{1,0:T(8,128)S(1)}, f32[16,304]{1,0:T(8,128)S(1)}, u32[]{:S(2)}, u32[]{:S(2)}) collective-permute-start(f32[16,304]{1,0:T(8,128)S(1)} %get-tuple-element.79), channel_id=1, source_target_pairs={{0,1},{1,0},{2,3},{3,2},{4,5},{5,4},{6,7},{7,6},{8,9},{9,8},{10,11... | collective-permute-start | bytes 58376 | tf_op jit(solution)/shard_map/ppermute | solution.py:52
  48.9 0.7 copy-done.8
  49.6 0.1 copy.35
  49.8 2.7 %first_forces.1 = (f32[8,256]{1,0:T(8,128)S(1)}, s32[18]{0:T(128)S(1)}) custom-call(s32[14]{0:T(128)S(1)} %concatenate.3.meta_ref, f32[8,256]{1,0:T(8,128)S(1)} %get-tuple-element.80.start_ref, s32[224,2]{1,0:T(8,128)S(1)} %bitcast.59, f32[48,256]{1,0:T(8,128)S(1)} %bitcast.63, f32[48,256]{1,0:T(8,128)S(1)} %bitcast.66, f32[48,256]{1,0:T(8,128)S(1)} %bitcast.67), custom_call_target="tpu_custom_call" | custom-call | tf_op jit(solution)/shard_map/first_forces/pallas_call | solution.py:904
  52.4 0.0 collective-permute-done.9.below_ref.above_ref
  52.5 1.0 finish_cells.1
  53.4 0.3 collective-permute-start.10
  53.8 3.0 %collide_0.1 = (f32[3,528,128]{2,1,0:T(8,128)}, f32[3,528,128]{2,1,0:T(8,128)}, f32[8,128]{1,0:T(8,128)S(1)}) custom-call(s32[14]{0:T(128)S(1)} %concatenate.3.meta_ref, f32[2,8,128]{2,1,0:T(8,128)S(1)} %broadcast_in_dim.2.dirs_ref, bf16[280,256]{1,0:T(8,128)(2,1)S(1)} %get-tuple-element.82.table_ref, f32[3,384,128]{2,1,0:T(8,128)S(1)} %bitcast.44, ...), custom_call_target="tpu_custom_call" | custom-call | tf_op jit(solution)/shard_map/collide_0/pallas_call | solution.py:979
  56.8 0.4 collective-permute-done.10.refs_1_
  57.2 1.7 %collective-permute-start.12 = (f32[16,256]{1,0:T(8,128)S(1)}, f32[16,256]{1,0:T(8,128)S(1)}, u32[]{:S(2)}, u32[]{:S(2)}) collective-permute-start(f32[16,256]{1,0:T(8,128)S(1)} %stack_rows.24.refs_0_), channel_id=1, source_target_pairs={{0,6},{2,0},{4,2},{6,4},{1,7},{3,1},{5,3},{7,5},{8,14},{10,8},{12,... | collective-permute-start | bytes 49160 | tf_op jit(solution)/shard_map/ppermute | solution.py:52
  58.9 3.0 %collide_1.1 = (f32[3,528,128]{2,1,0:T(8,128)}, f32[3,528,128]{2,1,0:T(8,128)}, f32[8,128]{1,0:T(8,128)S(1)}) custom-call(s32[14]{0:T(128)S(1)} %concatenate.3.meta_ref, f32[2,8,128]{2,1,0:T(8,128)S(1)} %broadcast_in_dim.2.dirs_ref, bf16[280,256]{1,0:T(8,128)(2,1)S(1)} %get-tuple-element.82.table_ref, ...), custom_call_target="tpu_custom_call", output_to_operand_aliasing={{0}: (5, {}), {1}: (6, {})} | custom-call | tf_op jit(solution)/shard_map/collide_1/pallas_call | solution.py:979
  61.9 0.9 collective-permute-start.13
  62.8 3.5 %collective-permute-start.14 = (f32[48,256]{1,0:T(8,128)S(1)}, f32[48,256]{1,0:T(8,128)S(1)}, u32[]{:S(2)}, u32[]{:S(2)}) collective-permute-start(f32[48,256]{1,0:T(8,128)S(1)} %stack_rows.25.refs_0_), channel_id=1, source_target_pairs={{0,24},{8,0},{16,8},{24,16},{1,25},{9,1},{17,9},{25,17},{2,26},{10... | collective-permute-start | bytes 147464 | tf_op jit(solution)/shard_map/ppermute | solution.py:52
  66.3 3.0 %collide_2.1 = (f32[3,528,128]{2,1,0:T(8,128)}, f32[3,528,128]{2,1,0:T(8,128)}, f32[8,128]{1,0:T(8,128)S(1)}) custom-call(s32[14]{0:T(128)S(1)} %concatenate.3.meta_ref, f32[2,8,128]{2,1,0:T(8,128)S(1)} %broadcast_in_dim.2.dirs_ref, bf16[280,256]{1,0:T(8,128)(2,1)S(1)} %get-tuple-element.82.table_ref, ...), custom_call_target="tpu_custom_call", output_to_operand_aliasing={{0}: (5, {}), {1}: (6, {})} | custom-call | tf_op jit(solution)/shard_map/collide_2/pallas_call | solution.py:979
  69.3 2.5 %substep_0.1 = (f32[8,256]{1,0:T(8,128)S(1)}, f32[8,256]{1,0:T(8,128)S(1)}, f32[8,256]{1,0:T(8,128)S(1)}) custom-call(s32[14]{0:T(128)S(1)} %concatenate.3.meta_ref, f32[8,256]{1,0:T(8,128)S(1)} %get-tuple-element.80.start_ref, s32[224,2]{1,0:T(8,128)S(1)} %bitcast.60, s32[18]{0:T(128)S(1)} %get-tuple-element.101.counts_ref, ...), custom_call_target="tpu_custom_call" | custom-call | tf_op jit(solution)/shard_map/substep_0/pallas_call | solution.py:998
  71.8 0.4 collective-permute-start.15
  72.3 3.0 %collide_3.1 = (f32[3,528,128]{2,1,0:T(8,128)}, f32[3,528,128]{2,1,0:T(8,128)}, f32[8,128]{1,0:T(8,128)S(1)}) custom-call(s32[14]{0:T(128)S(1)} %concatenate.3.meta_ref, f32[2,8,128]{2,1,0:T(8,128)S(1)} %broadcast_in_dim.2.dirs_ref, bf16[280,256]{1,0:T(8,128)(2,1)S(1)} %get-tuple-element.82.table_ref, ...), custom_call_target="tpu_custom_call", output_to_operand_aliasing={{0}: (5, {}), {1}: (6, {})} | custom-call | tf_op jit(solution)/shard_map/collide_3/pallas_call | solution.py:979
  75.3 0.3 collective-permute-done.15.refs_1_
  75.6 0.0 collective-permute-start.16
  75.6 1.7 %collective-permute-start.17 = (f32[16,256]{1,0:T(8,128)S(1)}, f32[16,256]{1,0:T(8,128)S(1)}, u32[]{:S(2)}, u32[]{:S(2)}) collective-permute-start(f32[16,256]{1,0:T(8,128)S(1)} %stack_rows.26.refs_0_), channel_id=1, source_target_pairs={{0,6},{2,0},{4,2},{6,4},{1,7},{3,1},{5,3},{7,5},{8,14},{10,8},{12,... | collective-permute-start | bytes 49160 | tf_op jit(solution)/shard_map/ppermute | solution.py:52
  77.3 3.0 %collide_4.1 = (f32[3,528,128]{2,1,0:T(8,128)}, f32[3,528,128]{2,1,0:T(8,128)}, f32[8,128]{1,0:T(8,128)S(1)}) custom-call(s32[14]{0:T(128)S(1)} %concatenate.3.meta_ref, f32[2,8,128]{2,1,0:T(8,128)S(1)} %broadcast_in_dim.2.dirs_ref, bf16[280,256]{1,0:T(8,128)(2,1)S(1)} %get-tuple-element.82.table_ref, ...), custom_call_target="tpu_custom_call", output_to_operand_aliasing={{0}: (5, {}), {1}: (6, {})} | custom-call | tf_op jit(solution)/shard_map/collide_4/pallas_call | solution.py:979
  80.3 1.1 %collective-permute-start.18 = (f32[48,256]{1,0:T(8,128)S(1)}, f32[48,256]{1,0:T(8,128)S(1)}, u32[]{:S(2)}, u32[]{:S(2)}) collective-permute-start(f32[48,256]{1,0:T(8,128)S(1)} %stack_rows.27.refs_0_), channel_id=1, source_target_pairs={{0,8},{8,16},{16,24},{24,0},{1,9},{9,17},{17,25},{25,1},{2,10},{10... | collective-permute-start | bytes 147464 | tf_op jit(solution)/shard_map/ppermute | solution.py:52
  81.5 2.9 %collective-permute-start.19 = (f32[48,256]{1,0:T(8,128)S(1)}, f32[48,256]{1,0:T(8,128)S(1)}, u32[]{:S(2)}, u32[]{:S(2)}) collective-permute-start(f32[48,256]{1,0:T(8,128)S(1)} %stack_rows.27.refs_0_), channel_id=1, source_target_pairs={{0,24},{8,0},{16,8},{24,16},{1,25},{9,1},{17,9},{25,17},{2,26},{10... | collective-permute-start | bytes 147464 | tf_op jit(solution)/shard_map/ppermute | solution.py:52
  84.4 3.0 %collide_5.1 = (f32[3,528,128]{2,1,0:T(8,128)}, f32[3,528,128]{2,1,0:T(8,128)}, f32[8,128]{1,0:T(8,128)S(1)}) custom-call(s32[14]{0:T(128)S(1)} %concatenate.3.meta_ref, f32[2,8,128]{2,1,0:T(8,128)S(1)} %broadcast_in_dim.2.dirs_ref, bf16[280,256]{1,0:T(8,128)(2,1)S(1)} %get-tuple-element.82.table_ref, ...), custom_call_target="tpu_custom_call", output_to_operand_aliasing={{0}: (5, {}), {1}: (6, {})} | custom-call | tf_op jit(solution)/shard_map/collide_5/pallas_call | solution.py:979
  87.4 2.5 %substep_1.1 = (f32[8,256]{1,0:T(8,128)S(1)}, f32[8,256]{1,0:T(8,128)S(1)}, f32[8,256]{1,0:T(8,128)S(1)}) custom-call(s32[14]{0:T(128)S(1)} %concatenate.3.meta_ref, f32[8,256]{1,0:T(8,128)S(1)} %get-tuple-element.80.start_ref, s32[224,2]{1,0:T(8,128)S(1)} %bitcast.61, s32[18]{0:T(128)S(1)} %get-tuple-element.101.counts_ref, ...), custom_call_target="tpu_custom_call" | custom-call | tf_op jit(solution)/shard_map/substep_1/pallas_call | solution.py:998
  89.9 0.1 collective-permute-start.20
  90.0 3.7 %collide_6.1 = (f32[3,528,128]{2,1,0:T(8,128)}, f32[3,528,128]{2,1,0:T(8,128)}, f32[8,128]{1,0:T(8,128)S(1)}) custom-call(s32[14]{0:T(128)S(1)} %concatenate.3.meta_ref, f32[2,8,128]{2,1,0:T(8,128)S(1)} %broadcast_in_dim.2.dirs_ref, bf16[280,256]{1,0:T(8,128)(2,1)S(1)} %get-tuple-element.82.table_ref, ...), custom_call_target="tpu_custom_call", output_to_operand_aliasing={{0}: (8, {}), {1}: (9, {})} | custom-call | tf_op jit(solution)/shard_map/collide_6/pallas_call | solution.py:979
  93.7 0.1 collective-permute-start.21
  93.8 1.7 %collective-permute-start.22 = (f32[16,256]{1,0:T(8,128)S(1)}, f32[16,256]{1,0:T(8,128)S(1)}, u32[]{:S(2)}, u32[]{:S(2)}) collective-permute-start(f32[16,256]{1,0:T(8,128)S(1)} %stack_rows.28.refs_0_), channel_id=1, source_target_pairs={{0,6},{2,0},{4,2},{6,4},{1,7},{3,1},{5,3},{7,5},{8,14},{10,8},{12,... | collective-permute-start | bytes 49160 | tf_op jit(solution)/shard_map/ppermute | solution.py:52
  95.5 3.3 %collide_7.1 = (f32[3,528,128]{2,1,0:T(8,128)}, f32[3,528,128]{2,1,0:T(8,128)}, f32[8,128]{1,0:T(8,128)S(1)}) custom-call(s32[14]{0:T(128)S(1)} %concatenate.3.meta_ref, f32[2,8,128]{2,1,0:T(8,128)S(1)} %broadcast_in_dim.2.dirs_ref, bf16[280,256]{1,0:T(8,128)(2,1)S(1)} %get-tuple-element.82.table_ref, ...), custom_call_target="tpu_custom_call", output_to_operand_aliasing={{0}: (8, {}), {1}: (9, {})} | custom-call | tf_op jit(solution)/shard_map/collide_7/pallas_call | solution.py:979
  98.9 0.1 collective-permute-start.23
  99.0 5.3 %collective-permute-start.24 = (f32[48,256]{1,0:T(8,128)S(1)}, f32[48,256]{1,0:T(8,128)S(1)}, u32[]{:S(2)}, u32[]{:S(2)}) collective-permute-start(f32[48,256]{1,0:T(8,128)S(1)} %stack_rows.29.refs_0_), channel_id=1, source_target_pairs={{0,24},{8,0},{16,8},{24,16},{1,25},{9,1},{17,9},{25,17},{2,26},{10... | collective-permute-start | bytes 147464 | tf_op jit(solution)/shard_map/ppermute | solution.py:52
  104.2 3.0 %collide_8.1 = (f32[3,528,128]{2,1,0:T(8,128)}, f32[3,528,128]{2,1,0:T(8,128)}, f32[8,128]{1,0:T(8,128)S(1)}) custom-call(s32[14]{0:T(128)S(1)} %concatenate.3.meta_ref, f32[2,8,128]{2,1,0:T(8,128)S(1)} %broadcast_in_dim.2.dirs_ref, bf16[280,256]{1,0:T(8,128)(2,1)S(1)} %get-tuple-element.82.table_ref, ...), custom_call_target="tpu_custom_call", output_to_operand_aliasing={{0}: (8, {}), {1}: (9, {})} | custom-call | tf_op jit(solution)/shard_map/collide_8/pallas_call | solution.py:979
  107.2 3.1 %substep_2.1 = (f32[3,1,1,1,256]{4,3,2,1,0:T(1,128)}, f32[3,1,1,1,256]{4,3,2,1,0:T(1,128)}) custom-call(s32[14]{0:T(128)S(1)} %concatenate.3.meta_ref, f32[8,256]{1,0:T(8,128)S(1)} %get-tuple-element.80.start_ref, s32[224,2]{1,0:T(8,128)S(1)} %bitcast.62, s32[18]{0:T(128)S(1)} %get-tuple-element.101.counts_ref, f32[8,256]{1,0:T(8,128)S(1)} %get-tuple-element.114.speed_ref, ...), custom_call_target="tpu_custom_call" | custom-call | tf_op jit(solution)/shard_map/substep_2/pallas_call | solution.py:998
  (45 shorter events, 0.3 us)
Async XLA Ops:
  0.6 9.3 %copy-start = (f32[3,1,1,1,49152]{4,3,2,1,0:T(1,128)S(1)}, f32[3,1,1,1,49152]{4,3,2,1,0:T(1,128)}, u32[]{:S(2)}) copy-start(f32[3,1,1,1,49152]{4,3,2,1,0:T(1,128)} %param.12) | copy-start | bytes 1769476
  2.8 0.9 copy-start.3
  3.7 0.9 copy-start.4
  4.6 0.7 copy-start.6
  5.3 0.7 copy-start.7
  6.9 8.1 %collective-permute-start = (f32[352,128]{1,0:T(8,128)S(1)}, f32[352,128]{1,0:T(8,128)S(1)}, u32[]{:S(2)}, u32[]{:S(2)}) collective-permute-start(f32[352,128]{1,0:T(8,128)S(1)} %stack_rows.15), channel_id=1, source_target_pairs={{0,1},{1,0},{2,3},{3,2},{4,5},{5,4},{6,7},{7,6},{8,9},{9,8},{10,11... | collective-permute-start | bytes 540680 | tf_op jit(solution)/shard_map/ppermute | solution.py:52
  9.9 1.1 copy-start.1
  15.0 1.9 %copy-start.2 = (f32[3,1,1,1,49152]{4,3,2,1,0:T(1,128)S(1)}, f32[3,1,1,1,49152]{4,3,2,1,0:T(1,128)}, u32[]{:S(2)}) copy-start(f32[3,1,1,1,49152]{4,3,2,1,0:T(1,128)} %param.13) | copy-start | bytes 1769476
  15.1 5.9 %collective-permute-start.1 = (f32[200,128]{1,0:T(8,128)S(1)}, f32[200,128]{1,0:T(8,128)S(1)}, u32[]{:S(2)}, u32[]{:S(2)}) collective-permute-start(f32[200,128]{1,0:T(8,128)S(1)} %stack_rows.17), channel_id=1, source_target_pairs={{0,2},{2,4},{4,6},{6,0},{1,3},{3,5},{5,7},{7,1},{8,10},{10,12},{12... | collective-permute-start | bytes 307208 | tf_op jit(solution)/shard_map/ppermute | solution.py:52
  15.2 5.8 %collective-permute-start.2 = (f32[200,128]{1,0:T(8,128)S(1)}, f32[200,128]{1,0:T(8,128)S(1)}, u32[]{:S(2)}, u32[]{:S(2)}) collective-permute-start(f32[200,128]{1,0:T(8,128)S(1)} %stack_rows.18), channel_id=1, source_target_pairs={{0,6},{2,0},{4,2},{6,4},{1,7},{3,1},{5,3},{7,5},{8,14},{10,8},{12,... | collective-permute-start | bytes 307208 | tf_op jit(solution)/shard_map/ppermute | solution.py:52
  21.0 8.3 %collective-permute-start.3 = (f32[264,128]{1,0:T(8,128)S(1)}, f32[264,128]{1,0:T(8,128)S(1)}, u32[]{:S(2)}, u32[]{:S(2)}) collective-permute-start(f32[264,128]{1,0:T(8,128)S(1)} %stack_rows.20), channel_id=1, source_target_pairs={{0,8},{8,16},{16,24},{24,0},{1,9},{9,17},{17,25},{25,1},{2,10},{10... | collective-permute-start | bytes 405512 | tf_op jit(solution)/shard_map/ppermute | solution.py:52
  22.7 8.1 %copy-start.5 = (s32[16,16,32]{2,1,0:T(8,128)S(1)}, s32[16,16,32]{2,1,0:T(8,128)}, u32[]{:S(2)}) copy-start(s32[16,16,32]{2,1,0:T(8,128)} %param.22) | copy-start | bytes 98308
  22.7 8.1 %collective-permute-start.4 = (f32[264,128]{1,0:T(8,128)S(1)}, f32[264,128]{1,0:T(8,128)S(1)}, u32[]{:S(2)}, u32[]{:S(2)}) collective-permute-start(f32[264,128]{1,0:T(8,128)S(1)} %stack_rows.21), channel_id=1, source_target_pairs={{0,24},{8,0},{16,8},{24,16},{1,25},{9,1},{17,9},{25,17},{2,26},{10... | collective-permute-start | bytes 405512 | tf_op jit(solution)/shard_map/ppermute | solution.py:52
  38.1 5.7 %collective-permute-start.5 = (f32[2,24,128]{2,1,0:T(8,128)S(1)}, f32[2,24,128]{2,1,0:T(8,128)S(1)}, u32[]{:S(2)}, u32[]{:S(2)}) collective-permute-start(f32[2,24,128]{2,1,0:T(8,128)S(1)} %get-tuple-element.73), channel_id=1, source_target_pairs={{0,8},{8,16},{16,24},{24,0},{1,9},{9,17},{17,25},{25,1},{2,10},{10... | collective-permute-start | bytes 73736 | tf_op jit(solution)/shard_map/ppermute | solution.py:52
  38.2 5.6 %collective-permute-start.6 = (f32[2,24,128]{2,1,0:T(8,128)S(1)}, f32[2,24,128]{2,1,0:T(8,128)S(1)}, u32[]{:S(2)}, u32[]{:S(2)}) collective-permute-start(f32[2,24,128]{2,1,0:T(8,128)S(1)} %get-tuple-element.74), channel_id=1, source_target_pairs={{0,24},{8,0},{16,8},{24,16},{1,25},{9,1},{17,9},{25,17},{2,26},{10... | collective-permute-start | bytes 73736 | tf_op jit(solution)/shard_map/ppermute | solution.py:52
  43.8 3.3 %collective-permute-start.7 = (f32[2,24,128]{2,1,0:T(8,128)S(1)}, f32[2,24,128]{2,1,0:T(8,128)S(1)}, u32[]{:S(2)}, u32[]{:S(2)}) collective-permute-start(f32[2,24,128]{2,1,0:T(8,128)S(1)} %get-tuple-element.76), channel_id=1, source_target_pairs={{0,2},{2,4},{4,6},{6,0},{1,3},{3,5},{5,7},{7,1},{8,10},{10,12},{12... | collective-permute-start | bytes 73736 | tf_op jit(solution)/shard_map/ppermute | solution.py:52
  43.9 3.3 %collective-permute-start.8 = (f32[2,24,128]{2,1,0:T(8,128)S(1)}, f32[2,24,128]{2,1,0:T(8,128)S(1)}, u32[]{:S(2)}, u32[]{:S(2)}) collective-permute-start(f32[2,24,128]{2,1,0:T(8,128)S(1)} %get-tuple-element.77), channel_id=1, source_target_pairs={{0,6},{2,0},{4,2},{6,4},{1,7},{3,1},{5,3},{7,5},{8,14},{10,8},{12,... | collective-permute-start | bytes 73736 | tf_op jit(solution)/shard_map/ppermute | solution.py:52
  47.3 5.1 %collective-permute-start.9 = (f32[16,304]{1,0:T(8,128)S(1)}, f32[16,304]{1,0:T(8,128)S(1)}, u32[]{:S(2)}, u32[]{:S(2)}) collective-permute-start(f32[16,304]{1,0:T(8,128)S(1)} %get-tuple-element.79), channel_id=1, source_target_pairs={{0,1},{1,0},{2,3},{3,2},{4,5},{5,4},{6,7},{7,6},{8,9},{9,8},{10,11... | collective-permute-start | bytes 58376 | tf_op jit(solution)/shard_map/ppermute | solution.py:52
  48.9 0.7 copy-start.8
  53.4 3.7 %collective-permute-start.10 = (f32[8,256]{1,0:T(8,128)S(1)}, f32[8,256]{1,0:T(8,128)S(1)}, u32[]{:S(2)}, u32[]{:S(2)}) collective-permute-start(f32[8,256]{1,0:T(8,128)S(1)} %get-tuple-element.104.refs_0_), channel_id=1, source_target_pairs={{0,1},{1,0},{2,3},{3,2},{4,5},{5,4},{6,7},{7,6},{8,9},{9,8},{10,11... | collective-permute-start | bytes 24584 | tf_op jit(solution)/shard_map/ppermute | solution.py:52
  57.2 4.7 %collective-permute-start.11 = (f32[16,256]{1,0:T(8,128)S(1)}, f32[16,256]{1,0:T(8,128)S(1)}, u32[]{:S(2)}, u32[]{:S(2)}) collective-permute-start(f32[16,256]{1,0:T(8,128)S(1)} %stack_rows.24.refs_0_), channel_id=1, source_target_pairs={{0,2},{2,4},{4,6},{6,0},{1,3},{3,5},{5,7},{7,1},{8,10},{10,12},{12... | collective-permute-start | bytes 49160 | tf_op jit(solution)/shard_map/ppermute | solution.py:52
  57.2 4.7 %collective-permute-start.12 = (f32[16,256]{1,0:T(8,128)S(1)}, f32[16,256]{1,0:T(8,128)S(1)}, u32[]{:S(2)}, u32[]{:S(2)}) collective-permute-start(f32[16,256]{1,0:T(8,128)S(1)} %stack_rows.24.refs_0_), channel_id=1, source_target_pairs={{0,6},{2,0},{4,2},{6,4},{1,7},{3,1},{5,3},{7,5},{8,14},{10,8},{12,... | collective-permute-start | bytes 49160 | tf_op jit(solution)/shard_map/ppermute | solution.py:52
  61.9 7.4 %collective-permute-start.13 = (f32[48,256]{1,0:T(8,128)S(1)}, f32[48,256]{1,0:T(8,128)S(1)}, u32[]{:S(2)}, u32[]{:S(2)}) collective-permute-start(f32[48,256]{1,0:T(8,128)S(1)} %stack_rows.25.refs_0_), channel_id=1, source_target_pairs={{0,8},{8,16},{16,24},{24,0},{1,9},{9,17},{17,25},{25,1},{2,10},{10... | collective-permute-start | bytes 147464 | tf_op jit(solution)/shard_map/ppermute | solution.py:52
  62.8 6.5 %collective-permute-start.14 = (f32[48,256]{1,0:T(8,128)S(1)}, f32[48,256]{1,0:T(8,128)S(1)}, u32[]{:S(2)}, u32[]{:S(2)}) collective-permute-start(f32[48,256]{1,0:T(8,128)S(1)} %stack_rows.25.refs_0_), channel_id=1, source_target_pairs={{0,24},{8,0},{16,8},{24,16},{1,25},{9,1},{17,9},{25,17},{2,26},{10... | collective-permute-start | bytes 147464 | tf_op jit(solution)/shard_map/ppermute | solution.py:52
  71.8 3.7 %collective-permute-start.15 = (f32[8,256]{1,0:T(8,128)S(1)}, f32[8,256]{1,0:T(8,128)S(1)}, u32[]{:S(2)}, u32[]{:S(2)}) collective-permute-start(f32[8,256]{1,0:T(8,128)S(1)} %get-tuple-element.110.refs_0_), channel_id=1, source_target_pairs={{0,1},{1,0},{2,3},{3,2},{4,5},{5,4},{6,7},{7,6},{8,9},{9,8},{10,11... | collective-permute-start | bytes 24584 | tf_op jit(solution)/shard_map/ppermute | solution.py:52
  75.6 4.7 %collective-permute-start.16 = (f32[16,256]{1,0:T(8,128)S(1)}, f32[16,256]{1,0:T(8,128)S(1)}, u32[]{:S(2)}, u32[]{:S(2)}) collective-permute-start(f32[16,256]{1,0:T(8,128)S(1)} %stack_rows.26.refs_0_), channel_id=1, source_target_pairs={{0,2},{2,4},{4,6},{6,0},{1,3},{3,5},{5,7},{7,1},{8,10},{10,12},{12... | collective-permute-start | bytes 49160 | tf_op jit(solution)/shard_map/ppermute | solution.py:52
  75.6 4.7 %collective-permute-start.17 = (f32[16,256]{1,0:T(8,128)S(1)}, f32[16,256]{1,0:T(8,128)S(1)}, u32[]{:S(2)}, u32[]{:S(2)}) collective-permute-start(f32[16,256]{1,0:T(8,128)S(1)} %stack_rows.26.refs_0_), channel_id=1, source_target_pairs={{0,6},{2,0},{4,2},{6,4},{1,7},{3,1},{5,3},{7,5},{8,14},{10,8},{12,... | collective-permute-start | bytes 49160 | tf_op jit(solution)/shard_map/ppermute | solution.py:52
  80.3 7.0 %collective-permute-start.18 = (f32[48,256]{1,0:T(8,128)S(1)}, f32[48,256]{1,0:T(8,128)S(1)}, u32[]{:S(2)}, u32[]{:S(2)}) collective-permute-start(f32[48,256]{1,0:T(8,128)S(1)} %stack_rows.27.refs_0_), channel_id=1, source_target_pairs={{0,8},{8,16},{16,24},{24,0},{1,9},{9,17},{17,25},{25,1},{2,10},{10... | collective-permute-start | bytes 147464 | tf_op jit(solution)/shard_map/ppermute | solution.py:52
  81.5 5.9 %collective-permute-start.19 = (f32[48,256]{1,0:T(8,128)S(1)}, f32[48,256]{1,0:T(8,128)S(1)}, u32[]{:S(2)}, u32[]{:S(2)}) collective-permute-start(f32[48,256]{1,0:T(8,128)S(1)} %stack_rows.27.refs_0_), channel_id=1, source_target_pairs={{0,24},{8,0},{16,8},{24,16},{1,25},{9,1},{17,9},{25,17},{2,26},{10... | collective-permute-start | bytes 147464 | tf_op jit(solution)/shard_map/ppermute | solution.py:52
  89.9 3.8 %collective-permute-start.20 = (f32[8,256]{1,0:T(8,128)S(1)}, f32[8,256]{1,0:T(8,128)S(1)}, u32[]{:S(2)}, u32[]{:S(2)}) collective-permute-start(f32[8,256]{1,0:T(8,128)S(1)} %get-tuple-element.116.refs_0_), channel_id=1, source_target_pairs={{0,1},{1,0},{2,3},{3,2},{4,5},{5,4},{6,7},{7,6},{8,9},{9,8},{10,11... | collective-permute-start | bytes 24584 | tf_op jit(solution)/shard_map/ppermute | solution.py:52
  93.7 5.1 %collective-permute-start.21 = (f32[16,256]{1,0:T(8,128)S(1)}, f32[16,256]{1,0:T(8,128)S(1)}, u32[]{:S(2)}, u32[]{:S(2)}) collective-permute-start(f32[16,256]{1,0:T(8,128)S(1)} %stack_rows.28.refs_0_), channel_id=1, source_target_pairs={{0,2},{2,4},{4,6},{6,0},{1,3},{3,5},{5,7},{7,1},{8,10},{10,12},{12... | collective-permute-start | bytes 49160 | tf_op jit(solution)/shard_map/ppermute | solution.py:52
  93.8 5.1 %collective-permute-start.22 = (f32[16,256]{1,0:T(8,128)S(1)}, f32[16,256]{1,0:T(8,128)S(1)}, u32[]{:S(2)}, u32[]{:S(2)}) collective-permute-start(f32[16,256]{1,0:T(8,128)S(1)} %stack_rows.28.refs_0_), channel_id=1, source_target_pairs={{0,6},{2,0},{4,2},{6,4},{1,7},{3,1},{5,3},{7,5},{8,14},{10,8},{12,... | collective-permute-start | bytes 49160 | tf_op jit(solution)/shard_map/ppermute | solution.py:52
  98.9 8.3 %collective-permute-start.23 = (f32[48,256]{1,0:T(8,128)S(1)}, f32[48,256]{1,0:T(8,128)S(1)}, u32[]{:S(2)}, u32[]{:S(2)}) collective-permute-start(f32[48,256]{1,0:T(8,128)S(1)} %stack_rows.29.refs_0_), channel_id=1, source_target_pairs={{0,8},{8,16},{16,24},{24,0},{1,9},{9,17},{17,25},{25,1},{2,10},{10... | collective-permute-start | bytes 147464 | tf_op jit(solution)/shard_map/ppermute | solution.py:52
  99.0 8.2 %collective-permute-start.24 = (f32[48,256]{1,0:T(8,128)S(1)}, f32[48,256]{1,0:T(8,128)S(1)}, u32[]{:S(2)}, u32[]{:S(2)}) collective-permute-start(f32[48,256]{1,0:T(8,128)S(1)} %stack_rows.29.refs_0_), channel_id=1, source_target_pairs={{0,24},{8,0},{16,8},{24,16},{1,25},{9,1},{17,9},{25,17},{2,26},{10... | collective-permute-start | bytes 147464 | tf_op jit(solution)/shard_map/ppermute | solution.py:52

commit v3 on v2

--- a/solution.py
+++ b/solution.py
@@ -14,6 +14,7 @@
 LANES = 128
 GROUP = 8
 TWIN = 4
+SENT = 4
 
 bead_mass = 5.0
 step_size = 0.02
@@ -27,7 +28,7 @@
 far_own = 3000.0
 far_ghost = 9000.0
 vmem_limit = 48 * 1024 * 1024
-vmem_most = 48 * 1024 * 1024
+vmem_most = 61 * 1024 * 1024
 NT = (((1,), (1,)), ((), ()))
 NN = (((1,), (0,)), ((), ()))
 exact = lax.Precision.HIGHEST
@@ -446,6 +447,8 @@
 
 
 def pack_inputs(
+    sheets,
+    face_rows,
     meta_ref,
     pos_ref,
     vel_ref,
@@ -457,16 +460,24 @@
     rows_vel_ref,
     *refs,
 ):
-    out_refs, (held_pos, held_vel, sems) = refs[:6], refs[6:]
+    out_refs, (held_pos, held_vel, sems) = refs[: len(sheets)], refs[len(sheets) :]
     copies = [(bead_pos_ref, held_pos), (bead_vel_ref, held_vel)]
-    for face, out_ref in enumerate(out_refs):
-        copies.append((pos_ref.at[:, face], out_ref.at[0:3]))
-        copies.append((vel_ref.at[:, face], out_ref.at[3:6]))
+    for faces, out_ref in zip(sheets, out_refs):
+        for k, face in enumerate(faces):
+            first = k * (6 * face_rows + GROUP)
+            for c in range(6):
+                source = pos_ref if c < 3 else vel_ref
+                rows = pl.ds(first + c * face_rows, face_rows)
+                copies.append((source.at[c % 3, face], out_ref.at[rows]))
     copies = [pltpu.make_async_copy(a, b, sems.at[k]) for k, (a, b) in enumerate(copies)]
     for copy in copies:
         copy.start()
-    for face, out_ref in enumerate(out_refs):
-        out_ref[6] = jnp.full(out_ref.shape[1:], meta_ref[8 + face], jnp.int32).astype(f32)
+    for faces, out_ref in zip(sheets, out_refs):
+        for k, face in enumerate(faces):
+            first = k * (6 * face_rows + GROUP) + 6 * face_rows
+            out_ref[first : first + GROUP, :] = jnp.full(
+                (GROUP, LANES), meta_ref[8 + face], jnp.int32
+            ).astype(f32)
     slots = start_ref.shape[1]
     start_ref[...] = jnp.zeros_like(start_ref)
     rows_pos_ref[...] = jnp.zeros_like(rows_pos_ref)
@@ -480,9 +491,7 @@
             rows_pos_ref[d, k : k + 1, :] = held_pos[d, k : k + 1, :]
             rows_vel_ref[d, k : k + 1, :] = held_vel[d, k : k + 1, :]
     start = start_ref[...]
-    whole = payload(start, slot_live(slots, meta_ref[7], GROUP))
-    for k in range(slots // LANES):
-        block_ref[k * GROUP : (k + 1) * GROUP, :] = whole[:, k * LANES : (k + 1) * LANES]
+    block_ref[...] = payload(start, slot_live(slots, meta_ref[7], GROUP))
 
 
 def stack_rows(parts, *refs):
@@ -499,9 +508,9 @@
 
 def payload(position, live):
     slots = position.shape[1]
-    row_ids = lax.broadcasted_iota(jnp.int32, (GROUP, slots), 0)
-    flag = jnp.where(live, 1.0, 0.0)
-    return jnp.where(row_ids == 3, flag, jnp.where(row_ids < 3, position, 0.0))
+    row_ids = lax.broadcasted_iota(jnp.int32, (SENT, slots), 0)
+    flag = jnp.where(live[:SENT], 1.0, 0.0)
+    return jnp.where(row_ids == 3, flag, position[:SENT])
 
 
 def thirds_of(value):
@@ -518,7 +527,7 @@
     return value[:GROUP] + (value[GROUP : 2 * GROUP] + value[2 * GROUP :])
 
 
-def forces(own, chains, counts, bonds_ref, blocks, centre, lengths, mine_ref, packed, push):
+def forces(own, chains, counts, bonds_ref, fetch, centre, lengths, mine_ref, packed, push):
     slots = own.shape[1]
     bond_slots = bonds_ref.shape[0]
     row_ids = lax.broadcasted_iota(jnp.int32, (GROUP, slots), 0)
@@ -534,31 +543,27 @@
         mine_ref[d] = jnp.broadcast_to(columns[:, d : d + 1], (slots, LANES))
 
     packed[...] = jnp.full(packed.shape, far_ghost, f32)
-    lane = lax.broadcasted_iota(jnp.int32, (GROUP, LANES), 1)
+    lane = lax.broadcasted_iota(jnp.int32, (SENT, LANES), 1)
     tiles = slots // LANES
     offset = jnp.int32(0)
-    index = 0
-    for ref in blocks:
-        for b in range(ref.shape[0] // GROUP):
-            near = ref[b * GROUP : (b + 1) * GROUP, :] - mid
-            near = near - length * jnp.floor(near * (1.0 / length) + 0.5)
-            tile, turn = offset // LANES, offset % LANES
-            turned = [
-                pltpu.roll(near[:, k * LANES : (k + 1) * LANES], turn, axis=1)
-                for k in range(tiles)
-            ]
-            for k in range(tiles + 1):
-                if k == 0:
-                    value = turned[0]
-                elif k == tiles:
-                    value = turned[-1]
-                else:
-                    value = jnp.where(lane < turn, turned[k - 1], turned[k])
-                place = (tile + k) * LANES + lane
-                taken = (place >= offset) & (place < offset + counts[index])
-                packed[tile + k] = jnp.where(taken, value, packed[tile + k])
-            offset = offset + counts[index]
-            index += 1
+    for block, count in zip(fetch(), counts):
+        near = block - mid[:SENT]
+        near = near - length[:SENT] * jnp.floor(near * (1.0 / length[:SENT]) + 0.5)
+        tile, turn = offset // LANES, offset % LANES
+        turned = [
+            pltpu.roll(near[:, k * LANES : (k + 1) * LANES], turn, axis=1) for k in range(tiles)
+        ]
+        for k in range(tiles + 1):
+            if k == 0:
+                value = turned[0]
+            elif k == tiles:
+                value = turned[-1]
+            else:
+                value = jnp.where(lane < turn, turned[k - 1], turned[k])
+            place = (tile + k) * LANES + lane
+            taken = (place >= offset) & (place < offset + count)
+            packed[tile + k, :SENT, :] = jnp.where(taken, value, packed[tile + k, :SENT, :])
+        offset = offset + count
 
     push[...] = jnp.zeros_like(push)
     chunk = 64
@@ -617,6 +622,8 @@
 def force_scratch(slots, blocks):
     tiles = -(-(blocks * slots // LANES + 2) // 2) * 2
     return [
+        pltpu.VMEM((blocks, SENT, slots), f32),
+        pltpu.SemaphoreType.DMA((blocks,)),
         pltpu.VMEM((3, slots, LANES), f32),
         pltpu.VMEM((tiles, GROUP, LANES), f32),
         pltpu.VMEM((3, slots, LANES), f32),
@@ -627,18 +634,38 @@
     return [meta[3 + d].astype(f32) + 0.5 * sizes[d] for d in range(3)]
 
 
-def first_forces(sizes, lengths, sources, meta_ref, start_ref, bonds_ref, *refs):
-    blocks, (push_ref, counts_ref), scratch = (
-        refs[:sources],
-        refs[sources : sources + 2],
-        refs[sources + 2 :],
-    )
+def fetching(meta, sizes, peers, blocks_ref, held, sems):
+    copies = [
+        pltpu.make_async_copy(blocks_ref.at[which], held.at[k], sems.at[k])
+        for k, which in enumerate(surrounding(meta, sizes, peers))
+    ]
+    for copy in copies:
+        copy.start()
+
+    def fetch():
+        for copy in copies:
+            copy.wait()
+        return [held[k] for k in range(len(copies))]
+
+    return fetch
+
+
+def first_forces(
+    sizes,
+    peers,
+    meta_ref,
+    start_ref,
+    bonds_ref,
+    blocks_ref,
+    push_ref,
+    counts_ref,
+    held,
+    sems,
+    *scratch,
+):
     meta = [meta_ref[k] for k in range(8)]
-    counts = []
-    for ref in blocks:
-        for b in range(ref.shape[0] // GROUP):
-            live = ref[b * GROUP + 3 : b * GROUP + 4, :]
-            counts.append(jnp.sum(live).astype(jnp.int32))
+    blocks = fetching(meta, sizes, peers, blocks_ref, held, sems)()
+    counts = [jnp.sum(block[3:4]).astype(jnp.int32) for block in blocks]
     for k, count in enumerate(counts):
         counts_ref[k] = count
     push_ref[...] = forces(
@@ -646,11 +673,15 @@
         meta[7],
         counts,
         bonds_ref,
-        blocks,
+        lambda: blocks,
         centre_of(meta, sizes),
-        lengths,
+        lengths_of(sizes, peers),
         *scratch,
     )
+
+
+def lengths_of(sizes, peers):
+    return [float(size * count) for size, count in zip(sizes, peers)]
 
 
 def finish_cells(
@@ -697,13 +728,23 @@
 
 
 def substep(
-    sizes, lengths, last, sources, meta_ref, start_ref, bonds_ref, counts_ref, speed_ref, moved_ref, *refs
+    sizes,
+    peers,
+    last,
+    meta_ref,
+    start_ref,
+    bonds_ref,
+    counts_ref,
+    speed_ref,
+    moved_ref,
+    blocks_ref,
+    order_ref,
+    *refs,
 ):
-    blocks, outs, scratch = refs[:sources], refs[sources + 1 : -3], refs[-3:]
+    outs, (held, sems, *scratch) = refs[:-5], refs[-5:]
     meta = [meta_ref[k] for k in range(8)]
-    counts = [
-        counts_ref[k] for k in range(sum(ref.shape[0] // GROUP for ref in blocks))
-    ]
+    fetch = fetching(meta, sizes, peers, blocks_ref, held, sems)
+    counts = [counts_ref[k] for k in range(held.shape[0])]
     start = start_ref[...]
     moved = moved_ref[...]
     push = forces(
@@ -711,9 +752,9 @@
         meta[7],
         counts,
         bonds_ref,
-        blocks,
+        fetch,
         centre_of(meta, sizes),
-        lengths,
+        lengths_of(sizes, peers),
         *scratch,
     )
     live = slot_live(start.shape[1], meta[7], GROUP)
@@ -754,13 +795,14 @@
     return [(k, 0, value.shape[0]) for k, value in enumerate(operands)]
 
 
-def halo(block, pieces):
-    parts = [block] + neighbours(block, "gz")
-    row = stacked(whole_rows(parts), parts, [pieces[0]()])
-    parts = [row] + neighbours(row, "gy")
-    plane = stacked(whole_rows(parts), parts, [pieces[1]()])
-    sides = neighbours(plane, "gx")
-    return [plane] + sides, pieces[2]()
+def surrounding(meta, sizes, peers):
+    found = [jnp.int32(0)]
+    for d in range(3):
+        here = meta[3 + d] // sizes[d]
+        steps = range(peers[d]) if peers[d] < 3 else (-1, 0, 1)
+        spots = [lax.rem(here + (step + peers[d]), peers[d]) for step in steps]
+        found = [f * peers[d] + spot for f in found for spot in spots]
+    return found
 
 
 def like(*shape, dtype=f32):
@@ -784,7 +826,7 @@
     sizes = cell_axis.shape
     cells = Cells(*sizes)
     names = ("gx", "gy", "gz")
-    lengths = tuple(float(sizes[d] * lax.axis_size(names[d])) for d in range(3))
+    peers = tuple(lax.axis_size(name) for name in names)
     slots_here = sol_pos.shape[-1]
     buffer_slots = mig_pos.shape[-1]
     bead_slots = bead_pos.shape[-1]
@@ -807,18 +849,24 @@
     velocity = sol_vel.reshape(3, rows_here, LANES)
 
     any_spec = pl.BlockSpec(memory_space=pl.ANY)
-    face_height = 7 * face_rows
+    face_height = 6 * face_rows + GROUP
     bead_shape = like(GROUP, bead_slots)
     tiles = bead_slots // LANES
     rows_shape = like(3, GROUP, LANES)
+    routes = []
+    for d, axis in enumerate(names):
+        if lax.axis_size(axis) == 2:
+            routes.append((axis, 1, (2 * d, 2 * d + 1)))
+        else:
+            routes += [(axis, 1, (2 * d + 1,)), (axis, -1, (2 * d,))]
     start, block, bead_rows_pos, bead_rows_vel, *packed = pl.pallas_call(
-        pack_inputs,
-        out_shape=[bead_shape, like(tiles * GROUP, LANES), rows_shape, rows_shape]
-        + [like(7, face_rows, LANES)] * 6,
+        functools.partial(pack_inputs, [faces for _, _, faces in routes], face_rows),
+        out_shape=[bead_shape, like(SENT, bead_slots), rows_shape, rows_shape]
+        + [like(len(faces) * face_height, LANES) for _, _, faces in routes],
         in_specs=[smem()] + [pl.BlockSpec(memory_space=pltpu.HBM)] * 4,
-        out_specs=[vmem()] * 10,
+        out_specs=[vmem()] * (4 + len(routes)),
         scratch_shapes=[pltpu.VMEM((3, tiles, LANES), f32)] * 2
-        + [pltpu.SemaphoreType.DMA((14,))],
+        + [pltpu.SemaphoreType.DMA((38,))],
         compiler_params=params(vmem_most),
         name="pack_inputs",
     )(
@@ -828,7 +876,12 @@
         bead_pos.reshape(3, tiles, LANES),
         bead_vel.reshape(3, tiles, LANES),
     )
-    packed = [value.reshape(face_height, LANES) for value in packed]
+    arriving, spots = [], [None] * 6
+    for (axis, step, faces), value in zip(routes, packed):
+        for k, face in enumerate(faces):
+            spots[face ^ 1] = (len(arriving), k * face_height)
+        arriving.append(moved_along(value, axis, step))
+    around = lax.all_gather(block, names)
     bonds = bond_list.reshape(2, bond_slots).T
 
     thirds = 3
@@ -849,43 +902,10 @@
             name=f"bin_residents_{piece}",
         )(meta, position, velocity, *earlier, *order)
 
-    def swap(axis, low, high, body):
-        if lax.axis_size(axis) == 2:
-            both = [packed[low], packed[high], body]
-            came = moved_along(stacked(whole_rows(both), both), axis, 1)
-            return [came], [(0, face_height), (0, 0)], [(0, 2 * face_height)]
-        up = stacked(whole_rows([packed[high], body]), [packed[high], body])
-        down = stacked(whole_rows([packed[low], body]), [packed[low], body])
-        came = [moved_along(up, axis, 1), moved_along(down, axis, -1)]
-        return came, [(0, 0), (1, 0)], [(0, face_height), (1, face_height)]
-
-    arrived, places, blocks = {}, {}, block
-    totals = None
-    for piece, (axis, low) in enumerate((("gz", 4), ("gy", 2), ("gx", 0))):
-        came, spots, bodies = swap(axis, low, low + 1, blocks)
-        totals = bin_piece(piece, [] if totals is None else [totals], [blocks])
-        height = blocks.shape[0]
-        arrived[axis], places[axis] = came, spots
-        if axis != "gx":
-            parts = [(0, 0, height)] + [(1 + w, at, height) for w, at in bodies]
-            blocks = stacked(parts, [blocks] + came, [totals])
-        else:
-            around = [blocks] + [
-                stacked([(0, at, height)], [came[w]]) for w, at in bodies
-            ]
-
-    def as_blocks(value):
-        n = value.shape[0] // (GROUP * tiles)
-        return (
-            value.reshape(n, tiles, GROUP, LANES)
-            .transpose(0, 2, 1, 3)
-            .reshape(n * GROUP, bead_slots)
-        )
-
-    arriving, spots = [], []
-    for axis in names:
-        spots += [(len(arriving) + w, at) for w, at in places[axis]]
-        arriving += arrived[axis]
+    totals = []
+    for piece in range(thirds):
+        totals = [bin_piece(piece, totals, [])]
+    totals = totals[0]
 
     face_x = like(2, -(-(sizes[1] + 1) // GROUP) * GROUP, LANES)
     face_y = like(2, -(-(sizes[0] + 1) // GROUP) * GROUP, LANES)
@@ -899,17 +919,17 @@
         name="bin_arrivals",
     )(meta, *arriving, bead_rows_pos, bead_rows_vel, axis_rows, totals)
 
-    around = [as_blocks(value) for value in around]
-    many = sum(value.shape[0] // GROUP for value in around)
+    many = math.prod(min(count, 3) for count in peers)
+    hbm_spec = pl.BlockSpec(memory_space=pltpu.HBM)
     push, counts = pl.pallas_call(
-        functools.partial(first_forces, sizes, lengths, len(around)),
+        functools.partial(first_forces, sizes, peers),
         out_shape=[bead_shape, like(many, dtype=jnp.int32)],
-        in_specs=[smem()] + [vmem()] * (2 + len(around)),
+        in_specs=[smem(), vmem(), vmem(), hbm_spec],
         out_specs=[vmem(), smem()],
         scratch_shapes=force_scratch(bead_slots, many),
         compiler_params=params(),
         name="first_forces",
-    )(meta, start, bonds, *around)
+    )(meta, start, bonds, around)
 
     below, above = moved_along(high, "gx", 1), moved_along(low, "gx", -1)
     totals, low, high = pl.pallas_call(
@@ -939,7 +959,7 @@
             like(7 * cells.height, cells.inner, dtype=bf16),
             bead_shape,
             bead_shape,
-            bead_shape,
+            like(SENT, bead_slots),
         ],
         in_specs=[smem()] + [vmem()] * 8,
         out_specs=[vmem()] * 4,
@@ -992,20 +1012,19 @@
 
     for step in range(3):
         last = step == 2
-        thunks = [functools.partial(collide_piece, 3 * step + k) for k in range(3)]
-        ghosts, order = halo(pay, thunks)
+        ghosts = lax.all_gather(pay, names)
+        for piece in range(3 * step, 3 * step + 3):
+            order = collide_piece(piece)
         final = like(3, 1, 1, 1, bead_slots)
         outcome = pl.pallas_call(
-            functools.partial(substep, sizes, lengths, last, len(ghosts)),
-            out_shape=[final] * 2 if last else [bead_shape] * 3,
-            in_specs=[smem(), vmem(), vmem(), smem()]
-            + [vmem()] * (2 + len(ghosts))
-            + [any_spec],
+            functools.partial(substep, sizes, peers, last),
+            out_shape=[final] * 2 if last else [bead_shape] * 2 + [like(SENT, bead_slots)],
+            in_specs=[smem(), vmem(), vmem(), smem(), vmem(), vmem(), hbm_spec, any_spec],
             out_specs=[vmem()] * (2 if last else 3),
             scratch_shapes=force_scratch(bead_slots, many),
             compiler_params=params(),
             name=f"substep_{step}",
-        )(meta, start, bonds, counts, speed, moved, *ghosts, order)
+        )(meta, start, bonds, counts, speed, moved, ghosts, order)
         speed, moved = outcome[:2]
         pay = outcome[-1]
 

time: 112 us -> 351 us (3.13); the launches traced: 110 us -> 353 us
  blocking collectives: 0 us -> 265 us
  starting transfers between devices: 35.9 us -> 15.7 us
    all_gather x0 -> x4, blocking collectives: none -> 265 us  [the longest x3 195 us: shards(): ghosts = lax.all_gather(pay, names)]
    ppermute x25 -> x10, starting transfers between devices: 35.9 us -> 15.7 us  [moved_along(): lax.ppermute(value, axis, [(i, (i + by) % peers) for i in range(peers)])]
    pallas_call x20 -> x5, Pallas kernels: 11.8 us -> 19.6 us  [the longest x3 12.8 us: shards(): pl.pallas_call(functools.partial(substep, sizes, peers, last), out_shape=...]
  transfers between devices with their start and end apart: 25 -> 10, of which waited for: 6 -> 3; matrix products, arithmetic and copies ran while one was open for 0% -> 0% of each run, Pallas kernels for 39% -> 4%
where the time goes in v3:
time: 351 us; the launch traced here: 353 us
  blocking collectives  265 us (75%)
  Pallas kernels  62.6 us (18%)
  starting transfers between devices  15.7 us (4%)
  local copies, waits for them, and re-layouts  4.34 us (1%)
    all_gather x3, blocking collectives, shards(): ghosts = lax.all_gather(pay, names)  195 us
    all_gather x1, blocking collectives, shards(): around = lax.all_gather(block, names)  69.4 us
    pallas_call x9, Pallas kernels, collide_piece(): pl.pallas_call(body, out_shape=[solvent_shape, solvent_shape, like(GROUP,...  27 us
    ppermute x10, starting transfers between devices, moved_along(): lax.ppermute(value, axis, [(i, (i + by) % peers) for i in range(peers)])  15.7 us
    pallas_call x3, Pallas kernels, shards(): pl.pallas_call(functools.partial(substep, sizes, peers, last), out_shape=...  12.8 us
    pallas_call x3, Pallas kernels, bin_piece(): pl.pallas_call(functools.partial(bin_residents, cells, piece * count, cou...  8.62 us
  transfers between devices with their start and end apart: 10, of which 3 were waited for; matrix products, arithmetic and copies ran while one was open for 0% of the time, Pallas kernels for 4%

profile of v3, /device:TPU:0, one launch (start us, length us, event | category | flops | bytes accessed | tf_op | source)
XLA Modules:
  0.0 353.0 jit_solution(4626968936068859707)
XLA Ops:
  1.9 0.0 copy-start.11
  1.9 0.0 copy-start.12
  1.9 0.6 copy-done.11
  2.6 0.0 copy-done.12
  2.6 0.6 concatenate.3.meta_ref
  3.2 2.8 pack_inputs.1
  5.9 3.0 collective-permute-start.4
  8.9 1.6 collective-permute-start
  10.5 2.2 collective-permute-start.1
  12.8 0.0 collective-permute-start.2
  12.8 1.7 collective-permute-start.3
  14.5 0.6 copy-done.5
  15.1 1.1 copy-done
  16.2 1.1 copy-done.2
  17.2 4.0 %bin_residents_0.1.refs_0_ = f32[304,256]{1,0:T(8,128)S(1)} custom-call(s32[14]{0:T(128)S(1)} %copy-done.5, f32[3,384,128]{2,1,0:T(8,128)S(1)} %bitcast.24, f32[3,384,128]{2,1,0:T(8,128)S(1)} %bitcast.33), custom_call_target="tpu_custom_call" | custom-call | tf_op jit(solution)/shard_map/bin_residents_0/pallas_call | solution.py:892
  21.3 4.0 %bin_residents_1.1.refs_0_ = f32[304,256]{1,0:T(8,128)S(1)} custom-call(s32[14]{0:T(128)S(1)} %copy-done.5, f32[3,384,128]{2,1,0:T(8,128)S(1)} %bitcast.25, f32[3,384,128]{2,1,0:T(8,128)S(1)} %bitcast.34, f32[304,256]{1,0:T(8,128)S(1)} %bin_residents_0.1.refs_0_), custom_call_target="tpu_custom_call" | custom-call | tf_op jit(solution)/shard_map/bin_residents_1/pallas_call | solution.py:892
  25.3 0.0 copy-start.6
  25.3 0.0 copy-start.7
  25.3 0.0 copy-start.8
  25.3 0.6 bin_residents_2.1.refs_8_
  25.9 0.0 collective-permute-done.refs_0_
  25.9 0.0 collective-permute-done.1.refs_1_
  25.9 0.0 collective-permute-done.2.refs_2_
  25.9 0.0 collective-permute-done.3.refs_3_
  25.9 0.0 collective-permute-done.4.refs_4_
  25.9 0.3 copy-done.6
  26.2 0.0 copy-done.7
  26.2 0.0 copy-done.8
  26.2 6.2 %bin_arrivals.1 = (f32[2,304,128]{2,1,0:T(8,128)S(1)}, f32[2,24,128]{2,1,0:T(8,128)S(1)}, f32[2,24,128]{2,1,0:T(8,128)S(1)}) custom-call(s32[14]{0:T(128)S(1)} %copy-done.5, f32[152,128]{1,0:T(8,128)S(1)} %collective-permute-done.refs_0_, f32[152,128]{1,0:T(8,128)S(1)} %collective-permute-done.1.refs_1_, f32[152,128]{1,0:T(8,128)S(1)} %collective-permute-done.2.refs_2_, ...), custom_call_target="tpu_custom_call" | custom-call | tf_op jit(solution)/shard_map/bin_arrivals/pallas_call | solution.py:912
  32.4 0.1 collective-permute-start.5
  32.5 3.8 %collective-permute-start.6 = (f32[2,24,128]{2,1,0:T(8,128)S(1)}, f32[2,24,128]{2,1,0:T(8,128)S(1)}, u32[]{:S(2)}, u32[]{:S(2)}) collective-permute-start(f32[2,24,128]{2,1,0:T(8,128)S(1)} %get-tuple-element.65), channel_id=1, source_target_pairs={{0,24},{8,0},{16,8},{24,16},{1,25},{9,1},{17,9},{25,17},{2,26},{10... | collective-permute-start | bytes 73736 | tf_op jit(solution)/shard_map/ppermute | solution.py:53
  36.3 1.8 collective-permute-done.5.below_ref
  38.1 0.0 collective-permute-done.6.above_ref
  38.1 2.8 collective-permute-start.7
  40.9 0.0 collective-permute-start.8
  40.9 0.8 collective-permute-done.7.below_ref
  41.8 0.7 collective-permute-done.8.above_ref
  42.5 0.2 add_faces_y.1
  42.7 0.5 collective-permute-start.9
  43.2 0.0 copy-done.9
  43.2 69.4 %all-gather.4.blocks_ref = f32[32,4,256]{2,1,0:T(4,128)S(1)} all-gather(f32[1,4,256]{2,1,0:T(4,128)S(1)} %bitcast.54), channel_id=2, replica_groups=mesh['gx'=4,'gy'=4,'gz'=2] {'gx','gy','gz'}, dimensions={0}, use_global_device_ids=true | all-gather | bytes 135168 | tf_op jit(solution)/shard_map/all_gather | solution.py:884
  112.6 0.0 copy-done.10
  112.6 0.1 copy.38
  112.7 0.0 copy-done.4
  112.7 4.1 %first_forces.1 = (f32[8,256]{1,0:T(8,128)S(1)}, s32[18]{0:T(128)S(1)}) custom-call(s32[14]{0:T(128)S(1)} %copy-done.5, f32[8,256]{1,0:T(8,128)S(1)} %copy-done.4, s32[224,2]{1,0:T(8,128)S(1)} %bitcast.42, f32[32,4,256]{2,1,0:T(4,128)S(1)} %all-gather.4.blocks_ref), custom_call_target="tpu_custom_call" | custom-call | tf_op jit(solution)/shard_map/first_forces/pallas_call | solution.py:924
  116.8 0.0 collective-permute-done.9.below_ref.above_ref
  116.9 1.0 finish_cells.1
  117.8 0.0 copy-done.1
  117.8 0.0 copy-done.3
  117.9 3.6 %collide_0.1 = (f32[3,528,128]{2,1,0:T(8,128)}, f32[3,528,128]{2,1,0:T(8,128)}, f32[8,128]{1,0:T(8,128)}) custom-call(s32[14]{0:T(128)S(1)} %copy-done.5, f32[2,8,128]{2,1,0:T(8,128)S(1)} %broadcast_in_dim.2.dirs_ref, bf16[280,256]{1,0:T(8,128)(2,1)S(1)} %get-tuple-element.74.table_ref, f32[3,384,128]{2,1,0:T(8,128)S(1)} %bitcast.27, f32[3,384,128]{2,1,0:T(8,128)S(1)} %bitcast.36), custom_call_target="tpu_custom_call" | custom-call | tf_op jit(solution)/shard_map/collide_0/pallas_call | solution.py:999
  121.4 64.0 %all-gather.5.blocks_ref = f32[32,4,256]{2,1,0:T(4,128)S(1)} all-gather(f32[1,4,256]{2,1,0:T(4,128)S(1)} %bitcast.47), channel_id=3, replica_groups=mesh['gx'=4,'gy'=4,'gz'=2] {'gx','gy','gz'}, dimensions={0}, use_global_device_ids=true | all-gather | bytes 135168 | tf_op jit(solution)/shard_map/all_gather | solution.py:1015
  185.4 3.6 %collide_1.1 = (f32[3,528,128]{2,1,0:T(8,128)}, f32[3,528,128]{2,1,0:T(8,128)}, f32[8,128]{1,0:T(8,128)}) custom-call(s32[14]{0:T(128)S(1)} %copy-done.5, f32[2,8,128]{2,1,0:T(8,128)S(1)} %broadcast_in_dim.2.dirs_ref, bf16[280,256]{1,0:T(8,128)(2,1)S(1)} %get-tuple-element.74.table_ref, ...), custom_call_target="tpu_custom_call", output_to_operand_aliasing={{0}: (5, {}), {1}: (6, {})} | custom-call | tf_op jit(solution)/shard_map/collide_1/pallas_call | solution.py:999
  189.0 3.0 collide_2.1
  192.0 4.1 %substep_0.1 = (f32[8,256]{1,0:T(8,128)S(1)}, f32[8,256]{1,0:T(8,128)S(1)}, f32[4,256]{1,0:T(4,128)S(1)}) custom-call(s32[14]{0:T(128)S(1)} %copy-done.5, f32[8,256]{1,0:T(8,128)S(1)} %copy-done.4, s32[224,2]{1,0:T(8,128)S(1)} %bitcast.43, s32[18]{0:T(128)S(1)} %get-tuple-element.93.counts_ref, f32[8,256]{1,0:T(8,128)S(1)} %get-tuple-element.94.speed_ref, ...), custom_call_target="tpu_custom_call" | custom-call | tf_op jit(solution)/shard_map/substep_0/pallas_call | solution.py:1019
  196.1 66.3 %all-gather.6.blocks_ref = f32[32,4,256]{2,1,0:T(4,128)S(1)} all-gather(f32[1,4,256]{2,1,0:T(4,128)S(1)} %bitcast.48), channel_id=4, replica_groups=mesh['gx'=4,'gy'=4,'gz'=2] {'gx','gy','gz'}, dimensions={0}, use_global_device_ids=true | all-gather | bytes 135168 | tf_op jit(solution)/shard_map/all_gather | solution.py:1015
  262.3 3.7 %collide_3.1 = (f32[3,528,128]{2,1,0:T(8,128)}, f32[3,528,128]{2,1,0:T(8,128)}, f32[8,128]{1,0:T(8,128)}) custom-call(s32[14]{0:T(128)S(1)} %copy-done.5, f32[2,8,128]{2,1,0:T(8,128)S(1)} %broadcast_in_dim.2.dirs_ref, bf16[280,256]{1,0:T(8,128)(2,1)S(1)} %get-tuple-element.74.table_ref, ...), custom_call_target="tpu_custom_call", output_to_operand_aliasing={{0}: (5, {}), {1}: (6, {})} | custom-call | tf_op jit(solution)/shard_map/collide_3/pallas_call | solution.py:999
  266.1 1.8 collide_4.1
  267.9 1.3 collide_5.1
  269.2 4.1 %substep_1.1 = (f32[8,256]{1,0:T(8,128)S(1)}, f32[8,256]{1,0:T(8,128)S(1)}, f32[4,256]{1,0:T(4,128)S(1)}) custom-call(s32[14]{0:T(128)S(1)} %copy-done.5, f32[8,256]{1,0:T(8,128)S(1)} %copy-done.4, s32[224,2]{1,0:T(8,128)S(1)} %bitcast.44, s32[18]{0:T(128)S(1)} %get-tuple-element.93.counts_ref, f32[8,256]{1,0:T(8,128)S(1)} %get-tuple-element.98.speed_ref, ...), custom_call_target="tpu_custom_call" | custom-call | tf_op jit(solution)/shard_map/substep_1/pallas_call | solution.py:1019
  273.3 64.8 %all-gather.7.blocks_ref = f32[32,4,256]{2,1,0:T(4,128)S(1)} all-gather(f32[1,4,256]{2,1,0:T(4,128)S(1)} %bitcast.49), channel_id=5, replica_groups=mesh['gx'=4,'gy'=4,'gz'=2] {'gx','gy','gz'}, dimensions={0}, use_global_device_ids=true | all-gather | bytes 135168 | tf_op jit(solution)/shard_map/all_gather | solution.py:1015
  338.1 3.2 collide_6.1
  341.3 3.9 %collide_7.1 = (f32[3,528,128]{2,1,0:T(8,128)}, f32[3,528,128]{2,1,0:T(8,128)}, f32[8,128]{1,0:T(8,128)}) custom-call(s32[14]{0:T(128)S(1)} %copy-done.5, f32[2,8,128]{2,1,0:T(8,128)S(1)} %broadcast_in_dim.2.dirs_ref, bf16[280,256]{1,0:T(8,128)(2,1)S(1)} %get-tuple-element.74.table_ref, ...), custom_call_target="tpu_custom_call", output_to_operand_aliasing={{0}: (8, {}), {1}: (9, {})} | custom-call | tf_op jit(solution)/shard_map/collide_7/pallas_call | solution.py:999
  345.2 3.0 collide_8.1
  348.2 4.6 %substep_2.1 = (f32[3,1,1,1,256]{4,3,2,1,0:T(1,128)}, f32[3,1,1,1,256]{4,3,2,1,0:T(1,128)}) custom-call(s32[14]{0:T(128)S(1)} %copy-done.5, f32[8,256]{1,0:T(8,128)S(1)} %copy-done.4, s32[224,2]{1,0:T(8,128)S(1)} %bitcast.45, s32[18]{0:T(128)S(1)} %get-tuple-element.93.counts_ref, f32[8,256]{1,0:T(8,128)S(1)} %get-tuple-element.102.speed_ref, ...), custom_call_target="tpu_custom_call" | custom-call | tf_op jit(solution)/shard_map/substep_2/pallas_call | solution.py:1019
  (12 shorter events, 0.1 us)
Async XLA Ops:
  1.9 0.7 copy-start.11
  1.9 0.7 copy-start.12
  5.9 20.0 %collective-permute-start.4 = (f32[304,128]{1,0:T(8,128)}, f32[304,128]{1,0:T(8,128)S(1)}, u32[]{:S(2)}, u32[]{:S(2)}) collective-permute-start(f32[304,128]{1,0:T(8,128)} %get-tuple-element.60), channel_id=1, source_target_pairs={{0,1},{1,0},{2,3},{3,2},{4,5},{5,4},{6,7},{7,6},{8,9},{9,8},{10,11... | collective-permute-start | bytes 466952 | tf_op jit(solution)/shard_map/ppermute | solution.py:53
  8.9 17.0 %collective-permute-start = (f32[152,128]{1,0:T(8,128)}, f32[152,128]{1,0:T(8,128)S(1)}, u32[]{:S(2)}, u32[]{:S(2)}) collective-permute-start(f32[152,128]{1,0:T(8,128)} %get-tuple-element.56), channel_id=1, source_target_pairs={{0,8},{8,16},{16,24},{24,0},{1,9},{9,17},{17,25},{25,1},{2,10},{10... | collective-permute-start | bytes 233480 | tf_op jit(solution)/shard_map/ppermute | solution.py:53
  10.5 15.4 %collective-permute-start.1 = (f32[152,128]{1,0:T(8,128)}, f32[152,128]{1,0:T(8,128)S(1)}, u32[]{:S(2)}, u32[]{:S(2)}) collective-permute-start(f32[152,128]{1,0:T(8,128)} %get-tuple-element.57), channel_id=1, source_target_pairs={{0,24},{8,0},{16,8},{24,16},{1,25},{9,1},{17,9},{25,17},{2,26},{10... | collective-permute-start | bytes 233480 | tf_op jit(solution)/shard_map/ppermute | solution.py:53
  12.8 13.1 %collective-permute-start.2 = (f32[152,128]{1,0:T(8,128)}, f32[152,128]{1,0:T(8,128)S(1)}, u32[]{:S(2)}, u32[]{:S(2)}) collective-permute-start(f32[152,128]{1,0:T(8,128)} %get-tuple-element.58), channel_id=1, source_target_pairs={{0,2},{2,4},{4,6},{6,0},{1,3},{3,5},{5,7},{7,1},{8,10},{10,12},{12... | collective-permute-start | bytes 233480 | tf_op jit(solution)/shard_map/ppermute | solution.py:53
  12.8 13.2 %collective-permute-start.3 = (f32[152,128]{1,0:T(8,128)}, f32[152,128]{1,0:T(8,128)S(1)}, u32[]{:S(2)}, u32[]{:S(2)}) collective-permute-start(f32[152,128]{1,0:T(8,128)} %get-tuple-element.59), channel_id=1, source_target_pairs={{0,6},{2,0},{4,2},{6,4},{1,7},{3,1},{5,3},{7,5},{8,14},{10,8},{12,... | collective-permute-start | bytes 233480 | tf_op jit(solution)/shard_map/ppermute | solution.py:53
  14.5 0.6 copy-start.5
  15.1 1.1 copy-start
  16.2 1.1 copy-start.2
  25.3 0.9 copy-start.6
  25.3 0.9 copy-start.7
  25.3 0.9 copy-start.8
  32.4 5.7 %collective-permute-start.5 = (f32[2,24,128]{2,1,0:T(8,128)S(1)}, f32[2,24,128]{2,1,0:T(8,128)S(1)}, u32[]{:S(2)}, u32[]{:S(2)}) collective-permute-start(f32[2,24,128]{2,1,0:T(8,128)S(1)} %get-tuple-element.64), channel_id=1, source_target_pairs={{0,8},{8,16},{16,24},{24,0},{1,9},{9,17},{17,25},{25,1},{2,10},{10... | collective-permute-start | bytes 73736 | tf_op jit(solution)/shard_map/ppermute | solution.py:53
  32.5 5.6 %collective-permute-start.6 = (f32[2,24,128]{2,1,0:T(8,128)S(1)}, f32[2,24,128]{2,1,0:T(8,128)S(1)}, u32[]{:S(2)}, u32[]{:S(2)}) collective-permute-start(f32[2,24,128]{2,1,0:T(8,128)S(1)} %get-tuple-element.65), channel_id=1, source_target_pairs={{0,24},{8,0},{16,8},{24,16},{1,25},{9,1},{17,9},{25,17},{2,26},{10... | collective-permute-start | bytes 73736 | tf_op jit(solution)/shard_map/ppermute | solution.py:53
  38.1 74.5 %copy-start.10 = (s32[2,1,1,1,224]{4,3,2,1,0:T(1,128)S(1)}, s32[2,1,1,1,224]{4,3,2,1,0:T(1,128)}, u32[]{:S(2)}) copy-start(s32[2,1,1,1,224]{4,3,2,1,0:T(1,128)} %param.21) | copy-start | bytes 5380
  38.1 74.6 %copy-start.4 = (f32[8,256]{1,0:T(8,128)S(1)}, f32[8,256]{1,0:T(8,128)}, u32[]{:S(2)}) copy-start(f32[8,256]{1,0:T(8,128)} %get-tuple-element.71.start_ref) | copy-start | bytes 24580
  38.1 3.6 %collective-permute-start.7 = (f32[2,24,128]{2,1,0:T(8,128)S(1)}, f32[2,24,128]{2,1,0:T(8,128)S(1)}, u32[]{:S(2)}, u32[]{:S(2)}) collective-permute-start(f32[2,24,128]{2,1,0:T(8,128)S(1)} %get-tuple-element.67), channel_id=1, source_target_pairs={{0,2},{2,4},{4,6},{6,0},{1,3},{3,5},{5,7},{7,1},{8,10},{10,12},{12... | collective-permute-start | bytes 73736 | tf_op jit(solution)/shard_map/ppermute | solution.py:53
  40.9 1.5 collective-permute-start.8
  42.5 0.7 copy-start.9
  42.5 75.4 %copy-start.1 = (f32[3,1,1,1,49152]{4,3,2,1,0:T(1,128)S(1)}, f32[3,1,1,1,49152]{4,3,2,1,0:T(1,128)}, u32[]{:S(2)}) copy-start(f32[3,1,1,1,49152]{4,3,2,1,0:T(1,128)} %param.12) | copy-start | bytes 1769476
  42.5 75.4 %copy-start.3 = (f32[3,1,1,1,49152]{4,3,2,1,0:T(1,128)S(1)}, f32[3,1,1,1,49152]{4,3,2,1,0:T(1,128)}, u32[]{:S(2)}) copy-start(f32[3,1,1,1,49152]{4,3,2,1,0:T(1,128)} %param.13) | copy-start | bytes 1769476
  42.7 74.2 %collective-permute-start.9 = (f32[16,304]{1,0:T(8,128)S(1)}, f32[16,304]{1,0:T(8,128)S(1)}, u32[]{:S(2)}, u32[]{:S(2)}) collective-permute-start(f32[16,304]{1,0:T(8,128)S(1)} %get-tuple-element.70), channel_id=1, source_target_pairs={{0,1},{1,0},{2,3},{3,2},{4,5},{5,4},{6,7},{7,6},{8,9},{9,8},{10,11... | collective-permute-start | bytes 58376 | tf_op jit(solution)/shard_map/ppermute | solution.py:53
